TPU v7x, 32 devices: a whole 2x2x4 slice. The times are simulated.
32 devices in a mesh: feat: 2 (over y), rows: 16 (over z, x, core).
Axes of the slice: x: 2, y: 2, z: 4, core: 2. Of those that a mesh axis runs over, the one named last changes fastest.
Arguments:
- x_vals: bfloat16 [32, 2, 8, 512, 128], P('rows', 'feat'), may hold values from -6 to 6
- x_blocks: int32 [32, 2, 8], P('rows', 'feat'), may hold values from 0 to 783
- y_vals: bfloat16 [16, 2, 8, 512, 128], P('rows', 'feat'), may hold values from -6 to 6
- y_blocks: int32 [16, 2, 8], P('rows', 'feat'), may hold values from 0 to 391
- user_weights: bfloat16 [256, 200704], P('rows', 'feat'), may hold values from -0.125 to 0.125
- item_weights: bfloat16 [256, 100352], P('rows', 'feat'), may hold values from -0.125 to 0.125
- observed: int32 [32, 16], P('rows'), may hold values 0 or 1
- ratings: bfloat16 [16384, 2, 4096], P('rows', 'feat'), may hold values from -6 to 6
Outputs:
- grad_user: float32 [256, 200704], P('rows', 'feat')
- grad_item: float32 [256, 100352], P('rows', 'feat')
Inputs may be any that keep to these rules, and one draw needn't show every extreme that they name: `x_blocks`: feature block numbers within one shard. `y_blocks`: feature block numbers within one shard.
All inputs are finite; a program needn't handle non-finite values. No bound on the sum of `observed` on one device may be relied on, other than what follows from the above.
Results may differ from a plain program's by a relative error of at most 0.008.
Values may be sent and summed in bfloat16 or wider, within the bound.
No kernel may reach another device: no remote copies, remote signals or barrier semaphores. Data moves between devices by JAX's collectives and lax.ppermute only.
A program may use at most 64 MiB of HBM per device.

v0:
```python
import math

import jax
import jax.numpy as jnp
from jax import lax
from jax.sharding import PartitionSpec as P

TILE = 512
FBW = 128
RANK = 256
IBD = 1


def lookup(weights, indices):
    rank_part = weights.shape[0]
    blocks_table = weights.reshape(rank_part, -1, FBW)
    picked = jnp.take(blocks_table, indices.reshape(-1), axis=1)
    return picked.reshape(rank_part, indices.shape[0], indices.shape[2], FBW)


def accumulate(returned, indices, weights):
    rank_part = weights.shape[0]
    totals = jnp.zeros((rank_part, weights.shape[1] // FBW, FBW), jnp.float32)
    totals = totals.at[:, indices.reshape(-1)].add(returned.reshape(rank_part, -1, FBW))
    return totals.reshape(rank_part, -1)


def on_device(x_vals, x_blocks, y_vals, y_blocks, user_weights, item_weights, observed, ratings):
    rank_scale = 1.0 / math.sqrt(RANK)
    grad_scale = 1.0 / (TILE * math.sqrt(RANK))
    user_blocks_n = x_vals.shape[0]
    item_blocks_n = y_vals.shape[0]
    user_ids, item_ids = (
        lax.all_gather(x_blocks, "rows", axis=0, tiled=True),
        lax.all_gather(y_blocks, "rows", axis=0, tiled=True),
    )
    user_ask = lookup(user_weights, user_ids)
    item_ask = lookup(item_weights, item_ids)
    user_cols, item_cols = (
        lax.all_to_all(user_ask, "rows", split_axis=1, concat_axis=0, tiled=True),
        lax.all_to_all(item_ask, "rows", split_axis=1, concat_axis=0, tiled=True),
    )
    user_part = jnp.einsum(
        "bktc,rbkc->btr", x_vals[:, 0], user_cols, preferred_element_type=jnp.float32
    ).reshape(-1, RANK)
    item_part = jnp.einsum(
        "bktc,rbkc->btr", y_vals[:, 0], item_cols, preferred_element_type=jnp.float32
    ).reshape(-1, RANK)
    user_proj = lax.psum(user_part, "feat").astype(jnp.bfloat16)
    item_share = lax.psum_scatter(item_part, "feat", scatter_dimension=0, tiled=True).astype(
        jnp.bfloat16
    )
    item_all = lax.all_gather(item_share, "rows", axis=0, tiled=True)
    columns_n = item_all.shape[0]
    share_n = item_share.shape[0]
    feat_id = lax.axis_index("feat")
    column = jnp.arange(columns_n, dtype=jnp.int32)
    item_group = column // share_n
    within = column % share_n
    block_column = item_group * IBD + (feat_id * share_n + within) // TILE
    onehot = (
        block_column[None, :] == jnp.arange(observed.shape[1], dtype=jnp.int32)[:, None]
    ).astype(jnp.float32)
    tile_mask = jnp.dot(observed.astype(jnp.float32), onehot)
    rating_local = ratings.reshape(user_blocks_n, TILE, columns_n).astype(jnp.float32)
    predicted = (
        jnp.einsum("ur,cr->uc", user_proj, item_all, preferred_element_type=jnp.float32)
        * rank_scale
    )
    residual = tile_mask[:, None, :] * (
        predicted.reshape(user_blocks_n, TILE, columns_n) - rating_local
    )
    residual = residual.reshape(-1, columns_n).astype(jnp.bfloat16)
    grad_part = jnp.dot(residual, item_all, preferred_element_type=jnp.float32) * grad_scale
    user_grad = lax.psum(grad_part, "feat").astype(jnp.bfloat16)
    item_terms = (
        jnp.einsum("uc,ur->cr", residual, user_proj, preferred_element_type=jnp.float32)
        * grad_scale
    )
    item_grad = lax.psum_scatter(
        item_terms.astype(jnp.bfloat16), "rows", scatter_dimension=0, tiled=True
    )
    item_grad_group = lax.all_gather(item_grad, "feat", axis=0, tiled=True)
    user_grad_blocks = jnp.einsum(
        "btr,bktc->rbkc",
        user_grad.reshape(user_blocks_n, TILE, RANK),
        x_vals[:, 0],
        preferred_element_type=jnp.float32,
    )
    item_grad_blocks = jnp.einsum(
        "btr,bktc->rbkc",
        item_grad_group.reshape(item_blocks_n, TILE, RANK),
        y_vals[:, 0],
        preferred_element_type=jnp.float32,
    )
    back_user, back_item = (
        lax.all_to_all(
            user_grad_blocks.astype(jnp.bfloat16), "rows", split_axis=0, concat_axis=1, tiled=True
        ).astype(user_grad_blocks.dtype),
        lax.all_to_all(
            item_grad_blocks.astype(jnp.bfloat16), "rows", split_axis=0, concat_axis=1, tiled=True
        ).astype(item_grad_blocks.dtype),
    )
    return (
        accumulate(back_user, user_ids, user_weights),
        accumulate(back_item, item_ids, item_weights),
    )


def solution(mesh):
    return jax.shard_map(
        on_device,
        mesh=mesh,
        in_specs=(
            P("rows", "feat", None, None, None),
            P("rows", "feat", None),
            P("rows", "feat", None, None, None),
            P("rows", "feat", None),
            P("rows", "feat"),
            P("rows", "feat"),
            P("rows", None),
            P("rows", "feat", None),
        ),
        out_specs=(P("rows", "feat"), P("rows", "feat")),
        check_vma=False,
    )
```

profile of v0, /device:TPU:0, one launch (start us, length us, event | category | flops | bytes accessed | tf_op | source)
XLA Modules:
  0.0 335.1 jit_solution(2291321699356848896)
XLA Ops:
  7.2 0.0 copy-start
  7.2 0.0 reduce-scatter.3.cloned.1.call-start
  7.2 23.3 %all_gather.13 = s32[16,1,8]{2,1,0:T(1,128)S(1)} all-gather(s32[1,1,8]{2,1,0:T(1,128)} %param.11), channel_id=1, replica_groups=mesh['feat'=2,'rows'=16] {'rows'}, dimensions={0}, use_global_device_ids=true | all-gather | bytes 544 | tf_op jit(solution)/shard_map/all_gather | solution.py:35
  30.5 0.1 copy.49
  30.6 0.6 broadcast.160
  31.1 0.6 reduce.7
  31.8 0.1 reshape.191
  31.9 0.1 copy.50
  32.0 2.8 copy_bitcast_fusion.3
  34.8 2.9 gather_fusion.1
  37.7 1.3 bitcast_select_fusion
  39.0 0.1 copy.53
  39.2 17.1 %all_to_all.51 = bf16[16,16,8,128]{3,2,0,1:T(8,128)(2,1)S(1)} all-to-all(bf16[16,16,8,128]{3,2,0,1:T(8,128)(2,1)S(1)} %copy.53), channel_id=1, replica_groups=mesh['feat'=2,'rows'=16] {'rows'}, dimensions={1} | all-to-all | bytes 1048576 | tf_op jit(solution)/shard_map/all_to_all | solution.py:41
  56.2 0.1 copy.54
  56.3 0.0 copy-done.4
  56.3 1.3 convolution_bitcast_fusion.1
  57.6 0.0 reduce-scatter.3.cloned.1.call-update
  57.6 0.0 all-gather.2.cloned.1.call-start
  57.7 0.0 copy-done.7
  57.7 19.8 %all_gather.12 = s32[32,1,8]{2,1,0:T(1,128)S(1)} all-gather(s32[2,1,8]{2,1,0:T(1,128)S(1)} %copy-done.7), channel_id=1, replica_groups=mesh['feat'=2,'rows'=16] {'rows'}, dimensions={0}, use_global_device_ids=true | all-gather | bytes 1088 | tf_op jit(solution)/shard_map/all_gather | solution.py:34
  77.4 0.7 reduce.6
  78.1 0.1 reshape.185
  78.2 0.0 copy-done
  78.2 2.2 copy_bitcast_fusion.2
  80.4 1.6 convert_element_type.72
  82.1 0.0 all-gather.2.cloned.1.call-update
  82.1 2.8 gather_fusion
  84.9 0.0 copy-start.3
  84.9 1.2 copy_select_fusion
  86.1 3.7 %all-to-all-start = ((bf16[16,32,8,128]{3,2,0,1:T(8,128)(2,1)}), bf16[16,32,8,128]{3,2,0,1:T(8,128)(2,1)S(1)}, u32[]{:S(2)}, u32[]{:S(2)}) async-start(bf16[16,32,8,128]{3,2,0,1:T(8,128)(2,1)} %copy_select_fusion), calls=%async_computation | async-start | bytes 2097152 | tf_op jit(solution)/shard_map/all_to_all | solution.py:40
  89.8 0.0 reduce-scatter.5.cloned.1.call-start
  89.9 0.0 copy-done.8
  89.9 0.2 convolution_bitcast_fusion
  90.0 25.6 %all-to-all-done = bf16[16,32,8,128]{3,2,0,1:T(8,128)(2,1)S(1)} async-done(((bf16[16,32,8,128]{3,2,0,1:T(8,128)(2,1)}), bf16[16,32,8,128]{3,2,0,1:T(8,128)(2,1)S(1)}, u32[]{:S(2)}, u32[]{:S(2)}) %all-to-all-start) | async-done | bytes 1048608 | tf_op jit(solution)/shard_map/all_to_all | solution.py:40
  115.6 0.2 copy.47
  115.8 0.0 copy-done.3
  115.8 1.7 fusion.13
  117.5 1.6 copy.48
  119.1 29.9 %all-reduce.2 = bf16[1024,256]{1,0:T(8,128)(2,1)} all-reduce(f32[1024,256]{1,0:T(8,128)S(1)} %bitcast.118), channel_id=1, replica_groups=mesh['feat'=2,'rows'=16] {'feat'}, use_global_device_ids=true, to_apply=%region_0.1 | all-reduce | flops 262144 | bytes 1572864 | tf_op jit(solution)/shard_map/psum | solution.py:49
  149.0 7.2 %fusion.1 = bf16[1024,4096]{1,0:T(8,128)(2,1)S(1)} fusion(bf16[4096,256]{0,1:T(8,128)(2,1)} %all-gather.2.cloned.1.call-done, bf16[1024,1,4096]{2,0,1:T(8,128)(2,1)} %param.15, f32[2,4096]{1,0:T(2,128)S(1)} %convolution_bitcast_fusion, bf16[1024,256]{1,0:T(8,128)(2,1)} %all-reduce.2), kind=kOutput, calls=%fused_computation.6 | convolution fusion | flops 2168455168 | bytes 19431424 | tf_op jit(solution)/shard_map/ur,cr->uc/dot_general | solution.py:67
  156.2 0.0 copy-start.2
  156.2 3.2 copy-done.2
  159.4 4.0 %fusion.2 = bf16[4096,256]{1,0:T(8,128)(2,1)} fusion(bf16[1024,4096]{1,0:T(8,128)(2,1)S(1)} %fusion.1, bf16[1024,256]{1,0:T(8,128)(2,1)S(1)} %copy-done.6), kind=kOutput, calls=%fused_computation.9 | convolution fusion | flops 2149580800 | bytes 11010048 | tf_op jit(solution)/shard_map/uc,ur->cr/dot_general | solution.py:77
  163.4 6.3 %convolution_multiply_fusion.1 = f32[1024,256]{1,0:T(8,128)S(1)} fusion(bf16[1024,4096]{1,0:T(8,128)(2,1)} %copy-done.2, bf16[4096,256]{0,1:T(8,128)(2,1)} %all-gather.2.cloned.1.call-done), kind=kOutput, calls=%fused_computation.22 | convolution fusion | flops 2147745792 | bytes 11534336 | tf_op jit(solution)/shard_map/dot_general | solution.py:74
  169.7 0.0 reduce-scatter.5.cloned.1.call-update
  169.8 29.9 %all-reduce.3 = bf16[1024,256]{1,0:T(8,128)(2,1)} all-reduce(f32[1024,256]{1,0:T(8,128)S(1)} %convolution_multiply_fusion.1), channel_id=1, replica_groups=mesh['feat'=2,'rows'=16] {'feat'}, use_global_device_ids=true, to_apply=%region_2.3 | all-reduce | flops 262144 | bytes 1572864 | tf_op jit(solution)/shard_map/psum | solution.py:75
  199.7 1.8 fusion.10
  201.5 0.7 copy.56
  202.2 42.7 %all_to_all.52 = bf16[256,2,8,128]{3,2,1,0:T(8,128)(2,1)S(1)} all-to-all(bf16[256,2,8,128]{3,2,1,0:T(8,128)(2,1)S(1)} %copy.56), channel_id=1, replica_groups=mesh['feat'=2,'rows'=16] {'rows'}, dimensions={0} | all-to-all | bytes 2097152 | tf_op jit(solution)/shard_map/all_to_all | solution.py:97
  244.9 0.2 convert_bitcast_fusion
  245.1 0.7 copy.57
  245.8 3.1 broadcast_in_dim.31
  248.9 28.3 %scatter_fusion = f32[16,784,128]{2,0,1:T(8,128)} fusion(f32[16,784,128]{2,0,1:T(8,128)} %broadcast_in_dim.31, s32[256]{0:T(256)S(1)} %bitcast.128, f32[256,16,128]{2,1,0:T(8,128)S(1)} %bitcast.114), kind=kCustom, calls=%fused_computation.2 | custom fusion | flops 524288 | bytes 6292480 | tf_op jit(solution)/shard_map/scatter-add | solution.py:24
  277.2 6.6 %all_gather.15 = bf16[512,256]{1,0:T(8,128)(2,1)S(1)} all-gather(bf16[256,256]{1,0:T(8,128)(2,1)} %reduce-scatter.5.cloned.1.call-done), channel_id=1, replica_groups=mesh['feat'=2,'rows'=16] {'feat'}, dimensions={0}, use_global_device_ids=true | all-gather | bytes 393216 | tf_op jit(solution)/shard_map/all_gather | solution.py:83
  283.8 0.5 fusion.16
  284.3 1.1 copy.60
  285.4 5.4 %all-to-all-start.3 = ((bf16[256,1,8,128]{3,2,1,0:T(8,128)(2,1)}), bf16[256,1,8,128]{3,2,1,0:T(8,128)(2,1)S(1)}, u32[]{:S(2)}, u32[]{:S(2)}) async-start(bf16[256,1,8,128]{3,2,1,0:T(8,128)(2,1)} %copy.60), calls=%async_computation.5 | async-start | bytes 1048576 | tf_op jit(solution)/shard_map/all_to_all | solution.py:100
  290.8 6.0 %copy_bitcast_fusion = f32[16,100352]{1,0:T(8,128)} fusion(f32[16,784,128]{2,0,1:T(8,128)} %scatter_fusion), kind=kLoop, calls=%fused_computation.7 | loop fusion | bytes 12845056 | tf_op jit(solution)/shard_map/reshape | solution.py:25
  296.8 8.5 %all-to-all-done.3 = bf16[256,1,8,128]{3,2,1,0:T(8,128)(2,1)S(1)} async-done(((bf16[256,1,8,128]{3,2,1,0:T(8,128)(2,1)}), bf16[256,1,8,128]{3,2,1,0:T(8,128)(2,1)S(1)}, u32[]{:S(2)}, u32[]{:S(2)}) %all-to-all-start.3) | async-done | bytes 524320 | tf_op jit(solution)/shard_map/all_to_all | solution.py:100
  305.2 0.1 convert_bitcast_fusion.1
  305.4 1.2 copy.61
  306.5 1.9 broadcast_in_dim.36
  308.4 16.4 %scatter_fusion.1 = f32[16,392,128]{2,0,1:T(8,128)} fusion(f32[16,392,128]{2,0,1:T(8,128)} %broadcast_in_dim.36, s32[128]{0:T(128)S(1)} %fusion.38, f32[128,16,128]{2,1,0:T(8,128)} %bitcast.117), kind=kCustom, calls=%fused_computation.3 | custom fusion | flops 262144 | bytes 3146240 | tf_op jit(solution)/shard_map/scatter-add | solution.py:24
  324.8 3.8 %copy_bitcast_fusion.1 = f32[16,50176]{1,0:T(8,128)} fusion(f32[16,392,128]{2,0,1:T(8,128)} %scatter_fusion.1), kind=kLoop, calls=%fused_computation.11 | loop fusion | bytes 6422528 | tf_op jit(solution)/shard_map/reshape | solution.py:25
  (19 shorter events, 0.1 us)
Async XLA Ops:
  7.2 71.0 %copy-start = (bf16[16,100352]{1,0:T(8,128)(2,1)S(1)}, bf16[16,100352]{1,0:T(8,128)(2,1)}, u32[]{:S(2)}) copy-start(bf16[16,100352]{1,0:T(8,128)(2,1)} %param.12) | copy-start | bytes 9633796
  7.2 73.3 %reduce-scatter.3.cloned.1.call-start = ((), (), s32[]{:S(2)}) async-start(), calls=%async_computation.6 | async-start | bytes 786432 | tf_op jit(solution)/shard_map/reduce_scatter | solution.py:50
  37.7 18.6 %copy-start.4 = (bf16[1,1,8,512,128]{4,3,2,1,0:T(8,128)(2,1)S(1)}, bf16[1,1,8,512,128]{4,3,2,1,0:T(8,128)(2,1)}, u32[]{:S(2)}) copy-start(bf16[1,1,8,512,128]{4,3,2,1,0:T(8,128)(2,1)} %param.10) | copy-start | bytes 3145732
  37.7 19.9 %copy-start.7 = (s32[2,1,8]{2,1,0:T(1,128)S(1)}, s32[2,1,8]{2,1,0:T(1,128)}, u32[]{:S(2)}) copy-start(s32[2,1,8]{2,1,0:T(1,128)} %param.9) | copy-start | bytes 196
  57.6 91.4 %all-gather.2.cloned.1.call-start = ((), (), s32[]{:S(2)}) async-start(), calls=%async_computation.7 | async-start | bytes 2228224 | tf_op jit(solution)/shard_map/all_gather | solution.py:53
  82.1 7.8 %copy-start.8 = (s32[2,16]{1,0:T(2,128)S(1)}, s32[2,16]{1,0:T(2,128)}, u32[]{:S(2)}) copy-start(s32[2,16]{1,0:T(2,128)} %param.14) | copy-start | bytes 388
  84.9 30.9 %copy-start.3 = (bf16[2,1,8,512,128]{4,3,2,1,0:T(8,128)(2,1)S(1)}, bf16[2,1,8,512,128]{4,3,2,1,0:T(8,128)(2,1)}, u32[]{:S(2)}) copy-start(bf16[2,1,8,512,128]{4,3,2,1,0:T(8,128)(2,1)} %param.8) | copy-start | bytes 6291460
  86.1 29.5 %all-to-all-start = ((bf16[16,32,8,128]{3,2,0,1:T(8,128)(2,1)}), bf16[16,32,8,128]{3,2,0,1:T(8,128)(2,1)S(1)}, u32[]{:S(2)}, u32[]{:S(2)}) async-start(bf16[16,32,8,128]{3,2,0,1:T(8,128)(2,1)} %copy_select_fusion), calls=%async_computation | async-start | bytes 2097152 | tf_op jit(solution)/shard_map/all_to_all | solution.py:40
  89.8 187.4 %reduce-scatter.5.cloned.1.call-start = ((), (), s32[]{:S(2)}) async-start(), calls=%async_computation.8 | async-start | bytes 2228224 | tf_op jit(solution)/shard_map/reduce_scatter | solution.py:80
  149.0 10.4 %copy-start.6 = (bf16[1024,256]{1,0:T(8,128)(2,1)S(1)}, bf16[1024,256]{1,0:T(8,128)(2,1)}, u32[]{:S(2)}) copy-start(bf16[1024,256]{1,0:T(8,128)(2,1)} %all-reduce.2) | copy-start | bytes 1572868
  156.2 3.2 copy-start.2
  248.9 34.9 %copy-start.5 = (bf16[1,1,8,512,128]{4,3,2,1,0:T(8,128)(2,1)S(1)}, bf16[1,1,8,512,128]{4,3,2,1,0:T(8,128)(2,1)}, u32[]{:S(2)}) copy-start(bf16[1,1,8,512,128]{4,3,2,1,0:T(8,128)(2,1)} %param.10) | copy-start | bytes 3145732
  285.4 19.9 %all-to-all-start.3 = ((bf16[256,1,8,128]{3,2,1,0:T(8,128)(2,1)}), bf16[256,1,8,128]{3,2,1,0:T(8,128)(2,1)S(1)}, u32[]{:S(2)}, u32[]{:S(2)}) async-start(bf16[256,1,8,128]{3,2,1,0:T(8,128)(2,1)} %copy.60), calls=%async_computation.5 | async-start | bytes 1048576 | tf_op jit(solution)/shard_map/all_to_all | solution.py:100
  308.4 20.2 %copy-start.1 = (bf16[16,100352]{1,0:T(8,128)(2,1)S(1)}, bf16[16,100352]{1,0:T(8,128)(2,1)}, u32[]{:S(2)}) copy-start(bf16[16,100352]{1,0:T(8,128)(2,1)} %param.12) | copy-start | bytes 9633796
Sparse Core Ops, SparseCore 0:
  57.7 13.9 reduce-scatter.2
  82.2 47.2 all-gather.1
  169.9 73.9 reduce-scatter.4
where the time goes:
time: 337 us; the launch traced here: 335 us
  blocking collectives  169 us (50%)
  other arithmetic  50.5 us (15%)
  local copies, waits for them, and re-layouts  35.3 us (10%)
  waiting for transfers between devices  34.1 us (10%)
  matrix products  22.9 us (7%)
  between operations  14 us (4%)
  starting transfers between devices  9.15 us (3%)
    scatter-add x2, other arithmetic, accumulate(): totals.at[:, indices.reshape(-1)].add(returned.reshape(rank_part, -1, FBW))  44.7 us
    all_to_all x1, blocking collectives, on_device(): lax.all_to_all(user_grad_blocks.astype(jnp.bfloat16), 'rows', split_axis=...  42.7 us
    psum x1, blocking collectives, on_device(): user_grad = lax.psum(grad_part, 'feat').astype(jnp.bfloat16)  29.9 us
    psum x1, blocking collectives, on_device(): user_proj = lax.psum(user_part, 'feat').astype(jnp.bfloat16)  29.9 us
    all_to_all x1, waiting for transfers between devices, on_device(): lax.all_to_all(user_ask, 'rows', split_axis=1, concat_axis=0, tiled=True)  25.6 us
    all_gather x1, blocking collectives, on_device(): lax.all_gather(y_blocks, 'rows', axis=0, tiled=True)  23.3 us
    all_gather x1, blocking collectives, on_device(): lax.all_gather(x_blocks, 'rows', axis=0, tiled=True)  19.8 us
    all_to_all x1, blocking collectives, on_device(): lax.all_to_all(item_ask, 'rows', split_axis=1, concat_axis=0, tiled=True)  17.1 us
  transfers between devices with their start and end apart: 5, of which 2 were waited for; matrix products, arithmetic and copies ran while one was open for 15% of the time, Pallas kernels for 0%

commit v1 on v0

v1 whole, which is shorter than its diff:
```python
import functools
import math

import jax
import jax.numpy as jnp
from jax import lax
from jax.experimental import pallas as pl
from jax.experimental.pallas import tpu as pltpu
from jax.sharding import PartitionSpec as P

FBW = 128
F32 = jnp.float32
BF16 = jnp.bfloat16
VMEM = pl.BlockSpec(memory_space=pltpu.VMEM)
SMEM = pl.BlockSpec(memory_space=pltpu.SMEM)


def params(mib):
    return pltpu.CompilerParams(vmem_limit_bytes=mib * 1024 * 1024)


def pick_kernel(ids, weights, out):
    peers, nb, _, width = out.shape
    kb = width // FBW

    def one(p, carry):
        for b in range(nb):
            for k in range(kb):
                at = pl.multiple_of(ids[(p * nb + b) * kb + k] * FBW, FBW)
                out[p, b, :, k * FBW : (k + 1) * FBW] = weights[:, pl.ds(at, FBW)]
        return carry

    lax.fori_loop(0, peers, one, 0)


def pick(ids, weights, peers, nb, kb):
    rp = weights.shape[0]
    return pl.pallas_call(
        pick_kernel,
        out_shape=jax.ShapeDtypeStruct((peers, nb, rp, kb * FBW), BF16),
        in_specs=[SMEM, VMEM],
        out_specs=VMEM,
        compiler_params=params(16),
        name="pick",
    )(ids, weights)


def joined(vals, b):
    return jnp.concatenate([vals[b, k] for k in range(vals.shape[1])], axis=1)


def project(vals, cols, b):
    peers, _, rp, width = cols.shape
    table = cols[:, b].reshape(peers * rp, width)
    return lax.dot_general(
        joined(vals, b), table, (((1,), (1,)), ((), ())), preferred_element_type=F32
    )


def user_proj_kernel(vals, cols, out):
    for b in range(vals.shape[0]):
        out[b] = project(vals, cols, b).astype(out.dtype)


def user_project(vals, cols):
    nb, _, tile, _ = vals.shape
    rank = cols.shape[0] * cols.shape[2]
    return pl.pallas_call(
        user_proj_kernel,
        out_shape=jax.ShapeDtypeStruct((nb, tile, rank), F32),
        in_specs=[VMEM, VMEM],
        out_specs=VMEM,
        compiler_params=params(24),
        name="user_project",
    )(vals, cols)


def grad_blocks_kernel(grads, vals, out):
    peers, nb, rp, width = out.shape
    for b in range(nb):
        blocks = lax.dot_general(
            grads[b], joined(vals, b), (((0,), (0,)), ((), ())), preferred_element_type=F32
        )
        out[:, b] = blocks.astype(out.dtype).reshape(peers, rp, width)


def grad_blocks(grads, vals, peers):
    nb, kb, tile, _ = vals.shape
    rank = grads.shape[-1]
    return pl.pallas_call(
        grad_blocks_kernel,
        out_shape=jax.ShapeDtypeStruct((peers, nb, rank // peers, kb * FBW), BF16),
        in_specs=[VMEM, VMEM],
        out_specs=VMEM,
        compiler_params=params(24),
        name="grad_blocks",
    )(grads, vals)


def gather_grads_kernel(ids, back, out):
    peers, nb, _, width = back.shape
    kb = width // FBW
    out[...] = jnp.zeros_like(out)

    def one(p, carry):
        for b in range(nb):
            for k in range(kb):
                at = pl.multiple_of(ids[(p * nb + b) * kb + k] * FBW, FBW)
                out[:, pl.ds(at, FBW)] += back[p, b, :, k * FBW : (k + 1) * FBW].astype(F32)
        return carry

    lax.fori_loop(0, peers, one, 0)


def gather_grads(ids, back, columns):
    return pl.pallas_call(
        gather_grads_kernel,
        out_shape=jax.ShapeDtypeStruct((back.shape[2], columns), F32),
        in_specs=[SMEM, VMEM],
        out_specs=VMEM,
        compiler_params=params(24),
        name="gather_grads",
    )(ids, back)


def rating_columns(ratings, row, tile, g, share):
    rows = pl.ds(row, tile)
    if share % FBW == 0:
        return ratings[rows, pl.ds(pl.multiple_of(g * share, share), share)]
    parts = FBW // share
    wide = ratings[rows, pl.ds(pl.multiple_of(g // parts * FBW, FBW), FBW)]
    picked = wide[:, :share]
    for part in range(1, parts):
        picked = jnp.where(g % parts == part, wide[:, part * share : (part + 1) * share], picked)
    return picked


def rating_kernel(
    rank_scale, grad_scale, me, observed, users, *refs
):
    peers = len(refs) - 5
    items, (ratings, grad, keep, give, total) = refs[:peers], refs[peers:]
    share = items[0].shape[0]
    nb, tile, rank = users.shape
    groups = observed.shape[0] // nb
    for b in range(nb):
        grad[b] = jnp.zeros((tile, rank), F32)
    for k in range(peers):
        g = lax.bitwise_xor(me[0], k)
        total[...] = jnp.zeros_like(total)

        def block(b, carry):
            @pl.when(observed[b * groups + g] != 0)
            def _():
                table = items[k][...]
                rows = users[b]
                predicted = lax.dot_general(
                    rows, table, (((1,), (1,)), ((), ())), preferred_element_type=F32
                )
                rated = rating_columns(ratings, pl.multiple_of(b * tile, tile), tile, g, share)
                residual = (predicted * rank_scale - rated.astype(F32)) * observed[
                    b * groups + g
                ].astype(F32)
                residual = residual.astype(BF16)
                grad[b] += jnp.dot(residual, table, preferred_element_type=F32) * grad_scale
                total[...] += lax.dot_general(
                    residual, rows, (((0,), (0,)), ((), ())), preferred_element_type=F32
                )

            return carry

        lax.fori_loop(0, nb, block, 0)
        (give if k % 2 else keep)[k // 2] = (total[...] * grad_scale).astype(BF16)


def rate(me, observed, users, items, ratings, rank_scale, grad_scale):
    peers = len(items)
    share, rank = items[0].shape
    half = jax.ShapeDtypeStruct((peers // 2, share, rank), BF16)
    return pl.pallas_call(
        functools.partial(rating_kernel, rank_scale, grad_scale),
        out_shape=(jax.ShapeDtypeStruct(users.shape, F32), half, half),
        in_specs=[SMEM, SMEM] + [VMEM] * (peers + 2),
        out_specs=(VMEM, VMEM, VMEM),
        scratch_shapes=[pltpu.VMEM((share, rank), F32)],
        compiler_params=params(40),
        name="rate",
    )(me, observed, users, *items, ratings)


def across(n, bit):
    return [(i, i ^ bit) for i in range(n)]


def on_device(n_feat, n_rows, x_vals, x_blocks, y_vals, y_blocks, user_weights, item_weights, observed, ratings):
    x_vals, y_vals = x_vals[:, 0], y_vals[:, 0]
    nb, kbu, tile, _ = x_vals.shape
    ni, kbi, _, _ = y_vals.shape
    rank = user_weights.shape[0] * n_rows
    rank_scale = 1.0 / math.sqrt(rank)
    grad_scale = 1.0 / (tile * math.sqrt(rank))
    share = ni * tile // n_feat
    feat_id = lax.axis_index("feat")
    row_id = lax.axis_index("rows")

    def swap(array):
        return lax.ppermute(array, "feat", across(2, 1))

    def every(array):
        return lax.all_to_all(array, "rows", split_axis=0, concat_axis=0, tiled=True)

    mine = jnp.concatenate([x_blocks.reshape(-1), y_blocks.reshape(-1)])
    ids = every(jnp.broadcast_to(mine, (n_rows, mine.shape[0])))
    user_ids = ids[:, : nb * kbu].reshape(-1)
    item_ids = ids[:, nb * kbu :].reshape(-1)

    item_cols = every(pick(item_ids, item_weights, n_rows, ni, kbi))
    item_part = user_project(y_vals, item_cols).reshape(ni * tile, rank)
    if n_feat == 2:
        own = lax.dynamic_slice_in_dim(item_part, feat_id * share, share, 0)
        other = lax.dynamic_slice_in_dim(item_part, (1 - feat_id) * share, share, 0)
        item_share = (own + swap(other.astype(BF16)).astype(F32)).astype(BF16)
    else:
        item_share = lax.psum_scatter(item_part, "feat", scatter_dimension=0, tiled=True).astype(BF16)

    items = {0: item_share}
    bit = n_rows // 2
    while bit:
        for k in list(items):
            items[k + bit] = lax.ppermute(items[k], "rows", across(n_rows, bit))
        bit //= 2
    items = [items[k] for k in range(n_rows)]

    user_cols = every(pick(user_ids, user_weights, n_rows, nb, kbu))
    user_part = user_project(x_vals, user_cols)
    if n_feat == 2:
        user_proj = (user_part + swap(user_part.astype(BF16)).astype(F32)).astype(BF16)
    else:
        user_proj = lax.psum(user_part, "feat").astype(BF16)

    grad_part, keep, give = rate(
        row_id.reshape(1).astype(jnp.int32),
        observed.reshape(-1),
        user_proj,
        items,
        ratings[:, 0],
        rank_scale,
        grad_scale,
    )
    if n_feat == 2:
        user_grad = (grad_part + swap(grad_part.astype(BF16)).astype(F32)).astype(BF16)
    else:
        user_grad = lax.psum(grad_part, "feat").astype(BF16)

    user_back = every(grad_blocks(user_grad, x_vals, n_rows))

    bit = 1
    while bit < n_rows:
        total = keep.astype(F32) + lax.ppermute(give, "rows", across(n_rows, bit)).astype(F32)
        total = total.astype(BF16)
        bit *= 2
        if bit < n_rows:
            pairs = total.reshape(-1, 2, share, rank)
            keep, give = pairs[:, 0], pairs[:, 1]
    item_grad = total[0]
    if n_feat == 2:
        other = swap(item_grad)
        first = feat_id == 0
        item_grad = jnp.concatenate(
            [jnp.where(first, item_grad, other), jnp.where(first, other, item_grad)]
        )
    else:
        item_grad = lax.all_gather(item_grad, "feat", axis=0, tiled=True)
    item_back = every(grad_blocks(item_grad.reshape(ni, tile, rank), y_vals, n_rows))

    return (
        gather_grads(user_ids, user_back, user_weights.shape[1]),
        gather_grads(item_ids, item_back, item_weights.shape[1]),
    )


def solution(mesh):
    return jax.shard_map(
        functools.partial(on_device, mesh.shape["feat"], mesh.shape["rows"]),
        mesh=mesh,
        in_specs=(
            P("rows", "feat", None, None, None),
            P("rows", "feat", None),
            P("rows", "feat", None, None, None),
            P("rows", "feat", None),
            P("rows", "feat"),
            P("rows", "feat"),
            P("rows", None),
            P("rows", "feat", None),
        ),
        out_specs=(P("rows", "feat"), P("rows", "feat")),
        check_vma=False,
    )
```

time: 337 us -> 199 us (0.59)
  blocking collectives: 169 us -> 13.6 us
  waiting for transfers between devices: 34.1 us -> 94.1 us
  other arithmetic: 50.5 us -> 5.99 us
  starting transfers between devices: 9.15 us -> 42.6 us
  Pallas kernels: 0 us -> 30.2 us
  local copies, waits for them, and re-layouts: 35.3 us -> 10.7 us
  matrix products: 22.9 us -> 0 us
  between operations: 14 us -> 0.93 us
    psum x2 -> x0, blocking collectives: 59.8 us -> none  [the longest x1 29.9 us: on_device(): user_grad = lax.psum(grad_part, 'feat').astype(jnp.bfloat16)]
    ppermute x0 -> x23, waiting for transfers between devices: none -> 54.9 us  [the longest x4 30.6 us: on_device(): lax.ppermute(give, 'rows', across(n_rows, bit)).astype(F32)]
    all_gather x3 -> x0, blocking collectives: 49.7 us -> none  [the longest x1 23.3 us: on_device(): lax.all_gather(y_blocks, 'rows', axis=0, tiled=True)]
    all_to_all x2 -> x1, blocking collectives: 59.8 us -> 13.6 us  [every(): lax.all_to_all(array, 'rows', split_axis=0, concat_axis=0, tiled=True)]
    scatter-add x2 -> x0, other arithmetic: 44.7 us -> none  [accumulate(): totals.at[:, indices.reshape(-1)].add(returned.reshape(rank_part, -1, FBW))]
    pallas_call x0 -> x9, Pallas kernels: none -> 30.2 us  [the longest x1 12.4 us: rate(): pl.pallas_call(functools.partial(rating_kernel, rank_scale, grad_scale),...]
    ppermute x0 -> x23, starting transfers between devices: none -> 23.8 us  [the longest x15 13.8 us: on_device(): items[k + bit] = lax.ppermute(items[k], 'rows', across(n_rows, bit))]
    dot_general x8 -> x0, matrix products: 22.9 us -> none  [the longest x1 7.16 us: on_device(): jnp.einsum('ur,cr->uc', user_proj, item_all, preferred_element_type=jnp.f...]
  transfers between devices with their start and end apart: 5 -> 27, of which waited for: 2 -> 12; matrix products, arithmetic and copies ran while one was open for 15% -> 3% of each run, Pallas kernels for 0% -> 7%
where the time goes in v1:
time: 199 us; the launch traced here: 198 us
  waiting for transfers between devices  94.1 us (47%)
  starting transfers between devices  42.6 us (21%)
  Pallas kernels  30.2 us (15%)
  blocking collectives  13.6 us (7%)
  local copies, waits for them, and re-layouts  10.7 us (5%)
  other arithmetic  5.99 us (3%)
    all_to_all x4, waiting for transfers between devices, every(): lax.all_to_all(array, 'rows', split_axis=0, concat_axis=0, tiled=True)  39.2 us
    ppermute x4, waiting for transfers between devices, on_device(): lax.ppermute(give, 'rows', across(n_rows, bit)).astype(F32)  30.6 us
    all_to_all x4, starting transfers between devices, every(): lax.all_to_all(array, 'rows', split_axis=0, concat_axis=0, tiled=True)  18.9 us
    ppermute x4, waiting for transfers between devices, swap(): return lax.ppermute(array, 'feat', across(2, 1))  14.1 us
    ppermute x15, starting transfers between devices, on_device(): items[k + bit] = lax.ppermute(items[k], 'rows', across(n_rows, bit))  13.8 us
    all_to_all x1, blocking collectives, every(): lax.all_to_all(array, 'rows', split_axis=0, concat_axis=0, tiled=True)  13.6 us
    pallas_call x1, Pallas kernels, rate(): pl.pallas_call(functools.partial(rating_kernel, rank_scale, grad_scale),...  12.4 us
    ppermute x15, waiting for transfers between devices, on_device(): items[k + bit] = lax.ppermute(items[k], 'rows', across(n_rows, bit))  10.3 us
  transfers between devices with their start and end apart: 27, of which 12 were waited for; matrix products, arithmetic and copies ran while one was open for 3% of the time, Pallas kernels for 7%

profile of v1, /device:TPU:0, one launch (start us, length us, event | category | flops | bytes accessed | tf_op | source)
XLA Modules:
  0.0 198.2 jit_solution(8827804516752481017)
XLA Ops:
  0.6 0.5 broadcast.6
  1.1 1.3 reduce.3
  2.5 0.1 reshape.60
  2.6 0.7 pad_add_fusion
  3.3 13.6 %all_to_all.29 = s32[16,1,24]{2,1,0:T(1,128)S(1)} all-to-all(s32[16,1,24]{2,1,0:T(1,128)S(1)} %broadcast_in_dim.3), channel_id=1, replica_groups=mesh['feat'=2,'rows'=16] {'rows'}, dimensions={0} | all-to-all | bytes 3072 | tf_op jit(solution)/shard_map/all_to_all | solution.py:210
  16.9 0.1 slice.33
  16.9 0.1 reshape.65.ids
  17.0 1.4 copy-done.5
  18.4 1.6 pick.3
  20.1 4.2 %all-to-all-start.2 = ((bf16[16,1,16,1024]{3,2,1,0:T(8,128)(2,1)}), bf16[16,1,16,1024]{3,2,1,0:T(8,128)(2,1)}, u32[]{:S(2)}, u32[]{:S(2)}) async-start(bf16[16,1,16,1024]{3,2,1,0:T(8,128)(2,1)} %pick.3), calls=%async_computation.2 | async-start | bytes 1048576 | tf_op jit(solution)/shard_map/all_to_all | solution.py:210
  24.3 0.1 reshape.62.ids
  24.4 1.9 copy-done.4
  26.3 2.0 %pick.2 = bf16[16,2,16,1024]{3,2,1,0:T(8,128)(2,1)} custom-call(s32[256]{0:T(256)S(1)} %reshape.62.ids, bf16[16,100352]{1,0:T(8,128)(2,1)S(1)} %copy-done.4), custom_call_target="tpu_custom_call" | custom-call | tf_op jit(solution)/shard_map/pick/pallas_call | solution.py:38
  28.3 10.4 %all-to-all-done.2.cols = bf16[16,1,16,1024]{3,2,1,0:T(8,128)(2,1)} async-done(((bf16[16,1,16,1024]{3,2,1,0:T(8,128)(2,1)}), bf16[16,1,16,1024]{3,2,1,0:T(8,128)(2,1)}, u32[]{:S(2)}, u32[]{:S(2)}) %all-to-all-start.2) | async-done | bytes 524320 | tf_op jit(solution)/shard_map/all_to_all | solution.py:210
  38.8 4.3 %all-to-all-start.1 = ((bf16[16,2,16,1024]{3,2,1,0:T(8,128)(2,1)}), bf16[16,2,16,1024]{3,2,1,0:T(8,128)(2,1)}, u32[]{:S(2)}, u32[]{:S(2)}) async-start(bf16[16,2,16,1024]{3,2,1,0:T(8,128)(2,1)} %pick.2), calls=%async_computation.1 | async-start | bytes 2097152 | tf_op jit(solution)/shard_map/all_to_all | solution.py:210
  43.1 1.5 user_project.3
  44.7 0.8 copy-done.6
  45.5 1.6 collective-permute-start.1
  47.1 19.0 %all-to-all-done.1.cols = bf16[16,2,16,1024]{3,2,1,0:T(8,128)(2,1)} async-done(((bf16[16,2,16,1024]{3,2,1,0:T(8,128)(2,1)}), bf16[16,2,16,1024]{3,2,1,0:T(8,128)(2,1)}, u32[]{:S(2)}, u32[]{:S(2)}) %all-to-all-start.1) | async-done | bytes 1048608 | tf_op jit(solution)/shard_map/all_to_all | solution.py:210
  66.1 2.0 %user_project.2 = f32[2,512,256]{2,1,0:T(8,128)S(1)} custom-call(bf16[2,8,512,128]{3,2,1,0:T(8,128)(2,1)S(1)} %bitcast.50, bf16[16,2,16,1024]{3,2,1,0:T(8,128)(2,1)} %all-to-all-done.1.cols), custom_call_target="tpu_custom_call" | custom-call | tf_op jit(solution)/shard_map/user_project/pallas_call | solution.py:68
  68.1 0.8 convert_element_type.83
  69.0 1.5 collective-permute-start
  70.5 1.8 collective-permute-start.3
  72.4 3.3 %collective-permute-start.9 = (bf16[256,256]{1,0:T(8,128)(2,1)S(1)}, bf16[256,256]{1,0:T(8,128)(2,1)S(1)}, u32[]{:S(2)}, u32[]{:S(2)}) collective-permute-start(bf16[256,256]{1,0:T(8,128)(2,1)S(1)} %fusion.4.refs_0_), channel_id=1, source_target_pairs={{0,8},{1,9},{2,10},{3,11},{4,12},{5,13},{6,14},{7,15},{8,0},{9,1},... | collective-permute-start | bytes 393224 | tf_op jit(solution)/shard_map/ppermute | solution.py:230
  75.7 1.5 collective-permute-start.5
  77.2 0.5 collective-permute-start.4
  77.7 3.2 %collective-permute-done.9.refs_8_ = bf16[256,256]{1,0:T(8,128)(2,1)S(1)} collective-permute-done((bf16[256,256]{1,0:T(8,128)(2,1)S(1)}, bf16[256,256]{1,0:T(8,128)(2,1)S(1)}, u32[]{:S(2)}, u32[]{:S(2)}) %collective-permute-start.9) | collective-permute-done | bytes 131104 | tf_op jit(solution)/shard_map/ppermute | solution.py:230
  80.9 2.1 %collective-permute-start.13 = (bf16[256,256]{1,0:T(8,128)(2,1)S(1)}, bf16[256,256]{1,0:T(8,128)(2,1)}, u32[]{:S(2)}, u32[]{:S(2)}) collective-permute-start(bf16[256,256]{1,0:T(8,128)(2,1)S(1)} %collective-permute-done.9.refs_8_), channel_id=1, source_target_pairs={{0,4},{1,5},{2,6},{3,7},{4,0},{5,1},{6,2},{7,3},{8,12},{9,13},{10,... | collective-permute-start | bytes 393224 | tf_op jit(solution)/shard_map/ppermute | solution.py:230
  83.1 0.6 copy-done.8
  83.7 1.6 collective-permute-start.7
  85.4 0.7 copy-done.10
  86.0 0.4 collective-permute-start.11
  86.4 2.0 collective-permute-start.15
  88.4 0.1 reshape.64.observed
  88.5 1.8 collective-permute-done.7.refs_6_
  90.3 2.8 %collective-permute-done.11.refs_10_ = bf16[256,256]{1,0:T(8,128)(2,1)} collective-permute-done((bf16[256,256]{1,0:T(8,128)(2,1)S(1)}, bf16[256,256]{1,0:T(8,128)(2,1)}, u32[]{:S(2)}, u32[]{:S(2)}) %collective-permute-start.11) | collective-permute-done | bytes 131104 | tf_op jit(solution)/shard_map/ppermute | solution.py:230
  93.1 2.4 %collective-permute-done.15.refs_14_ = bf16[256,256]{1,0:T(8,128)(2,1)} collective-permute-done((bf16[256,256]{1,0:T(8,128)(2,1)}, bf16[256,256]{1,0:T(8,128)(2,1)}, u32[]{:S(2)}, u32[]{:S(2)}) %collective-permute-start.15) | collective-permute-done | bytes 131104 | tf_op jit(solution)/shard_map/ppermute | solution.py:230
  95.6 0.5 collective-permute-start.16
  96.1 1.2 add_convert_fusion.2.users
  97.3 3.4 %copy-done.1 = bf16[1024,1,4096]{2,0,1:T(8,128)(2,1)S(1)} copy-done((bf16[1024,1,4096]{2,0,1:T(8,128)(2,1)S(1)}, bf16[1024,1,4096]{2,0,1:T(8,128)(2,1)}, u32[]{:S(2)}) %copy-start.1) | copy-done | bytes 8388632
  100.7 12.4 %rate.1 = (f32[2,512,256]{2,1,0:T(8,128)S(1)}, bf16[8,256,256]{2,1,0:T(8,128)(2,1)S(1)}, bf16[8,256,256]{2,1,0:T(8,128)(2,1)S(1)}) custom-call(s32[1]{0:T(128)} %bitcast.2.me, s32[32]{0:T(128)S(1)} %reshape.64.observed, bf16[2,512,256]{2,1,0:T(8,128)(2,1)S(1)} %add_convert_fusion.2.users, bf16[256,256]{1,0:T(8,128)(2,1)S(1)} %fusion.4.refs_0_, ...), custom_call_target="tpu_custom_call" | custom-call | tf_op jit(solution)/shard_map/rate/pallas_call | solution.py:180
  113.1 0.1 collective-permute-start.18
  113.2 0.6 collective-permute-start.17
  113.8 2.0 %collective-permute-done.18 = bf16[8,256,256]{2,1,0:T(8,128)(2,1)S(1)} collective-permute-done((bf16[8,256,256]{2,1,0:T(8,128)(2,1)S(1)}, bf16[8,256,256]{2,1,0:T(8,128)(2,1)S(1)}, u32[]{:S(2)}, u32[]{:S(2)}) %collective-permute-start.18) | collective-permute-done | bytes 1048608 | tf_op jit(solution)/shard_map/ppermute | solution.py:259
  115.8 0.3 add_convert_fusion
  116.1 0.9 slice_bitcast_fusion
  117.0 1.0 collective-permute-start.19
  118.1 9.5 %collective-permute-done.17 = bf16[2,512,256]{2,1,0:T(8,128)(2,1)S(1)} collective-permute-done((bf16[2,512,256]{2,1,0:T(8,128)(2,1)S(1)}, bf16[2,512,256]{2,1,0:T(8,128)(2,1)S(1)}, u32[]{:S(2)}, u32[]{:S(2)}) %collective-permute-start.17) | collective-permute-done | bytes 524320 | tf_op jit(solution)/shard_map/ppermute | solution.py:207
  127.6 0.1 add_convert_fusion.1.grads
  127.8 1.7 grad_blocks.2
  129.5 5.8 %all-to-all-start.3 = ((bf16[16,2,16,1024]{3,2,1,0:T(8,128)(2,1)}), bf16[16,2,16,1024]{3,2,1,0:T(8,128)(2,1)S(1)}, u32[]{:S(2)}, u32[]{:S(2)}) async-start(bf16[16,2,16,1024]{3,2,1,0:T(8,128)(2,1)} %grad_blocks.2), calls=%async_computation.3 | async-start | bytes 2097152 | tf_op jit(solution)/shard_map/all_to_all | solution.py:210
  135.3 1.2 fusion
  136.5 2.0 %collective-permute-start.20 = (bf16[2,256,256]{2,1,0:T(8,128)(2,1)S(1)}, bf16[2,256,256]{2,1,0:T(8,128)(2,1)S(1)}, u32[]{:S(2)}, u32[]{:S(2)}) collective-permute-start(bf16[2,256,256]{2,1,0:T(8,128)(2,1)S(1)} %slice_bitcast_fusion.2), channel_id=1, source_target_pairs={{0,4},{1,5},{2,6},{3,7},{4,0},{5,1},{6,2},{7,3},{8,12},{9,13},{10,... | collective-permute-start | bytes 786440 | tf_op jit(solution)/shard_map/ppermute | solution.py:259
  138.5 22.3 %collective-permute-done.20 = bf16[2,256,256]{2,1,0:T(8,128)(2,1)S(1)} collective-permute-done((bf16[2,256,256]{2,1,0:T(8,128)(2,1)S(1)}, bf16[2,256,256]{2,1,0:T(8,128)(2,1)S(1)}, u32[]{:S(2)}, u32[]{:S(2)}) %collective-permute-start.20) | collective-permute-done | bytes 262176 | tf_op jit(solution)/shard_map/ppermute | solution.py:259
  160.8 0.1 fusion.2
  160.9 2.6 %collective-permute-start.21 = (bf16[1,256,256]{2,1,0:T(8,128)(2,1)S(1)}, bf16[1,256,256]{2,1,0:T(8,128)(2,1)S(1)}, u32[]{:S(2)}, u32[]{:S(2)}) collective-permute-start(bf16[1,256,256]{2,1,0:T(8,128)(2,1)S(1)} %slice_bitcast_fusion.4), channel_id=1, source_target_pairs={{0,8},{1,9},{2,10},{3,11},{4,12},{5,13},{6,14},{7,15},{8,0},{9,1},... | collective-permute-start | bytes 393224 | tf_op jit(solution)/shard_map/ppermute | solution.py:259
  163.5 6.2 %collective-permute-done.21 = bf16[1,256,256]{2,1,0:T(8,128)(2,1)S(1)} collective-permute-done((bf16[1,256,256]{2,1,0:T(8,128)(2,1)S(1)}, bf16[1,256,256]{2,1,0:T(8,128)(2,1)S(1)}, u32[]{:S(2)}, u32[]{:S(2)}) %collective-permute-start.21) | collective-permute-done | bytes 131104 | tf_op jit(solution)/shard_map/ppermute | solution.py:259
  169.8 0.6 collective-permute-start.22
  170.3 4.6 %collective-permute-done.22 = bf16[256,256]{1,0:T(8,128)(2,1)S(1)} collective-permute-done((bf16[256,256]{1,0:T(8,128)(2,1)S(1)}, bf16[256,256]{1,0:T(8,128)(2,1)S(1)}, u32[]{:S(2)}, u32[]{:S(2)}) %collective-permute-start.22) | collective-permute-done | bytes 131104 | tf_op jit(solution)/shard_map/ppermute | solution.py:207
  175.0 1.3 grad_blocks.3
  176.2 4.5 %all-to-all-start.4 = ((bf16[16,1,16,1024]{3,2,1,0:T(8,128)(2,1)}), bf16[16,1,16,1024]{3,2,1,0:T(8,128)(2,1)S(1)}, u32[]{:S(2)}, u32[]{:S(2)}) async-start(bf16[16,1,16,1024]{3,2,1,0:T(8,128)(2,1)} %grad_blocks.3), calls=%async_computation.4 | async-start | bytes 1048576 | tf_op jit(solution)/shard_map/all_to_all | solution.py:210
  180.8 4.8 %gather_grads.2 = f32[16,100352]{1,0:T(8,128)} custom-call(s32[256]{0:T(256)S(1)} %reshape.62.ids, bf16[16,2,16,1024]{3,2,1,0:T(8,128)(2,1)S(1)} %all-to-all-done.3.back), custom_call_target="tpu_custom_call" | custom-call | tf_op jit(solution)/shard_map/gather_grads/pallas_call | solution.py:116
  185.5 9.7 %all-to-all-done.4.back = bf16[16,1,16,1024]{3,2,1,0:T(8,128)(2,1)S(1)} async-done(((bf16[16,1,16,1024]{3,2,1,0:T(8,128)(2,1)}), bf16[16,1,16,1024]{3,2,1,0:T(8,128)(2,1)S(1)}, u32[]{:S(2)}, u32[]{:S(2)}) %all-to-all-start.4) | async-done | bytes 524320 | tf_op jit(solution)/shard_map/all_to_all | solution.py:210
  195.2 3.0 %gather_grads.3 = f32[16,50176]{1,0:T(8,128)} custom-call(s32[128]{0:T(128)S(1)} %reshape.65.ids, bf16[16,1,16,1024]{3,2,1,0:T(8,128)(2,1)S(1)} %all-to-all-done.4.back), custom_call_target="tpu_custom_call" | custom-call | tf_op jit(solution)/shard_map/gather_grads/pallas_call | solution.py:116
  (54 shorter events, 0.4 us)
Async XLA Ops:
  17.0 1.4 copy-start.5
  20.1 18.7 %all-to-all-start.2 = ((bf16[16,1,16,1024]{3,2,1,0:T(8,128)(2,1)}), bf16[16,1,16,1024]{3,2,1,0:T(8,128)(2,1)}, u32[]{:S(2)}, u32[]{:S(2)}) async-start(bf16[16,1,16,1024]{3,2,1,0:T(8,128)(2,1)} %pick.3), calls=%async_computation.2 | async-start | bytes 1048576 | tf_op jit(solution)/shard_map/all_to_all | solution.py:210
  24.4 1.9 copy-start.4
  26.3 16.8 %copy-start.2 = (bf16[1,1,8,512,128]{4,3,2,1,0:T(8,128)(2,1)S(1)}, bf16[1,1,8,512,128]{4,3,2,1,0:T(8,128)(2,1)}, u32[]{:S(2)}) copy-start(bf16[1,1,8,512,128]{4,3,2,1,0:T(8,128)(2,1)} %param.10) | copy-start | bytes 3145732
  28.3 37.7 %copy-start = (bf16[2,1,8,512,128]{4,3,2,1,0:T(8,128)(2,1)S(1)}, bf16[2,1,8,512,128]{4,3,2,1,0:T(8,128)(2,1)}, u32[]{:S(2)}) copy-start(bf16[2,1,8,512,128]{4,3,2,1,0:T(8,128)(2,1)} %param.8) | copy-start | bytes 6291460
  38.8 27.3 %all-to-all-start.1 = ((bf16[16,2,16,1024]{3,2,1,0:T(8,128)(2,1)}), bf16[16,2,16,1024]{3,2,1,0:T(8,128)(2,1)}, u32[]{:S(2)}, u32[]{:S(2)}) async-start(bf16[16,2,16,1024]{3,2,1,0:T(8,128)(2,1)} %pick.2), calls=%async_computation.1 | async-start | bytes 2097152 | tf_op jit(solution)/shard_map/all_to_all | solution.py:210
  44.7 0.8 copy-start.6
  45.5 25.0 %collective-permute-start.1 = (bf16[256,256]{1,0:T(8,128)(2,1)S(1)}, bf16[256,256]{1,0:T(8,128)(2,1)S(1)}, u32[]{:S(2)}, u32[]{:S(2)}) collective-permute-start(bf16[256,256]{1,0:T(8,128)(2,1)S(1)} %fusion.5), channel_id=1, source_target_pairs={{0,16},{16,0},{1,17},{17,1},{2,18},{18,2},{3,19},{19,3},{4,20},{20... | collective-permute-start | bytes 393224 | tf_op jit(solution)/shard_map/ppermute | solution.py:207
  66.1 4.4 %copy-start.7 = (f32[1,512,256]{2,1,0:T(8,128)S(1)}, f32[1,512,256]{2,1,0:T(8,128)}, u32[]{:S(2)}) copy-start(f32[1,512,256]{2,1,0:T(8,128)} %copy-done.6) | copy-start | bytes 1572868
  68.1 20.3 %copy-start.14 = (s32[2,16]{1,0:T(2,128)S(1)}, s32[2,16]{1,0:T(2,128)}, u32[]{:S(2)}) copy-start(s32[2,16]{1,0:T(2,128)} %param.14) | copy-start | bytes 388
  69.0 26.6 %collective-permute-start = (bf16[2,512,256]{2,1,0:T(8,128)(2,1)}, bf16[2,512,256]{2,1,0:T(8,128)(2,1)}, u32[]{:S(2)}, u32[]{:S(2)}) collective-permute-start(bf16[2,512,256]{2,1,0:T(8,128)(2,1)} %convert_element_type.83), channel_id=1, source_target_pairs={{0,16},{16,0},{1,17},{17,1},{2,18},{18,2},{3,19},{19,3},{4,20},{20... | collective-permute-start | bytes 1572872 | tf_op jit(solution)/shard_map/ppermute | solution.py:207
  70.5 6.6 %collective-permute-start.3 = (bf16[256,256]{1,0:T(8,128)(2,1)S(1)}, bf16[256,256]{1,0:T(8,128)(2,1)S(1)}, u32[]{:S(2)}, u32[]{:S(2)}) collective-permute-start(bf16[256,256]{1,0:T(8,128)(2,1)S(1)} %fusion.4.refs_0_), channel_id=1, source_target_pairs={{0,2},{1,3},{2,0},{3,1},{4,6},{5,7},{6,4},{7,5},{8,10},{9,11},{10,... | collective-permute-start | bytes 393224 | tf_op jit(solution)/shard_map/ppermute | solution.py:230
  72.4 8.5 %collective-permute-start.9 = (bf16[256,256]{1,0:T(8,128)(2,1)S(1)}, bf16[256,256]{1,0:T(8,128)(2,1)S(1)}, u32[]{:S(2)}, u32[]{:S(2)}) collective-permute-start(bf16[256,256]{1,0:T(8,128)(2,1)S(1)} %fusion.4.refs_0_), channel_id=1, source_target_pairs={{0,8},{1,9},{2,10},{3,11},{4,12},{5,13},{6,14},{7,15},{8,0},{9,1},... | collective-permute-start | bytes 393224 | tf_op jit(solution)/shard_map/ppermute | solution.py:230
  75.7 7.3 %collective-permute-start.5 = (bf16[256,256]{1,0:T(8,128)(2,1)S(1)}, bf16[256,256]{1,0:T(8,128)(2,1)}, u32[]{:S(2)}, u32[]{:S(2)}) collective-permute-start(bf16[256,256]{1,0:T(8,128)(2,1)S(1)} %fusion.4.refs_0_), channel_id=1, source_target_pairs={{0,4},{1,5},{2,6},{3,7},{4,0},{5,1},{6,2},{7,3},{8,12},{9,13},{10,... | collective-permute-start | bytes 393224 | tf_op jit(solution)/shard_map/ppermute | solution.py:230
  77.1 5.9 %collective-permute-start.2 = (bf16[256,256]{1,0:T(8,128)(2,1)S(1)}, bf16[256,256]{1,0:T(8,128)(2,1)S(1)}, u32[]{:S(2)}, u32[]{:S(2)}) collective-permute-start(bf16[256,256]{1,0:T(8,128)(2,1)S(1)} %fusion.4.refs_0_), channel_id=1, source_target_pairs={{0,1},{1,0},{2,3},{3,2},{4,5},{5,4},{6,7},{7,6},{8,9},{9,8},{10,11... | collective-permute-start | bytes 393224 | tf_op jit(solution)/shard_map/ppermute | solution.py:230
  77.2 8.2 %collective-permute-start.4 = (bf16[256,256]{1,0:T(8,128)(2,1)S(1)}, bf16[256,256]{1,0:T(8,128)(2,1)S(1)}, u32[]{:S(2)}, u32[]{:S(2)}) collective-permute-start(bf16[256,256]{1,0:T(8,128)(2,1)S(1)} %collective-permute-done.3.refs_2_), channel_id=1, source_target_pairs={{0,1},{1,0},{2,3},{3,2},{4,5},{5,4},{6,7},{7,6},{8,9},{9,8},{10,11... | collective-permute-start | bytes 393224 | tf_op jit(solution)/shard_map/ppermute | solution.py:230
  80.9 5.5 %collective-permute-start.13 = (bf16[256,256]{1,0:T(8,128)(2,1)S(1)}, bf16[256,256]{1,0:T(8,128)(2,1)}, u32[]{:S(2)}, u32[]{:S(2)}) collective-permute-start(bf16[256,256]{1,0:T(8,128)(2,1)S(1)} %collective-permute-done.9.refs_8_), channel_id=1, source_target_pairs={{0,4},{1,5},{2,6},{3,7},{4,0},{5,1},{6,2},{7,3},{8,12},{9,13},{10,... | collective-permute-start | bytes 393224 | tf_op jit(solution)/shard_map/ppermute | solution.py:230
  83.0 5.4 %collective-permute-start.6 = (bf16[256,256]{1,0:T(8,128)(2,1)}, bf16[256,256]{1,0:T(8,128)(2,1)}, u32[]{:S(2)}, u32[]{:S(2)}) collective-permute-start(bf16[256,256]{1,0:T(8,128)(2,1)} %collective-permute-done.5.refs_4_), channel_id=1, source_target_pairs={{0,1},{1,0},{2,3},{3,2},{4,5},{5,4},{6,7},{7,6},{8,9},{9,8},{10,11... | collective-permute-start | bytes 393224 | tf_op jit(solution)/shard_map/ppermute | solution.py:230
  83.1 0.7 copy-start.8
  83.7 6.6 %collective-permute-start.7 = (bf16[256,256]{1,0:T(8,128)(2,1)}, bf16[256,256]{1,0:T(8,128)(2,1)}, u32[]{:S(2)}, u32[]{:S(2)}) collective-permute-start(bf16[256,256]{1,0:T(8,128)(2,1)} %collective-permute-done.5.refs_4_), channel_id=1, source_target_pairs={{0,2},{1,3},{2,0},{3,1},{4,6},{5,7},{6,4},{7,5},{8,10},{9,11},{10,... | collective-permute-start | bytes 393224 | tf_op jit(solution)/shard_map/ppermute | solution.py:230
  85.4 0.7 copy-start.10
  86.0 7.1 %collective-permute-start.11 = (bf16[256,256]{1,0:T(8,128)(2,1)S(1)}, bf16[256,256]{1,0:T(8,128)(2,1)}, u32[]{:S(2)}, u32[]{:S(2)}) collective-permute-start(bf16[256,256]{1,0:T(8,128)(2,1)S(1)} %collective-permute-done.9.refs_8_), channel_id=1, source_target_pairs={{0,2},{1,3},{2,0},{3,1},{4,6},{5,7},{6,4},{7,5},{8,10},{9,11},{10,... | collective-permute-start | bytes 393224 | tf_op jit(solution)/shard_map/ppermute | solution.py:230
  86.4 9.2 %collective-permute-start.15 = (bf16[256,256]{1,0:T(8,128)(2,1)}, bf16[256,256]{1,0:T(8,128)(2,1)}, u32[]{:S(2)}, u32[]{:S(2)}) collective-permute-start(bf16[256,256]{1,0:T(8,128)(2,1)} %collective-permute-done.13.refs_12_), channel_id=1, source_target_pairs={{0,2},{1,3},{2,0},{3,1},{4,6},{5,7},{6,4},{7,5},{8,10},{9,11},{10,... | collective-permute-start | bytes 393224 | tf_op jit(solution)/shard_map/ppermute | solution.py:230
  88.4 8.8 %copy-start.9 = (bf16[256,256]{1,0:T(8,128)(2,1)S(1)}, bf16[256,256]{1,0:T(8,128)(2,1)}, u32[]{:S(2)}) copy-start(bf16[256,256]{1,0:T(8,128)(2,1)} %copy-done.8) | copy-start | bytes 393220
  88.5 8.9 %copy-start.11 = (bf16[256,256]{1,0:T(8,128)(2,1)S(1)}, bf16[256,256]{1,0:T(8,128)(2,1)}, u32[]{:S(2)}) copy-start(bf16[256,256]{1,0:T(8,128)(2,1)} %copy-done.10) | copy-start | bytes 393220
  88.5 8.8 %collective-permute-start.10 = (bf16[256,256]{1,0:T(8,128)(2,1)S(1)}, bf16[256,256]{1,0:T(8,128)(2,1)S(1)}, u32[]{:S(2)}, u32[]{:S(2)}) collective-permute-start(bf16[256,256]{1,0:T(8,128)(2,1)S(1)} %collective-permute-done.9.refs_8_), channel_id=1, source_target_pairs={{0,1},{1,0},{2,3},{3,2},{4,5},{5,4},{6,7},{7,6},{8,9},{9,8},{10,11... | collective-permute-start | bytes 393224 | tf_op jit(solution)/shard_map/ppermute | solution.py:230
  90.3 6.9 %collective-permute-start.14 = (bf16[256,256]{1,0:T(8,128)(2,1)}, bf16[256,256]{1,0:T(8,128)(2,1)S(1)}, u32[]{:S(2)}, u32[]{:S(2)}) collective-permute-start(bf16[256,256]{1,0:T(8,128)(2,1)} %collective-permute-done.13.refs_12_), channel_id=1, source_target_pairs={{0,1},{1,0},{2,3},{3,2},{4,5},{5,4},{6,7},{7,6},{8,9},{9,8},{10,11... | collective-permute-start | bytes 393224 | tf_op jit(solution)/shard_map/ppermute | solution.py:230
  93.1 4.1 %collective-permute-start.8 = (bf16[256,256]{1,0:T(8,128)(2,1)}, bf16[256,256]{1,0:T(8,128)(2,1)S(1)}, u32[]{:S(2)}, u32[]{:S(2)}) collective-permute-start(bf16[256,256]{1,0:T(8,128)(2,1)} %collective-permute-done.7.refs_6_), channel_id=1, source_target_pairs={{0,1},{1,0},{2,3},{3,2},{4,5},{5,4},{6,7},{7,6},{8,9},{9,8},{10,11... | collective-permute-start | bytes 393224 | tf_op jit(solution)/shard_map/ppermute | solution.py:230
  95.5 1.7 collective-permute-start.12
  95.6 1.7 collective-permute-start.16
  97.3 3.4 %copy-start.1 = (bf16[1024,1,4096]{2,0,1:T(8,128)(2,1)S(1)}, bf16[1024,1,4096]{2,0,1:T(8,128)(2,1)}, u32[]{:S(2)}) copy-start(bf16[1024,1,4096]{2,0,1:T(8,128)(2,1)} %param.15) | copy-start | bytes 25165828
  113.1 2.7 %collective-permute-start.18 = (bf16[8,256,256]{2,1,0:T(8,128)(2,1)S(1)}, bf16[8,256,256]{2,1,0:T(8,128)(2,1)S(1)}, u32[]{:S(2)}, u32[]{:S(2)}) collective-permute-start(bf16[8,256,256]{2,1,0:T(8,128)(2,1)S(1)} %get-tuple-element.7), channel_id=1, source_target_pairs={{0,1},{1,0},{2,3},{3,2},{4,5},{5,4},{6,7},{7,6},{8,9},{9,8},{10,11... | collective-permute-start | bytes 3145736 | tf_op jit(solution)/shard_map/ppermute | solution.py:259
  113.2 14.4 %collective-permute-start.17 = (bf16[2,512,256]{2,1,0:T(8,128)(2,1)S(1)}, bf16[2,512,256]{2,1,0:T(8,128)(2,1)S(1)}, u32[]{:S(2)}, u32[]{:S(2)}) collective-permute-start(bf16[2,512,256]{2,1,0:T(8,128)(2,1)S(1)} %convert_element_type.90), channel_id=1, source_target_pairs={{0,16},{16,0},{1,17},{17,1},{2,18},{18,2},{3,19},{19,3},{4,20},{20... | collective-permute-start | bytes 1572872 | tf_op jit(solution)/shard_map/ppermute | solution.py:207
  116.1 11.6 %copy-start.12 = (bf16[8,256,256]{2,1,0:T(8,128)(2,1)}, bf16[8,256,256]{2,1,0:T(8,128)(2,1)S(1)}, u32[]{:S(2)}) copy-start(bf16[8,256,256]{2,1,0:T(8,128)(2,1)S(1)} %add_convert_fusion) | copy-start | bytes 3145732
  117.0 18.2 %collective-permute-start.19 = (bf16[4,256,256]{2,1,0:T(8,128)(2,1)}, bf16[4,256,256]{2,1,0:T(8,128)(2,1)}, u32[]{:S(2)}, u32[]{:S(2)}) collective-permute-start(bf16[4,256,256]{2,1,0:T(8,128)(2,1)} %slice_bitcast_fusion), channel_id=1, source_target_pairs={{0,2},{1,3},{2,0},{3,1},{4,6},{5,7},{6,4},{7,5},{8,10},{9,11},{10,... | collective-permute-start | bytes 1572872 | tf_op jit(solution)/shard_map/ppermute | solution.py:259
  129.5 5.8 %copy-start.13 = (bf16[8,256,256]{2,1,0:T(8,128)(2,1)S(1)}, bf16[8,256,256]{2,1,0:T(8,128)(2,1)}, u32[]{:S(2)}) copy-start(bf16[8,256,256]{2,1,0:T(8,128)(2,1)} %copy-done.12) | copy-start | bytes 3145732
  129.5 46.7 %all-to-all-start.3 = ((bf16[16,2,16,1024]{3,2,1,0:T(8,128)(2,1)}), bf16[16,2,16,1024]{3,2,1,0:T(8,128)(2,1)S(1)}, u32[]{:S(2)}, u32[]{:S(2)}) async-start(bf16[16,2,16,1024]{3,2,1,0:T(8,128)(2,1)} %grad_blocks.2), calls=%async_computation.3 | async-start | bytes 2097152 | tf_op jit(solution)/shard_map/all_to_all | solution.py:210
  135.2 39.7 %copy-start.3 = (bf16[1,1,8,512,128]{4,3,2,1,0:T(8,128)(2,1)S(1)}, bf16[1,1,8,512,128]{4,3,2,1,0:T(8,128)(2,1)}, u32[]{:S(2)}) copy-start(bf16[1,1,8,512,128]{4,3,2,1,0:T(8,128)(2,1)} %param.10) | copy-start | bytes 3145732
  136.5 24.3 %collective-permute-start.20 = (bf16[2,256,256]{2,1,0:T(8,128)(2,1)S(1)}, bf16[2,256,256]{2,1,0:T(8,128)(2,1)S(1)}, u32[]{:S(2)}, u32[]{:S(2)}) collective-permute-start(bf16[2,256,256]{2,1,0:T(8,128)(2,1)S(1)} %slice_bitcast_fusion.2), channel_id=1, source_target_pairs={{0,4},{1,5},{2,6},{3,7},{4,0},{5,1},{6,2},{7,3},{8,12},{9,13},{10,... | collective-permute-start | bytes 786440 | tf_op jit(solution)/shard_map/ppermute | solution.py:259
  160.9 8.8 %collective-permute-start.21 = (bf16[1,256,256]{2,1,0:T(8,128)(2,1)S(1)}, bf16[1,256,256]{2,1,0:T(8,128)(2,1)S(1)}, u32[]{:S(2)}, u32[]{:S(2)}) collective-permute-start(bf16[1,256,256]{2,1,0:T(8,128)(2,1)S(1)} %slice_bitcast_fusion.4), channel_id=1, source_target_pairs={{0,8},{1,9},{2,10},{3,11},{4,12},{5,13},{6,14},{7,15},{8,0},{9,1},... | collective-permute-start | bytes 393224 | tf_op jit(solution)/shard_map/ppermute | solution.py:259
  169.8 5.1 %collective-permute-start.22 = (bf16[256,256]{1,0:T(8,128)(2,1)S(1)}, bf16[256,256]{1,0:T(8,128)(2,1)S(1)}, u32[]{:S(2)}, u32[]{:S(2)}) collective-permute-start(bf16[256,256]{1,0:T(8,128)(2,1)S(1)} %fusion.6), channel_id=1, source_target_pairs={{0,16},{16,0},{1,17},{17,1},{2,18},{18,2},{3,19},{19,3},{4,20},{20... | collective-permute-start | bytes 393224 | tf_op jit(solution)/shard_map/ppermute | solution.py:207
  176.2 19.0 %all-to-all-start.4 = ((bf16[16,1,16,1024]{3,2,1,0:T(8,128)(2,1)}), bf16[16,1,16,1024]{3,2,1,0:T(8,128)(2,1)S(1)}, u32[]{:S(2)}, u32[]{:S(2)}) async-start(bf16[16,1,16,1024]{3,2,1,0:T(8,128)(2,1)} %grad_blocks.3), calls=%async_computation.4 | async-start | bytes 1048576 | tf_op jit(solution)/shard_map/all_to_all | solution.py:210

commit v2 on v0

v2 whole, which is shorter than its diff:
```python
import functools
import math

import jax
import jax.numpy as jnp
from jax import lax
from jax.experimental import pallas as pl
from jax.experimental.pallas import tpu as pltpu
from jax.sharding import PartitionSpec as P

FBW = 128
F32 = jnp.float32
BF16 = jnp.bfloat16
VMEM = pl.BlockSpec(memory_space=pltpu.VMEM)
SMEM = pl.BlockSpec(memory_space=pltpu.SMEM)
HBM = pl.BlockSpec(memory_space=pltpu.HBM)
ANY = pl.BlockSpec(memory_space=pl.ANY)


def params(mib):
    return pltpu.CompilerParams(vmem_limit_bytes=mib * 1024 * 1024)


def ask_kernel(x_blocks, y_blocks, out):
    rows = [x_blocks[b] for b in range(x_blocks.shape[0])]
    rows += [y_blocks[b] for b in range(y_blocks.shape[0])]
    used = sum(row.shape[1] for row in rows)
    rows.append(jnp.zeros((1, out.shape[2] - used), jnp.int32))
    out[...] = jnp.broadcast_to(jnp.concatenate(rows, axis=1)[None], out.shape)


def ask(x_blocks, y_blocks, peers):
    return pl.pallas_call(
        ask_kernel,
        out_shape=jax.ShapeDtypeStruct((peers, 1, FBW), jnp.int32),
        in_specs=[VMEM, VMEM],
        out_specs=VMEM,
        name="ask",
    )(x_blocks, y_blocks)


def preload_kernel(*refs):
    n = len(refs) // 2
    sems = refs[-1]
    copies = [
        pltpu.make_async_copy(refs[i], refs[n + i], sems.at[i]) for i in range(n)
    ]
    for copy in copies:
        copy.start()
    for copy in copies:
        copy.wait()


def preload(*arrays):
    return pl.pallas_call(
        preload_kernel,
        out_shape=[pltpu.VMEM(array.shape, array.dtype) for array in arrays],
        in_specs=[HBM] * len(arrays),
        out_specs=[VMEM] * len(arrays),
        scratch_shapes=[pltpu.SemaphoreType.DMA((len(arrays),))],
        compiler_params=params(12),
        name="preload",
    )(*[in_hbm(array) for array in arrays])


def pick_kernel(first, nb, ids, item_table, user_weights, out, user_table, sem, table_sem):
    peers, _, width = out.shape
    kb = width // FBW // (1 + nb)
    fetch_users = pltpu.make_async_copy(user_weights, user_table, table_sem)
    fetch_users.start()

    def picks(source, ids_at, to):
        def one(p, carry):
            for k in range(kb):
                at = pl.multiple_of(ids[p, 0, ids_at + k] * FBW, FBW)
                pltpu.make_async_copy(
                    source.at[:, pl.ds(at, FBW)], out.at[p, :, pl.ds((to + k) * FBW, FBW)], sem
                ).start()
            return carry

        lax.fori_loop(0, peers, one, 0)

    picks(item_table, first, 0)
    fetch_users.wait()
    for b in range(nb):
        picks(user_table, b * kb, (1 + b) * kb)
    pltpu.make_async_copy(out, out, sem).wait()


def pick(ids, item_table, user_weights, first, nb, kb):
    shape = (ids.shape[0], item_table.shape[0], (1 + nb) * kb * FBW)
    return pl.pallas_call(
        functools.partial(pick_kernel, first, nb),
        out_shape=pltpu.HBM(shape, BF16),
        in_specs=[SMEM, VMEM, HBM],
        out_specs=HBM,
        scratch_shapes=[
            pltpu.VMEM(user_weights.shape, BF16),
            pltpu.SemaphoreType.DMA,
            pltpu.SemaphoreType.DMA,
        ],
        compiler_params=params(8),
        name="pick",
    )(ids, item_table, in_hbm(user_weights))


def joined(vals):
    return jnp.concatenate([vals[k] for k in range(vals.shape[0])], axis=1)


def block_spec(vals, b):
    return pl.BlockSpec((1,) + vals.shape[1:], lambda i: (b, 0, 0, 0))


def part_spec(vals, cols, part):
    width = vals.shape[1] * FBW
    return pl.BlockSpec((cols.shape[0], cols.shape[1], width), lambda i: (0, 0, part))


def projected(vals, cols):
    peers, rp, width = cols.shape
    return lax.dot_general(
        joined(vals[0]),
        cols[...].reshape(peers * rp, width),
        (((1,), (1,)), ((), ())),
        preferred_element_type=F32,
    )


def project_kernel(vals, cols, *refs):
    own, send = refs[-2:]
    part = projected(vals, cols)
    own[...] = part
    send[...] = part.astype(BF16)


def project(vals, b, cols, part, follows=()):
    shape = (vals.shape[2], cols.shape[0] * cols.shape[1])
    return pl.pallas_call(
        project_kernel,
        out_shape=(jax.ShapeDtypeStruct(shape, F32), jax.ShapeDtypeStruct(shape, BF16)),
        grid=(1,),
        in_specs=[block_spec(vals, b), part_spec(vals, cols, part)]
        + [ANY] * len(follows),
        out_specs=(VMEM, VMEM),
        compiler_params=params(12),
        name="project",
    )(vals, cols, *follows)


def halves_kernel(feat, vals, cols, own, send):
    share = own.shape[0]
    part = projected(vals, cols)
    low, high = part[:share], part[share:]
    first = feat[0] == 0
    own[...] = jnp.where(first, low, high)
    send[...] = jnp.where(first, high, low).astype(BF16)


def project_halves(feat, vals, cols, part):
    share, rank = vals.shape[2] // 2, cols.shape[0] * cols.shape[1]
    return pl.pallas_call(
        halves_kernel,
        out_shape=(
            jax.ShapeDtypeStruct((share, rank), F32),
            jax.ShapeDtypeStruct((share, rank), BF16),
        ),
        grid=(1,),
        in_specs=[SMEM, block_spec(vals, 0), part_spec(vals, cols, part)],
        out_specs=(VMEM, VMEM),
        compiler_params=params(12),
        name="project_halves",
    )(feat, vals, cols)


def user_grad_kernel(vals, *refs):
    grads, out = refs[: 2 * vals.shape[0]], refs[-1]
    peers, rp, _ = out.shape
    kb = vals.shape[1]
    for b in range(vals.shape[0]):
        own, other = grads[2 * b], grads[2 * b + 1]
        grad = (own[...] + other[...].astype(F32)).astype(BF16)
        blocks = lax.dot_general(
            grad, joined(vals[b]), (((0,), (0,)), ((), ())), preferred_element_type=F32
        )
        out[:, :, b * kb * FBW : (b + 1) * kb * FBW] = blocks.astype(out.dtype).reshape(
            peers, rp, kb * FBW
        )


def user_grad_blocks(grads, vals, peers, follows):
    nb, kb, _, _ = vals.shape
    rank = grads[0].shape[1]
    shape = (peers, rank // peers, nb * kb * FBW)
    return pl.pallas_call(
        user_grad_kernel,
        out_shape=pltpu.HBM(shape, BF16),
        grid=(1,),
        in_specs=[VMEM] * (1 + len(grads)) + [ANY] * len(follows),
        out_specs=pl.BlockSpec(shape, lambda i: (0, 0, 0)),
        compiler_params=params(16),
        name="user_grad_blocks",
    )(vals, *grads, *follows)


def item_grad_kernel(grads, vals, follows, out):
    peers, rp, width = out.shape
    blocks = jnp.dot(grads[...], joined(vals[0]), preferred_element_type=F32)
    out[...] = blocks.astype(out.dtype).reshape(peers, rp, width)


def item_grad_blocks(grads, vals, b, peers, follows):
    _, kb, _, _ = vals.shape
    shape = (peers, grads.shape[0] // peers, kb * FBW)
    return pl.pallas_call(
        item_grad_kernel,
        out_shape=pltpu.HBM(shape, BF16),
        in_specs=[VMEM, block_spec(vals, b), ANY],
        out_specs=pl.BlockSpec(shape, lambda i: (0, 0, 0)),
        grid=(1,),
        compiler_params=params(12),
        name="item_grad_blocks",
    )(grads, vals, follows)


def collect_kernel(first, ids, back, out):
    peers, _, width = back.shape
    out[...] = jnp.zeros_like(out)

    def one(p, carry):
        for k in range(width // FBW):
            at = pl.multiple_of(ids[p, 0, first + k] * FBW, FBW)
            out[:, pl.ds(at, FBW)] += back[p, :, k * FBW : (k + 1) * FBW].astype(F32)
        return carry

    lax.fori_loop(0, peers, one, 0)


def collect(ids, back, first, columns):
    return pl.pallas_call(
        functools.partial(collect_kernel, first),
        out_shape=jax.ShapeDtypeStruct((back.shape[1], columns), F32),
        in_specs=[SMEM, VMEM],
        out_specs=VMEM,
        compiler_params=params(12),
        name="collect",
    )(ids, back)


def rating_columns(rated, g, share):
    if share % FBW == 0:
        return rated
    parts = FBW // share
    picked = rated[:, :share]
    for part in range(1, parts):
        picked = jnp.where(g % parts == part, rated[:, part * share : (part + 1) * share], picked)
    return picked


def place(k, bits):
    index = 0
    for bit in bits:
        index = 2 * index + (k & bit != 0)
    return k & 1, index


def rating_kernel(orders, rank_scale, grad_scale, me, observed, *refs):
    peers = 2 << len(orders[0])
    nb = observed.shape[0]
    parts, refs = refs[: 2 * nb], refs[2 * nb :]
    items, ratings, refs = refs[:peers], refs[peers], refs[peers + 1 :]
    grads, totals, refs = refs[: 2 * nb], refs[2 * nb : 2 * nb + 4], refs[2 * nb + 4 :]
    rated, table, sems, users, users_t, residuals = refs
    share = items[0].shape[0]
    tile, rank = parts[0].shape
    wide = rated.shape[2]
    width = 4

    def fetch(k):
        g = lax.bitwise_xor(me[0], k)
        at = pl.multiple_of(g * share // wide * wide, wide)
        return (
            pltpu.make_async_copy(ratings.at[:, pl.ds(at, wide)], rated.at[k], sems.at[0, k]),
            pltpu.make_async_copy(items[k], table.at[pl.ds(k * share, share), :], sems.at[1, k]),
        )

    for k in range(peers):
        for copy in fetch(k):
            copy.start()
    for b in range(nb):
        own, other = parts[2 * b], parts[2 * b + 1]
        rows = (own[...] + other[...].astype(F32)).astype(BF16)
        users[b * tile : (b + 1) * tile, :] = rows
        users_t[:, b * tile : (b + 1) * tile] = rows.T
    for k in range(peers):
        g = lax.bitwise_xor(me[0], k)
        columns = pl.ds(k * share, share)
        for copy in fetch(k):
            copy.wait()
        for b in range(nb):
            rows = slice(b * tile, (b + 1) * tile)
            seen = observed[b, g]

            @pl.when(seen != 0)
            def _():
                predicted = lax.dot_general(
                    users[rows, :],
                    table[columns, :],
                    (((1,), (1,)), ((), ())),
                    preferred_element_type=F32,
                )
                rating = rating_columns(rated[k, rows, :], g, share).astype(F32)
                residual = (predicted * rank_scale - rating) * seen.astype(F32)
                residuals[rows, columns] = residual.astype(BF16)

            @pl.when(seen == 0)
            def _():
                residuals[rows, columns] = jnp.zeros((tile, share), BF16)

        if k % width == width - 1:
            start = k - width + 1
            terms = jnp.dot(
                users_t[...],
                residuals[:, pl.ds(start * share, width * share)],
                preferred_element_type=F32,
            )
            for j in range(width):
                term = terms[:, j * share : (j + 1) * share] * grad_scale
                for h, order in enumerate(orders):
                    group, index = place(start + j, order)
                    part = term[h * rank // 2 : (h + 1) * rank // 2]
                    totals[2 * h + group][index] = part.astype(BF16)
    step = tile // 4
    for b in range(nb):
        grad, grad_send = grads[2 * b], grads[2 * b + 1]
        for r in range(0, tile, step):
            part = jnp.dot(
                residuals[b * tile + r : b * tile + r + step, :],
                table[...],
                preferred_element_type=F32,
            )
            part = part * grad_scale
            grad[r : r + step, :] = part
            grad_send[r : r + step, :] = part.astype(BF16)


def in_hbm(array):
    return pltpu.with_memory_space_constraint(array, pltpu.HBM)


def rate(orders, me, observed, parts, items, ratings, rank_scale, grad_scale):
    peers = len(items)
    share, rank = items[0].shape
    nb = observed.shape[0]
    tile = parts[0].shape[0]
    quarter = jax.ShapeDtypeStruct((peers // 2, rank // 2, share), BF16)
    outs = [jax.ShapeDtypeStruct((tile, rank), F32), jax.ShapeDtypeStruct((tile, rank), BF16)]
    outs = outs * nb + [quarter] * 4
    return pl.pallas_call(
        functools.partial(rating_kernel, orders, rank_scale, grad_scale),
        out_shape=outs,
        in_specs=[SMEM, SMEM] + [VMEM] * (2 * nb) + [ANY] * peers + [HBM],
        out_specs=[VMEM] * len(outs),
        scratch_shapes=[
            pltpu.VMEM((peers, nb * tile, max(share, FBW)), BF16),
            pltpu.VMEM((peers * share, rank), BF16),
            pltpu.SemaphoreType.DMA((2, peers)),
            pltpu.VMEM((nb * tile, rank), BF16),
            pltpu.VMEM((rank, nb * tile), BF16),
            pltpu.VMEM((nb * tile, peers * share), BF16),
        ],
        compiler_params=params(36),
        name="rate",
    )(me, observed, *parts, *items, in_hbm(ratings))


def after_kernel(*refs):
    pass


def after(arrays, follows):
    n = len(arrays)
    return pl.pallas_call(
        after_kernel,
        out_shape=[jax.ShapeDtypeStruct(array.shape, array.dtype) for array in arrays],
        in_specs=[ANY] * (n + len(follows)),
        out_specs=[ANY] * n,
        input_output_aliases={i: i for i in range(n)},
        name="after",
    )(*arrays, *follows)


def across(n, bit):
    return [(i, i ^ bit) for i in range(n)]


def on_device(n_feat, n_rows, x_vals, x_blocks, y_vals, y_blocks, user_weights, item_weights, observed, ratings):
    x_vals, y_vals = x_vals[:, 0], y_vals[:, 0]
    nb, kbu, tile, _ = x_vals.shape
    ni, kbi, _, _ = y_vals.shape
    rank = user_weights.shape[0] * n_rows
    rank_scale = 1.0 / math.sqrt(rank)
    grad_scale = 1.0 / (tile * math.sqrt(rank))
    share = ni * tile // n_feat
    feat_id = lax.axis_index("feat")
    row_id = lax.axis_index("rows")

    def swap(array):
        return lax.ppermute(array, "feat", across(2, 1))

    def every(array):
        return lax.all_to_all(array, "rows", split_axis=0, concat_axis=0, tiled=True)

    def feat_sum(own, send):
        if n_feat == 2:
            return own, swap(send)
        return lax.psum(own, "feat"), jnp.zeros_like(send)

    ids = every(ask(x_blocks, y_blocks, n_rows))
    (item_table,) = preload(item_weights)
    cols = every(pick(ids, item_table, user_weights, nb * kbu, nb, kbu))
    if n_feat == 2:
        feat = feat_id.reshape(1).astype(jnp.int32)
        own, send = project_halves(feat, y_vals, cols, 0)
        item_share = (own + swap(send).astype(F32)).astype(BF16)
    else:
        own, send = project(y_vals, 0, cols, 0)
        item_share = lax.psum_scatter(own, "feat", scatter_dimension=0, tiled=True).astype(BF16)
    parts = []
    for b in range(nb):
        parts.extend(feat_sum(*project(x_vals, b, cols, 1 + b, (send,))))

    items = {0: item_share}
    bit = n_rows // 2
    while bit:
        for k in list(items):
            items[k + bit] = lax.ppermute(items[k], "rows", across(n_rows, bit))
        bit //= 2
    items = [items[k] for k in range(n_rows)]

    me = row_id.reshape(1).astype(jnp.int32)
    bits = [1 << i for i in range(1, n_rows.bit_length() - 1)]
    orders = [bits, bits[1:] + bits[:1]]
    *grads, first, first_give, second, second_give = rate(
        orders, me, observed, parts, items, ratings[:, 0], rank_scale, grad_scale
    )
    grads = [part for b in range(nb) for part in feat_sum(*grads[2 * b : 2 * b + 2])]

    def plus(a, b):
        return (a.astype(F32) + b.astype(F32)).astype(BF16)

    def give(array, bit):
        return lax.ppermute(array, "rows", across(n_rows, bit))

    sums = [plus(first, give(first_give, 1)), plus(second, give(second_give, 1))]
    for step in range(len(bits)):
        for h, order in enumerate(orders):
            half = sums[h].shape[0] // 2
            sums[h] = plus(sums[h][:half], give(sums[h][half:], order[step]))
        if step == len(bits) - 2:
            user_ask = user_grad_blocks(grads, x_vals, n_rows, sums)
    item_grad = jnp.concatenate([part[0] for part in sums])
    user_back = every(*after([user_ask], [item_grad]))
    if n_feat == 2:
        other = swap(item_grad)
        first = feat_id == 0
        item_grad = jnp.concatenate(
            [jnp.where(first, item_grad, other), jnp.where(first, other, item_grad)], axis=1
        )
    else:
        item_grad = lax.all_gather(item_grad, "feat", axis=1, tiled=True)
    item_back = every(item_grad_blocks(item_grad, y_vals, 0, n_rows, user_back))

    return (
        collect(ids, user_back, 0, user_weights.shape[1]),
        collect(ids, item_back, nb * kbu, item_weights.shape[1]),
    )


def solution(mesh):
    return jax.shard_map(
        functools.partial(on_device, mesh.shape["feat"], mesh.shape["rows"]),
        mesh=mesh,
        in_specs=(
            P("rows", "feat", None, None, None),
            P("rows", "feat", None),
            P("rows", "feat", None, None, None),
            P("rows", "feat", None),
            P("rows", "feat"),
            P("rows", "feat"),
            P("rows", None),
            P("rows", "feat", None),
        ),
        out_specs=(P("rows", "feat"), P("rows", "feat")),
        check_vma=False,
    )
```

time: 337 us -> 185 us (0.55)
  blocking collectives: 169 us -> 0 us
  waiting for transfers between devices: 34.1 us -> 96.4 us
  other arithmetic: 50.5 us -> 1.28 us
  starting transfers between devices: 9.15 us -> 51.5 us
  local copies, waits for them, and re-layouts: 35.3 us -> 1.15 us
  Pallas kernels: 0 us -> 32.8 us
  matrix products: 22.9 us -> 0 us
  between operations: 14 us -> 0.91 us
    all_to_all x2 -> x0, blocking collectives: 59.8 us -> none  [the longest x1 42.7 us: on_device(): lax.all_to_all(user_grad_blocks.astype(jnp.bfloat16), 'rows', split_axis=...]
    psum x2 -> x0, blocking collectives: 59.8 us -> none  [the longest x1 29.9 us: on_device(): user_grad = lax.psum(grad_part, 'feat').astype(jnp.bfloat16)]
    all_gather x3 -> x0, blocking collectives: 49.7 us -> none  [the longest x1 23.3 us: on_device(): lax.all_gather(y_blocks, 'rows', axis=0, tiled=True)]
    scatter-add x2 -> x0, other arithmetic: 44.7 us -> none  [accumulate(): totals.at[:, indices.reshape(-1)].add(returned.reshape(rank_part, -1, FBW))]
    ppermute x0 -> x29, waiting for transfers between devices: none -> 33.1 us  [the longest x15 14.2 us: on_device(): items[k + bit] = lax.ppermute(items[k], 'rows', across(n_rows, bit))]
    pallas_call x0 -> x12, Pallas kernels: none -> 32.8 us  [the longest x1 13.2 us: rate(): pl.pallas_call(functools.partial(rating_kernel, orders, rank_scale, grad_...]
    ppermute x0 -> x29, starting transfers between devices: none -> 29.6 us  [the longest x15 12.1 us: on_device(): items[k + bit] = lax.ppermute(items[k], 'rows', across(n_rows, bit))]
    all_to_all x2 -> x4, waiting for transfers between devices: 34.1 us -> 63.2 us  [every(): lax.all_to_all(array, 'rows', split_axis=0, concat_axis=0, tiled=True)]
  transfers between devices with their start and end apart: 5 -> 33, of which waited for: 2 -> 18; matrix products, arithmetic and copies ran while one was open for 15% -> 0% of each run, Pallas kernels for 0% -> 5%
where the time goes in v2:
time: 185 us; the launch traced here: 184 us
  waiting for transfers between devices  96.4 us (52%)
  starting transfers between devices  51.5 us (28%)
  Pallas kernels  32.8 us (18%)
    all_to_all x4, waiting for transfers between devices, every(): lax.all_to_all(array, 'rows', split_axis=0, concat_axis=0, tiled=True)  63.2 us
    all_to_all x4, starting transfers between devices, every(): lax.all_to_all(array, 'rows', split_axis=0, concat_axis=0, tiled=True)  22 us
    ppermute x15, waiting for transfers between devices, on_device(): items[k + bit] = lax.ppermute(items[k], 'rows', across(n_rows, bit))  14.2 us
    pallas_call x1, Pallas kernels, rate(): pl.pallas_call(functools.partial(rating_kernel, orders, rank_scale, grad_...  13.2 us
    ppermute x8, waiting for transfers between devices, give(): return lax.ppermute(array, 'rows', across(n_rows, bit))  13.1 us
    ppermute x15, starting transfers between devices, on_device(): items[k + bit] = lax.ppermute(items[k], 'rows', across(n_rows, bit))  12.1 us
    ppermute x8, starting transfers between devices, give(): return lax.ppermute(array, 'rows', across(n_rows, bit))  9.93 us
    pallas_call x2, Pallas kernels, collect(): pl.pallas_call(functools.partial(collect_kernel, first), out_shape=jax.Sh...  8.07 us
  transfers between devices with their start and end apart: 33, of which 18 were waited for; matrix products, arithmetic and copies ran while one was open for 0% of the time, Pallas kernels for 5%

profile of v2, /device:TPU:0, one launch (start us, length us, event | category | flops | bytes accessed | tf_op | source)
XLA Modules:
  0.0 184.0 jit_solution(3562267248000198802)
XLA Ops:
  0.6 1.4 ask.1
  2.0 7.4 %all-to-all-start = ((s32[16,1,128]{2,1,0:T(1,128)}), s32[16,1,128]{2,1,0:T(1,128)S(1)}, u32[]{:S(2)}, u32[]{:S(2)}) async-start(s32[16,1,128]{2,1,0:T(1,128)} %ask.1), calls=%async_computation | async-start | bytes 16384 | tf_op jit(solution)/shard_map/all_to_all | solution.py:412
  9.3 1.4 preload.1.item_table
  10.8 4.9 %all-to-all-done.ids = s32[16,1,128]{2,1,0:T(1,128)S(1)} async-done(((s32[16,1,128]{2,1,0:T(1,128)}), s32[16,1,128]{2,1,0:T(1,128)S(1)}, u32[]{:S(2)}, u32[]{:S(2)}) %all-to-all-start) | async-done | bytes 8224 | tf_op jit(solution)/shard_map/all_to_all | solution.py:412
  15.7 4.3 %pick.1 = bf16[16,16,3072]{2,1,0:T(8,128)(2,1)} custom-call(s32[16,1,128]{2,1,0:T(1,128)S(1)} %all-to-all-done.ids, bf16[16,50176]{1,0:T(8,128)(2,1)S(1)} %preload.1.item_table, bf16[16,100352]{1,0:T(8,128)(2,1)} %user_weights.1), custom_call_target="tpu_custom_call" | custom-call | tf_op jit(solution)/shard_map/pick/pallas_call | solution.py:92
  20.0 0.0 copy-start.2
  20.0 3.9 %all-to-all-start.1 = ((bf16[16,16,3072]{2,1,0:T(8,128)(2,1)}), bf16[16,16,3072]{2,1,0:T(8,128)(2,1)S(1)}, u32[]{:S(2)}, u32[]{:S(2)}) async-start(bf16[16,16,3072]{2,1,0:T(8,128)(2,1)} %pick.1), calls=%async_computation.1 | async-start | bytes 3145728 | tf_op jit(solution)/shard_map/all_to_all | solution.py:412
  23.9 31.9 %all-to-all-done.1.cols = bf16[16,16,3072]{2,1,0:T(8,128)(2,1)S(1)} async-done(((bf16[16,16,3072]{2,1,0:T(8,128)(2,1)}), bf16[16,16,3072]{2,1,0:T(8,128)(2,1)S(1)}, u32[]{:S(2)}, u32[]{:S(2)}) %all-to-all-start.1) | async-done | bytes 1572896 | tf_op jit(solution)/shard_map/all_to_all | solution.py:412
  55.8 0.5 project_halves.1
  56.3 1.6 collective-permute-start.2
  57.9 0.5 project.2
  58.4 0.0 copy-start.5
  58.4 1.1 collective-permute-start
  59.5 0.5 project.3
  60.0 0.0 copy-start.3
  60.0 1.0 collective-permute-start.1
  61.0 1.7 collective-permute-done.2
  62.8 7.1 %collective-permute-start.10 = (bf16[256,256]{1,0:T(8,128)(2,1)S(1)}, bf16[256,256]{1,0:T(8,128)(2,1)S(1)}, u32[]{:S(2)}, u32[]{:S(2)}) collective-permute-start(bf16[256,256]{1,0:T(8,128)(2,1)S(1)} %add_convert_fusion.6.refs_4_), channel_id=1, source_target_pairs={{0,8},{1,9},{2,10},{3,11},{4,12},{5,13},{6,14},{7,15},{8,0},{9,1},... | collective-permute-start | bytes 393224 | tf_op jit(solution)/shard_map/ppermute | solution.py:437
  69.8 1.8 collective-permute-start.6
  71.6 3.0 %collective-permute-done.10.refs_12_ = bf16[256,256]{1,0:T(8,128)(2,1)S(1)} collective-permute-done((bf16[256,256]{1,0:T(8,128)(2,1)S(1)}, bf16[256,256]{1,0:T(8,128)(2,1)S(1)}, u32[]{:S(2)}, u32[]{:S(2)}) %collective-permute-start.10) | collective-permute-done | bytes 131104 | tf_op jit(solution)/shard_map/ppermute | solution.py:437
  74.6 0.3 collective-permute-start.14
  74.9 1.1 collective-permute-done.6.refs_8_
  76.1 1.3 collective-permute-start.8
  77.4 0.7 collective-permute-start.12
  78.1 1.5 collective-permute-done.14.refs_16_
  79.5 0.4 collective-permute-start.16
  79.9 0.5 collective-permute-start.15
  80.4 1.9 %collective-permute-done.8.refs_10_ = bf16[256,256]{1,0:T(8,128)(2,1)S(1)} collective-permute-done((bf16[256,256]{1,0:T(8,128)(2,1)S(1)}, bf16[256,256]{1,0:T(8,128)(2,1)S(1)}, u32[]{:S(2)}, u32[]{:S(2)}) %collective-permute-start.8) | collective-permute-done | bytes 131104 | tf_op jit(solution)/shard_map/ppermute | solution.py:437
  82.4 2.8 %collective-permute-done.12.refs_14_ = bf16[256,256]{1,0:T(8,128)(2,1)S(1)} collective-permute-done((bf16[256,256]{1,0:T(8,128)(2,1)S(1)}, bf16[256,256]{1,0:T(8,128)(2,1)S(1)}, u32[]{:S(2)}, u32[]{:S(2)}) %collective-permute-start.12) | collective-permute-done | bytes 131104 | tf_op jit(solution)/shard_map/ppermute | solution.py:437
  85.2 2.4 %collective-permute-done.16.refs_18_ = bf16[256,256]{1,0:T(8,128)(2,1)S(1)} collective-permute-done((bf16[256,256]{1,0:T(8,128)(2,1)S(1)}, bf16[256,256]{1,0:T(8,128)(2,1)S(1)}, u32[]{:S(2)}, u32[]{:S(2)}) %collective-permute-start.16) | collective-permute-done | bytes 131104 | tf_op jit(solution)/shard_map/ppermute | solution.py:437
  87.6 1.4 collective-permute-done.17.refs_19_
  89.1 1.0 copy-done.4
  90.1 13.2 %rate.1 = (f32[512,256]{1,0:T(8,128)S(1)}, bf16[512,256]{1,0:T(8,128)(2,1)S(1)}, f32[512,256]{1,0:T(8,128)S(1)}, bf16[512,256]{1,0:T(8,128)(2,1)S(1)}, bf16[8,12...) custom-call(s32[1]{0:T(128)} %bitcast.1.me, ...), custom_call_target="tpu_custom_call" | custom-call | tf_op jit(solution)/shard_map/rate/pallas_call | solution.py:359
  103.4 0.1 collective-permute-start.23
  103.4 0.5 collective-permute-start.20
  103.9 1.4 collective-permute-done.23
  105.3 0.1 add_convert_fusion
  105.5 2.5 %collective-permute-start.24 = (bf16[4,128,256]{2,1,0:T(8,128)(2,1)S(1)}, bf16[4,128,256]{2,1,0:T(8,128)(2,1)S(1)}, u32[]{:S(2)}, u32[]{:S(2)}) collective-permute-start(bf16[4,128,256]{2,1,0:T(8,128)(2,1)S(1)} %slice.53), channel_id=1, source_target_pairs={{0,4},{1,5},{2,6},{3,7},{4,0},{5,1},{6,2},{7,3},{8,12},{9,13},{10,... | collective-permute-start | bytes 786440 | tf_op jit(solution)/shard_map/ppermute | solution.py:453
  108.0 0.1 add_convert_fusion.1
  108.1 0.0 copy-start.1
  108.2 1.8 collective-permute-start.21
  110.0 1.5 collective-permute-start.18
  111.5 0.5 collective-permute-start.19
  112.0 2.8 %collective-permute-done.24 = bf16[4,128,256]{2,1,0:T(8,128)(2,1)S(1)} collective-permute-done((bf16[4,128,256]{2,1,0:T(8,128)(2,1)S(1)}, bf16[4,128,256]{2,1,0:T(8,128)(2,1)S(1)}, u32[]{:S(2)}, u32[]{:S(2)}) %collective-permute-start.24) | collective-permute-done | bytes 262176 | tf_op jit(solution)/shard_map/ppermute | solution.py:453
  114.8 0.1 add_convert_fusion.2
  114.9 1.7 collective-permute-start.25
  116.6 0.1 add_convert_fusion.3
  116.7 1.8 collective-permute-start.22
  118.5 5.3 %collective-permute-done.25 = bf16[2,128,256]{2,1,0:T(8,128)(2,1)S(1)} collective-permute-done((bf16[2,128,256]{2,1,0:T(8,128)(2,1)S(1)}, bf16[2,128,256]{2,1,0:T(8,128)(2,1)S(1)}, u32[]{:S(2)}, u32[]{:S(2)}) %collective-permute-start.25) | collective-permute-done | bytes 131104 | tf_op jit(solution)/shard_map/ppermute | solution.py:453
  123.9 1.4 collective-permute-start.27
  125.4 0.1 collective-permute-start.26
  125.5 1.7 user_grad_blocks.1.refs_0_
  127.3 1.0 collective-permute-done.27
  128.3 2.5 %collective-permute-done.26 = bf16[1,128,256]{2,1,0:T(8,128)(2,1)S(1)} collective-permute-done((bf16[1,128,256]{2,1,0:T(8,128)(2,1)S(1)}, bf16[1,128,256]{2,1,0:T(8,128)(2,1)S(1)}, u32[]{:S(2)}, u32[]{:S(2)}) %collective-permute-start.26) | collective-permute-done | bytes 65568 | tf_op jit(solution)/shard_map/ppermute | solution.py:453
  130.8 0.7 pad_maximum_fusion.1.refs_1_
  131.5 3.9 %all-to-all-start.2 = ((bf16[16,16,2048]{2,1,0:T(8,128)(2,1)}), bf16[16,16,2048]{2,1,0:T(8,128)(2,1)S(1)}, u32[]{:S(2)}, u32[]{:S(2)}) async-start(bf16[16,16,2048]{2,1,0:T(8,128)(2,1)} %after.1), calls=%async_computation.2 | async-start | bytes 2097152 | tf_op jit(solution)/shard_map/all_to_all | solution.py:412
  135.4 1.8 collective-permute-start.28
  137.2 4.1 %collective-permute-done.28 = bf16[256,256]{1,0:T(8,128)(2,1)S(1)} collective-permute-done((bf16[256,256]{1,0:T(8,128)(2,1)S(1)}, bf16[256,256]{1,0:T(8,128)(2,1)S(1)}, u32[]{:S(2)}, u32[]{:S(2)}) %collective-permute-start.28) | collective-permute-done | bytes 131104 | tf_op jit(solution)/shard_map/ppermute | solution.py:409
  141.4 17.0 %all-to-all-done.2.back.follows = bf16[16,16,2048]{2,1,0:T(8,128)(2,1)S(1)} async-done(((bf16[16,16,2048]{2,1,0:T(8,128)(2,1)}), bf16[16,16,2048]{2,1,0:T(8,128)(2,1)S(1)}, u32[]{:S(2)}, u32[]{:S(2)}) %all-to-all-start.2) | async-done | bytes 1048608 | tf_op jit(solution)/shard_map/all_to_all | solution.py:412
  158.4 1.2 item_grad_blocks.1
  159.6 6.9 %all-to-all-start.3 = ((bf16[16,16,1024]{2,1,0:T(8,128)(2,1)}), bf16[16,16,1024]{2,1,0:T(8,128)(2,1)S(1)}, u32[]{:S(2)}, u32[]{:S(2)}) async-start(bf16[16,16,1024]{2,1,0:T(8,128)(2,1)} %item_grad_blocks.1), calls=%async_computation.3 | async-start | bytes 1048576 | tf_op jit(solution)/shard_map/all_to_all | solution.py:412
  166.5 5.0 %collect.2 = f32[16,100352]{1,0:T(8,128)} custom-call(s32[16,1,128]{2,1,0:T(1,128)S(1)} %all-to-all-done.ids, bf16[16,16,2048]{2,1,0:T(8,128)(2,1)S(1)} %all-to-all-done.2.back.follows), custom_call_target="tpu_custom_call" | custom-call | tf_op jit(solution)/shard_map/collect/pallas_call | solution.py:240
  171.5 9.5 %all-to-all-done.3.back = bf16[16,16,1024]{2,1,0:T(8,128)(2,1)S(1)} async-done(((bf16[16,16,1024]{2,1,0:T(8,128)(2,1)}), bf16[16,16,1024]{2,1,0:T(8,128)(2,1)S(1)}, u32[]{:S(2)}, u32[]{:S(2)}) %all-to-all-start.3) | async-done | bytes 524320 | tf_op jit(solution)/shard_map/all_to_all | solution.py:412
  180.9 3.1 %collect.3 = f32[16,50176]{1,0:T(8,128)} custom-call(s32[16,1,128]{2,1,0:T(1,128)S(1)} %all-to-all-done.ids, bf16[16,16,1024]{2,1,0:T(8,128)(2,1)S(1)} %all-to-all-done.3.back), custom_call_target="tpu_custom_call" | custom-call | tf_op jit(solution)/shard_map/collect/pallas_call | solution.py:240
  (46 shorter events, 0.3 us)
Async XLA Ops:
  2.0 13.7 %all-to-all-start = ((s32[16,1,128]{2,1,0:T(1,128)}), s32[16,1,128]{2,1,0:T(1,128)S(1)}, u32[]{:S(2)}, u32[]{:S(2)}) async-start(s32[16,1,128]{2,1,0:T(1,128)} %ask.1), calls=%async_computation | async-start | bytes 16384 | tf_op jit(solution)/shard_map/all_to_all | solution.py:412
  20.0 35.8 %copy-start.2 = (bf16[1,1,8,512,128]{4,3,2,1,0:T(8,128)(2,1)S(1)}, bf16[1,1,8,512,128]{4,3,2,1,0:T(8,128)(2,1)}, u32[]{:S(2)}) copy-start(bf16[1,1,8,512,128]{4,3,2,1,0:T(8,128)(2,1)} %param.10) | copy-start | bytes 3145732
  20.0 35.8 %all-to-all-start.1 = ((bf16[16,16,3072]{2,1,0:T(8,128)(2,1)}), bf16[16,16,3072]{2,1,0:T(8,128)(2,1)S(1)}, u32[]{:S(2)}, u32[]{:S(2)}) async-start(bf16[16,16,3072]{2,1,0:T(8,128)(2,1)} %pick.1), calls=%async_computation.1 | async-start | bytes 3145728 | tf_op jit(solution)/shard_map/all_to_all | solution.py:412
  55.8 2.1 %copy-start = (bf16[2,1,8,512,128]{4,3,2,1,0:T(8,128)(2,1)S(1)}, bf16[2,1,8,512,128]{4,3,2,1,0:T(8,128)(2,1)}, u32[]{:S(2)}) copy-start(bf16[2,1,8,512,128]{4,3,2,1,0:T(8,128)(2,1)} %param.8) | copy-start | bytes 6291460
  56.3 6.4 %collective-permute-start.2 = (bf16[256,256]{1,0:T(8,128)(2,1)S(1)}, bf16[256,256]{1,0:T(8,128)(2,1)S(1)}, u32[]{:S(2)}, u32[]{:S(2)}) collective-permute-start(bf16[256,256]{1,0:T(8,128)(2,1)S(1)} %get-tuple-element.16.refs_0_), channel_id=1, source_target_pairs={{0,16},{16,0},{1,17},{17,1},{2,18},{18,2},{3,19},{19,3},{4,20},{20... | collective-permute-start | bytes 393224 | tf_op jit(solution)/shard_map/ppermute | solution.py:409
  58.4 30.7 %copy-start.5 = (s32[2,16]{1,0:T(2,128)S(1)}, s32[2,16]{1,0:T(2,128)}, u32[]{:S(2)}) copy-start(s32[2,16]{1,0:T(2,128)} %observed.1) | copy-start | bytes 388
  58.4 13.2 %collective-permute-start = (bf16[512,256]{1,0:T(8,128)(2,1)S(1)}, bf16[512,256]{1,0:T(8,128)(2,1)S(1)}, u32[]{:S(2)}, u32[]{:S(2)}) collective-permute-start(bf16[512,256]{1,0:T(8,128)(2,1)S(1)} %get-tuple-element.18), channel_id=1, source_target_pairs={{0,16},{16,0},{1,17},{17,1},{2,18},{18,2},{3,19},{19,3},{4,20},{20... | collective-permute-start | bytes 786440 | tf_op jit(solution)/shard_map/ppermute | solution.py:409
  60.0 17.4 %copy-start.3 = (f32[512,256]{1,0:T(8,128)}, f32[512,256]{1,0:T(8,128)S(1)}, u32[]{:S(2)}) copy-start(f32[512,256]{1,0:T(8,128)S(1)} %get-tuple-element.19.refs_2_) | copy-start | bytes 1572868
  60.0 16.1 %collective-permute-start.1 = (bf16[512,256]{1,0:T(8,128)(2,1)S(1)}, bf16[512,256]{1,0:T(8,128)(2,1)S(1)}, u32[]{:S(2)}, u32[]{:S(2)}) collective-permute-start(bf16[512,256]{1,0:T(8,128)(2,1)S(1)} %get-tuple-element.20), channel_id=1, source_target_pairs={{0,16},{16,0},{1,17},{17,1},{2,18},{18,2},{3,19},{19,3},{4,20},{20... | collective-permute-start | bytes 786440 | tf_op jit(solution)/shard_map/ppermute | solution.py:409
  62.8 11.8 %collective-permute-start.10 = (bf16[256,256]{1,0:T(8,128)(2,1)S(1)}, bf16[256,256]{1,0:T(8,128)(2,1)S(1)}, u32[]{:S(2)}, u32[]{:S(2)}) collective-permute-start(bf16[256,256]{1,0:T(8,128)(2,1)S(1)} %add_convert_fusion.6.refs_4_), channel_id=1, source_target_pairs={{0,8},{1,9},{2,10},{3,11},{4,12},{5,13},{6,14},{7,15},{8,0},{9,1},... | collective-permute-start | bytes 393224 | tf_op jit(solution)/shard_map/ppermute | solution.py:437
  69.8 5.1 %collective-permute-start.4 = (bf16[256,256]{1,0:T(8,128)(2,1)S(1)}, bf16[256,256]{1,0:T(8,128)(2,1)S(1)}, u32[]{:S(2)}, u32[]{:S(2)}) collective-permute-start(bf16[256,256]{1,0:T(8,128)(2,1)S(1)} %add_convert_fusion.6.refs_4_), channel_id=1, source_target_pairs={{0,2},{1,3},{2,0},{3,1},{4,6},{5,7},{6,4},{7,5},{8,10},{9,11},{10,... | collective-permute-start | bytes 393224 | tf_op jit(solution)/shard_map/ppermute | solution.py:437
  69.8 6.2 %collective-permute-start.6 = (bf16[256,256]{1,0:T(8,128)(2,1)S(1)}, bf16[256,256]{1,0:T(8,128)(2,1)S(1)}, u32[]{:S(2)}, u32[]{:S(2)}) collective-permute-start(bf16[256,256]{1,0:T(8,128)(2,1)S(1)} %add_convert_fusion.6.refs_4_), channel_id=1, source_target_pairs={{0,4},{1,5},{2,6},{3,7},{4,0},{5,1},{6,2},{7,3},{8,12},{9,13},{10,... | collective-permute-start | bytes 393224 | tf_op jit(solution)/shard_map/ppermute | solution.py:437
  71.6 5.8 %collective-permute-start.3 = (bf16[256,256]{1,0:T(8,128)(2,1)S(1)}, bf16[256,256]{1,0:T(8,128)(2,1)S(1)}, u32[]{:S(2)}, u32[]{:S(2)}) collective-permute-start(bf16[256,256]{1,0:T(8,128)(2,1)S(1)} %add_convert_fusion.6.refs_4_), channel_id=1, source_target_pairs={{0,1},{1,0},{2,3},{3,2},{4,5},{5,4},{6,7},{7,6},{8,9},{9,8},{10,11... | collective-permute-start | bytes 393224 | tf_op jit(solution)/shard_map/ppermute | solution.py:437
  74.6 5.0 %collective-permute-start.14 = (bf16[256,256]{1,0:T(8,128)(2,1)S(1)}, bf16[256,256]{1,0:T(8,128)(2,1)S(1)}, u32[]{:S(2)}, u32[]{:S(2)}) collective-permute-start(bf16[256,256]{1,0:T(8,128)(2,1)S(1)} %collective-permute-done.10.refs_12_), channel_id=1, source_target_pairs={{0,4},{1,5},{2,6},{3,7},{4,0},{5,1},{6,2},{7,3},{8,12},{9,13},{10,... | collective-permute-start | bytes 393224 | tf_op jit(solution)/shard_map/ppermute | solution.py:437
  74.9 5.0 %collective-permute-start.5 = (bf16[256,256]{1,0:T(8,128)(2,1)S(1)}, bf16[256,256]{1,0:T(8,128)(2,1)S(1)}, u32[]{:S(2)}, u32[]{:S(2)}) collective-permute-start(bf16[256,256]{1,0:T(8,128)(2,1)S(1)} %collective-permute-done.4.refs_6_), channel_id=1, source_target_pairs={{0,1},{1,0},{2,3},{3,2},{4,5},{5,4},{6,7},{7,6},{8,9},{9,8},{10,11... | collective-permute-start | bytes 393224 | tf_op jit(solution)/shard_map/ppermute | solution.py:437
  76.0 3.9 %collective-permute-start.7 = (bf16[256,256]{1,0:T(8,128)(2,1)S(1)}, bf16[256,256]{1,0:T(8,128)(2,1)S(1)}, u32[]{:S(2)}, u32[]{:S(2)}) collective-permute-start(bf16[256,256]{1,0:T(8,128)(2,1)S(1)} %collective-permute-done.6.refs_8_), channel_id=1, source_target_pairs={{0,1},{1,0},{2,3},{3,2},{4,5},{5,4},{6,7},{7,6},{8,9},{9,8},{10,11... | collective-permute-start | bytes 393224 | tf_op jit(solution)/shard_map/ppermute | solution.py:437
  76.1 6.3 %collective-permute-start.8 = (bf16[256,256]{1,0:T(8,128)(2,1)S(1)}, bf16[256,256]{1,0:T(8,128)(2,1)S(1)}, u32[]{:S(2)}, u32[]{:S(2)}) collective-permute-start(bf16[256,256]{1,0:T(8,128)(2,1)S(1)} %collective-permute-done.6.refs_8_), channel_id=1, source_target_pairs={{0,2},{1,3},{2,0},{3,1},{4,6},{5,7},{6,4},{7,5},{8,10},{9,11},{10,... | collective-permute-start | bytes 393224 | tf_op jit(solution)/shard_map/ppermute | solution.py:437
  77.4 7.8 %collective-permute-start.12 = (bf16[256,256]{1,0:T(8,128)(2,1)S(1)}, bf16[256,256]{1,0:T(8,128)(2,1)S(1)}, u32[]{:S(2)}, u32[]{:S(2)}) collective-permute-start(bf16[256,256]{1,0:T(8,128)(2,1)S(1)} %collective-permute-done.10.refs_12_), channel_id=1, source_target_pairs={{0,2},{1,3},{2,0},{3,1},{4,6},{5,7},{6,4},{7,5},{8,10},{9,11},{10,... | collective-permute-start | bytes 393224 | tf_op jit(solution)/shard_map/ppermute | solution.py:437
  79.5 8.0 %collective-permute-start.16 = (bf16[256,256]{1,0:T(8,128)(2,1)S(1)}, bf16[256,256]{1,0:T(8,128)(2,1)S(1)}, u32[]{:S(2)}, u32[]{:S(2)}) collective-permute-start(bf16[256,256]{1,0:T(8,128)(2,1)S(1)} %collective-permute-done.14.refs_16_), channel_id=1, source_target_pairs={{0,2},{1,3},{2,0},{3,1},{4,6},{5,7},{6,4},{7,5},{8,10},{9,11},{10,... | collective-permute-start | bytes 393224 | tf_op jit(solution)/shard_map/ppermute | solution.py:437
  79.9 7.7 %collective-permute-start.11 = (bf16[256,256]{1,0:T(8,128)(2,1)S(1)}, bf16[256,256]{1,0:T(8,128)(2,1)}, u32[]{:S(2)}, u32[]{:S(2)}) collective-permute-start(bf16[256,256]{1,0:T(8,128)(2,1)S(1)} %collective-permute-done.10.refs_12_), channel_id=1, source_target_pairs={{0,1},{1,0},{2,3},{3,2},{4,5},{5,4},{6,7},{7,6},{8,9},{9,8},{10,11... | collective-permute-start | bytes 393224 | tf_op jit(solution)/shard_map/ppermute | solution.py:437
  79.9 7.7 %collective-permute-start.15 = (bf16[256,256]{1,0:T(8,128)(2,1)S(1)}, bf16[256,256]{1,0:T(8,128)(2,1)}, u32[]{:S(2)}, u32[]{:S(2)}) collective-permute-start(bf16[256,256]{1,0:T(8,128)(2,1)S(1)} %collective-permute-done.14.refs_16_), channel_id=1, source_target_pairs={{0,1},{1,0},{2,3},{3,2},{4,5},{5,4},{6,7},{7,6},{8,9},{9,8},{10,11... | collective-permute-start | bytes 393224 | tf_op jit(solution)/shard_map/ppermute | solution.py:437
  82.4 5.2 %collective-permute-start.9 = (bf16[256,256]{1,0:T(8,128)(2,1)S(1)}, bf16[256,256]{1,0:T(8,128)(2,1)}, u32[]{:S(2)}, u32[]{:S(2)}) collective-permute-start(bf16[256,256]{1,0:T(8,128)(2,1)S(1)} %collective-permute-done.8.refs_10_), channel_id=1, source_target_pairs={{0,1},{1,0},{2,3},{3,2},{4,5},{5,4},{6,7},{7,6},{8,9},{9,8},{10,11... | collective-permute-start | bytes 393224 | tf_op jit(solution)/shard_map/ppermute | solution.py:437
  85.2 2.4 %collective-permute-start.13 = (bf16[256,256]{1,0:T(8,128)(2,1)S(1)}, bf16[256,256]{1,0:T(8,128)(2,1)}, u32[]{:S(2)}, u32[]{:S(2)}) collective-permute-start(bf16[256,256]{1,0:T(8,128)(2,1)S(1)} %collective-permute-done.12.refs_14_), channel_id=1, source_target_pairs={{0,1},{1,0},{2,3},{3,2},{4,5},{5,4},{6,7},{7,6},{8,9},{9,8},{10,11... | collective-permute-start | bytes 393224 | tf_op jit(solution)/shard_map/ppermute | solution.py:437
  87.6 1.5 collective-permute-start.17
  89.1 1.0 copy-start.4
  103.4 2.0 %collective-permute-start.23 = (bf16[8,128,256]{2,1,0:T(8,128)(2,1)S(1)}, bf16[8,128,256]{2,1,0:T(8,128)(2,1)S(1)}, u32[]{:S(2)}, u32[]{:S(2)}) collective-permute-start(bf16[8,128,256]{2,1,0:T(8,128)(2,1)S(1)} %get-tuple-element.29), channel_id=1, source_target_pairs={{0,1},{1,0},{2,3},{3,2},{4,5},{5,4},{6,7},{7,6},{8,9},{9,8},{10,11... | collective-permute-start | bytes 1572872 | tf_op jit(solution)/shard_map/ppermute | solution.py:453
  103.4 4.5 %collective-permute-start.20 = (bf16[8,128,256]{2,1,0:T(8,128)(2,1)S(1)}, bf16[8,128,256]{2,1,0:T(8,128)(2,1)S(1)}, u32[]{:S(2)}, u32[]{:S(2)}) collective-permute-start(bf16[8,128,256]{2,1,0:T(8,128)(2,1)S(1)} %get-tuple-element.27), channel_id=1, source_target_pairs={{0,1},{1,0},{2,3},{3,2},{4,5},{5,4},{6,7},{7,6},{8,9},{9,8},{10,11... | collective-permute-start | bytes 1572872 | tf_op jit(solution)/shard_map/ppermute | solution.py:453
  105.5 9.3 %collective-permute-start.24 = (bf16[4,128,256]{2,1,0:T(8,128)(2,1)S(1)}, bf16[4,128,256]{2,1,0:T(8,128)(2,1)S(1)}, u32[]{:S(2)}, u32[]{:S(2)}) collective-permute-start(bf16[4,128,256]{2,1,0:T(8,128)(2,1)S(1)} %slice.53), channel_id=1, source_target_pairs={{0,4},{1,5},{2,6},{3,7},{4,0},{5,1},{6,2},{7,3},{8,12},{9,13},{10,... | collective-permute-start | bytes 786440 | tf_op jit(solution)/shard_map/ppermute | solution.py:453
  108.1 17.4 %copy-start.1 = (bf16[2,1,8,512,128]{4,3,2,1,0:T(8,128)(2,1)S(1)}, bf16[2,1,8,512,128]{4,3,2,1,0:T(8,128)(2,1)}, u32[]{:S(2)}) copy-start(bf16[2,1,8,512,128]{4,3,2,1,0:T(8,128)(2,1)} %param.8) | copy-start | bytes 6291460
  108.2 8.5 %collective-permute-start.21 = (bf16[4,128,256]{2,1,0:T(8,128)(2,1)S(1)}, bf16[4,128,256]{2,1,0:T(8,128)(2,1)S(1)}, u32[]{:S(2)}, u32[]{:S(2)}) collective-permute-start(bf16[4,128,256]{2,1,0:T(8,128)(2,1)S(1)} %slice.49), channel_id=1, source_target_pairs={{0,2},{1,3},{2,0},{3,1},{4,6},{5,7},{6,4},{7,5},{8,10},{9,11},{10,... | collective-permute-start | bytes 786440 | tf_op jit(solution)/shard_map/ppermute | solution.py:453
  110.0 15.6 %collective-permute-start.18 = (bf16[512,256]{1,0:T(8,128)(2,1)S(1)}, bf16[512,256]{1,0:T(8,128)(2,1)S(1)}, u32[]{:S(2)}, u32[]{:S(2)}) collective-permute-start(bf16[512,256]{1,0:T(8,128)(2,1)S(1)} %get-tuple-element.23), channel_id=1, source_target_pairs={{0,16},{16,0},{1,17},{17,1},{2,18},{18,2},{3,19},{19,3},{4,20},{20... | collective-permute-start | bytes 786440 | tf_op jit(solution)/shard_map/ppermute | solution.py:409
  111.5 14.0 %collective-permute-start.19 = (bf16[512,256]{1,0:T(8,128)(2,1)S(1)}, bf16[512,256]{1,0:T(8,128)(2,1)S(1)}, u32[]{:S(2)}, u32[]{:S(2)}) collective-permute-start(bf16[512,256]{1,0:T(8,128)(2,1)S(1)} %get-tuple-element.25), channel_id=1, source_target_pairs={{0,16},{16,0},{1,17},{17,1},{2,18},{18,2},{3,19},{19,3},{4,20},{20... | collective-permute-start | bytes 786440 | tf_op jit(solution)/shard_map/ppermute | solution.py:409
  114.9 9.0 %collective-permute-start.25 = (bf16[2,128,256]{2,1,0:T(8,128)(2,1)S(1)}, bf16[2,128,256]{2,1,0:T(8,128)(2,1)S(1)}, u32[]{:S(2)}, u32[]{:S(2)}) collective-permute-start(bf16[2,128,256]{2,1,0:T(8,128)(2,1)S(1)} %slice.55), channel_id=1, source_target_pairs={{0,8},{1,9},{2,10},{3,11},{4,12},{5,13},{6,14},{7,15},{8,0},{9,1},... | collective-permute-start | bytes 393224 | tf_op jit(solution)/shard_map/ppermute | solution.py:453
  116.7 8.6 %collective-permute-start.22 = (bf16[2,128,256]{2,1,0:T(8,128)(2,1)S(1)}, bf16[2,128,256]{2,1,0:T(8,128)(2,1)S(1)}, u32[]{:S(2)}, u32[]{:S(2)}) collective-permute-start(bf16[2,128,256]{2,1,0:T(8,128)(2,1)S(1)} %slice.51), channel_id=1, source_target_pairs={{0,4},{1,5},{2,6},{3,7},{4,0},{5,1},{6,2},{7,3},{8,12},{9,13},{10,... | collective-permute-start | bytes 393224 | tf_op jit(solution)/shard_map/ppermute | solution.py:453
  123.9 4.3 %collective-permute-start.27 = (bf16[1,128,256]{2,1,0:T(8,128)(2,1)S(1)}, bf16[1,128,256]{2,1,0:T(8,128)(2,1)S(1)}, u32[]{:S(2)}, u32[]{:S(2)}) collective-permute-start(bf16[1,128,256]{2,1,0:T(8,128)(2,1)S(1)} %slice.59), channel_id=1, source_target_pairs={{0,2},{1,3},{2,0},{3,1},{4,6},{5,7},{6,4},{7,5},{8,10},{9,11},{10,... | collective-permute-start | bytes 196616 | tf_op jit(solution)/shard_map/ppermute | solution.py:453
  125.4 5.4 %collective-permute-start.26 = (bf16[1,128,256]{2,1,0:T(8,128)(2,1)S(1)}, bf16[1,128,256]{2,1,0:T(8,128)(2,1)S(1)}, u32[]{:S(2)}, u32[]{:S(2)}) collective-permute-start(bf16[1,128,256]{2,1,0:T(8,128)(2,1)S(1)} %slice.57), channel_id=1, source_target_pairs={{0,8},{1,9},{2,10},{3,11},{4,12},{5,13},{6,14},{7,15},{8,0},{9,1},... | collective-permute-start | bytes 196616 | tf_op jit(solution)/shard_map/ppermute | solution.py:453
  131.5 3.9 %copy-start.6 = (bf16[256,256]{1,0:T(8,128)(2,1)S(1)}, bf16[256,256]{1,0:T(8,128)(2,1)}, u32[]{:S(2)}) copy-start(bf16[256,256]{1,0:T(8,128)(2,1)} %pad_maximum_fusion.1.refs_1_) | copy-start | bytes 393220
  131.5 26.9 %all-to-all-start.2 = ((bf16[16,16,2048]{2,1,0:T(8,128)(2,1)}), bf16[16,16,2048]{2,1,0:T(8,128)(2,1)S(1)}, u32[]{:S(2)}, u32[]{:S(2)}) async-start(bf16[16,16,2048]{2,1,0:T(8,128)(2,1)} %after.1), calls=%async_computation.2 | async-start | bytes 2097152 | tf_op jit(solution)/shard_map/all_to_all | solution.py:412
  135.4 5.9 %collective-permute-start.28 = (bf16[256,256]{1,0:T(8,128)(2,1)S(1)}, bf16[256,256]{1,0:T(8,128)(2,1)S(1)}, u32[]{:S(2)}, u32[]{:S(2)}) collective-permute-start(bf16[256,256]{1,0:T(8,128)(2,1)S(1)} %copy-done.6), channel_id=1, source_target_pairs={{0,16},{16,0},{1,17},{17,1},{2,18},{18,2},{3,19},{19,3},{4,20},{20... | collective-permute-start | bytes 393224 | tf_op jit(solution)/shard_map/ppermute | solution.py:409
  159.6 21.3 %all-to-all-start.3 = ((bf16[16,16,1024]{2,1,0:T(8,128)(2,1)}), bf16[16,16,1024]{2,1,0:T(8,128)(2,1)S(1)}, u32[]{:S(2)}, u32[]{:S(2)}) async-start(bf16[16,16,1024]{2,1,0:T(8,128)(2,1)} %item_grad_blocks.1), calls=%async_computation.3 | async-start | bytes 1048576 | tf_op jit(solution)/shard_map/all_to_all | solution.py:412

commit v3 on v2

--- a/solution.py
+++ b/solution.py
@@ -63,28 +63,31 @@
     )(*[in_hbm(array) for array in arrays])
 
 
-def pick_kernel(first, nb, ids, item_table, user_weights, out, user_table, sem, table_sem):
+def pick_kernel(first, nb, ids, item_table, user_weights, out, user_table, message, sem, table_sem):
     peers, _, width = out.shape
     kb = width // FBW // (1 + nb)
     fetch_users = pltpu.make_async_copy(user_weights, user_table, table_sem)
     fetch_users.start()
 
-    def picks(source, ids_at, to):
-        def one(p, carry):
-            for k in range(kb):
-                at = pl.multiple_of(ids[p, 0, ids_at + k] * FBW, FBW)
-                pltpu.make_async_copy(
-                    source.at[:, pl.ds(at, FBW)], out.at[p, :, pl.ds((to + k) * FBW, FBW)], sem
-                ).start()
-            return carry
-
-        lax.fori_loop(0, peers, one, 0)
-
-    picks(item_table, first, 0)
+    def pick_one(p, source, ids_at, to):
+        at = pl.multiple_of(ids[p, 0, ids_at] * FBW, FBW)
+        message[p, :, to * FBW : (to + 1) * FBW] = source[:, pl.ds(at, FBW)]
+
+    def item_blocks(p, carry):
+        for k in range(kb):
+            pick_one(p, item_table, first + k, k)
+        return carry
+
+    def user_blocks(p, carry):
+        for k in range(nb * kb):
+            pick_one(p, user_table, k, kb + k)
+        pltpu.make_async_copy(message.at[p], out.at[p], sem).start()
+        return carry
+
+    lax.fori_loop(0, peers, item_blocks, 0)
     fetch_users.wait()
-    for b in range(nb):
-        picks(user_table, b * kb, (1 + b) * kb)
-    pltpu.make_async_copy(out, out, sem).wait()
+    lax.fori_loop(0, peers, user_blocks, 0)
+    pltpu.make_async_copy(message, out, sem).wait()
 
 
 def pick(ids, item_table, user_weights, first, nb, kb):
@@ -96,10 +99,11 @@
         out_specs=HBM,
         scratch_shapes=[
             pltpu.VMEM(user_weights.shape, BF16),
+            pltpu.VMEM(shape, BF16),
             pltpu.SemaphoreType.DMA,
             pltpu.SemaphoreType.DMA,
         ],
-        compiler_params=params(8),
+        compiler_params=params(10),
         name="pick",
     )(ids, item_table, in_hbm(user_weights))
 
@@ -203,24 +207,24 @@
     )(vals, *grads, *follows)
 
 
-def item_grad_kernel(grads, vals, follows, out):
+def item_grad_kernel(grads, vals, out):
     peers, rp, width = out.shape
     blocks = jnp.dot(grads[...], joined(vals[0]), preferred_element_type=F32)
     out[...] = blocks.astype(out.dtype).reshape(peers, rp, width)
 
 
-def item_grad_blocks(grads, vals, b, peers, follows):
+def item_grad_blocks(grads, vals, b, peers):
     _, kb, _, _ = vals.shape
     shape = (peers, grads.shape[0] // peers, kb * FBW)
     return pl.pallas_call(
         item_grad_kernel,
         out_shape=pltpu.HBM(shape, BF16),
-        in_specs=[VMEM, block_spec(vals, b), ANY],
+        in_specs=[VMEM, block_spec(vals, b)],
         out_specs=pl.BlockSpec(shape, lambda i: (0, 0, 0)),
         grid=(1,),
         compiler_params=params(12),
         name="item_grad_blocks",
-    )(grads, vals, follows)
+    )(grads, vals)
 
 
 def collect_kernel(first, ids, back, out):
@@ -240,9 +244,10 @@
     return pl.pallas_call(
         functools.partial(collect_kernel, first),
         out_shape=jax.ShapeDtypeStruct((back.shape[1], columns), F32),
-        in_specs=[SMEM, VMEM],
+        grid=(1,),
+        in_specs=[SMEM, pl.BlockSpec(back.shape, lambda i: (0, 0, 0))],
         out_specs=VMEM,
-        compiler_params=params(12),
+        compiler_params=params(16),
         name="collect",
     )(ids, back)
 
@@ -274,7 +279,7 @@
     share = items[0].shape[0]
     tile, rank = parts[0].shape
     wide = rated.shape[2]
-    width = 4
+    width = 8
 
     def fetch(k):
         g = lax.bitwise_xor(me[0], k)
@@ -292,30 +297,25 @@
         rows = (own[...] + other[...].astype(F32)).astype(BF16)
         users[b * tile : (b + 1) * tile, :] = rows
         users_t[:, b * tile : (b + 1) * tile] = rows.T
+    residuals[...] = jnp.zeros_like(residuals)
     for k in range(peers):
         g = lax.bitwise_xor(me[0], k)
         columns = pl.ds(k * share, share)
         for copy in fetch(k):
             copy.wait()
+        def tiles(rows):
+            predicted = lax.dot_general(
+                users[rows, :], table[columns, :], (((1,), (1,)), ((), ())), preferred_element_type=F32
+            )
+            rating = rating_columns(rated[k, rows, :], g, share).astype(F32)
+            residuals[rows, columns] = (predicted * rank_scale - rating).astype(BF16)
+
+        seen = [observed[b, g] != 0 for b in range(nb)]
+        all_seen = functools.reduce(jnp.logical_and, seen)
+        pl.when(all_seen)(functools.partial(tiles, slice(0, nb * tile)))
         for b in range(nb):
-            rows = slice(b * tile, (b + 1) * tile)
-            seen = observed[b, g]
-
-            @pl.when(seen != 0)
-            def _():
-                predicted = lax.dot_general(
-                    users[rows, :],
-                    table[columns, :],
-                    (((1,), (1,)), ((), ())),
-                    preferred_element_type=F32,
-                )
-                rating = rating_columns(rated[k, rows, :], g, share).astype(F32)
-                residual = (predicted * rank_scale - rating) * seen.astype(F32)
-                residuals[rows, columns] = residual.astype(BF16)
-
-            @pl.when(seen == 0)
-            def _():
-                residuals[rows, columns] = jnp.zeros((tile, share), BF16)
+            alone = jnp.logical_and(seen[b], jnp.logical_not(all_seen))
+            pl.when(alone)(functools.partial(tiles, slice(b * tile, (b + 1) * tile)))
 
         if k % width == width - 1:
             start = k - width + 1
@@ -382,12 +382,12 @@
     n = len(arrays)
     return pl.pallas_call(
         after_kernel,
-        out_shape=[jax.ShapeDtypeStruct(array.shape, array.dtype) for array in arrays],
-        in_specs=[ANY] * (n + len(follows)),
-        out_specs=[ANY] * n,
+        out_shape=[pltpu.HBM(array.shape, array.dtype) for array in arrays],
+        in_specs=[HBM] * n + [ANY] * len(follows),
+        out_specs=[HBM] * n,
         input_output_aliases={i: i for i in range(n)},
         name="after",
-    )(*arrays, *follows)
+    )(*map(in_hbm, arrays), *follows)
 
 
 def across(n, bit):
@@ -460,7 +460,7 @@
         if step == len(bits) - 2:
             user_ask = user_grad_blocks(grads, x_vals, n_rows, sums)
     item_grad = jnp.concatenate([part[0] for part in sums])
-    user_back = every(*after([user_ask], [item_grad]))
+    user_back = in_hbm(every(*after([user_ask], sums)))
     if n_feat == 2:
         other = swap(item_grad)
         first = feat_id == 0
@@ -469,7 +469,7 @@
         )
     else:
         item_grad = lax.all_gather(item_grad, "feat", axis=1, tiled=True)
-    item_back = every(item_grad_blocks(item_grad, y_vals, 0, n_rows, user_back))
+    item_back = every(*after([item_grad_blocks(item_grad, y_vals, 0, n_rows)], [user_back]))
 
     return (
         collect(ids, user_back, 0, user_weights.shape[1]),

time: 185 us -> 183 us (0.989)
  waiting for transfers between devices: 96.4 us -> 90.9 us
  starting transfers between devices: 51.5 us -> 55.5 us
    ppermute x8, waiting for transfers between devices: 13.1 us -> 9.25 us  [give(): return lax.ppermute(array, 'rows', across(n_rows, bit))]
    ppermute x8, starting transfers between devices: 9.93 us -> 12.8 us  [give(): return lax.ppermute(array, 'rows', across(n_rows, bit))]
  transfers between devices with their start and end apart: 33 -> 33, of which waited for: 18 -> 18; matrix products, arithmetic and copies ran while one was open for 0% -> 1% of each run, Pallas kernels for 5% -> 6%
where the time goes in v3:
time: 183 us
  waiting for transfers between devices  90.9 us (50%)
  starting transfers between devices  55.5 us (30%)
  Pallas kernels  31.7 us (17%)
  local copies, waits for them, and re-layouts  2.12 us (1%)
  other arithmetic  1.89 us (1%)
    all_to_all x4, waiting for transfers between devices, every(): lax.all_to_all(array, 'rows', split_axis=0, concat_axis=0, tiled=True)  61.5 us
    all_to_all x4, starting transfers between devices, every(): lax.all_to_all(array, 'rows', split_axis=0, concat_axis=0, tiled=True)  23.2 us
    ppermute x15, waiting for transfers between devices, on_device(): items[k + bit] = lax.ppermute(items[k], 'rows', across(n_rows, bit))  14.1 us
    ppermute x8, starting transfers between devices, give(): return lax.ppermute(array, 'rows', across(n_rows, bit))  12.8 us
    pallas_call x1, Pallas kernels, rate(): pl.pallas_call(functools.partial(rating_kernel, orders, rank_scale, grad_...  12.3 us
    ppermute x15, starting transfers between devices, on_device(): items[k + bit] = lax.ppermute(items[k], 'rows', across(n_rows, bit))  12.1 us
    ppermute x8, waiting for transfers between devices, give(): return lax.ppermute(array, 'rows', across(n_rows, bit))  9.25 us
    pallas_call x2, Pallas kernels, collect(): pl.pallas_call(functools.partial(collect_kernel, first), out_shape=jax.Sh...  8.5 us
  transfers between devices with their start and end apart: 33, of which 18 were waited for; matrix products, arithmetic and copies ran while one was open for 1% of the time, Pallas kernels for 6%

profile of v3, /device:TPU:0, one launch (start us, length us, event | category | flops | bytes accessed | tf_op | source)
XLA Modules:
  0.0 183.0 jit_solution(10404260360196964458)
XLA Ops:
  0.6 1.4 ask.1
  2.0 7.4 %all-to-all-start = ((s32[16,1,128]{2,1,0:T(1,128)}), s32[16,1,128]{2,1,0:T(1,128)S(1)}, u32[]{:S(2)}, u32[]{:S(2)}) async-start(s32[16,1,128]{2,1,0:T(1,128)} %ask.1), calls=%async_computation | async-start | bytes 16384 | tf_op jit(solution)/shard_map/all_to_all | solution.py:412
  9.3 1.4 preload.1.item_table
  10.8 4.9 %all-to-all-done.ids = s32[16,1,128]{2,1,0:T(1,128)S(1)} async-done(((s32[16,1,128]{2,1,0:T(1,128)}), s32[16,1,128]{2,1,0:T(1,128)S(1)}, u32[]{:S(2)}, u32[]{:S(2)}) %all-to-all-start) | async-done | bytes 8224 | tf_op jit(solution)/shard_map/all_to_all | solution.py:412
  15.7 3.7 %pick.1 = bf16[16,16,3072]{2,1,0:T(8,128)(2,1)} custom-call(s32[16,1,128]{2,1,0:T(1,128)S(1)} %all-to-all-done.ids, bf16[16,50176]{1,0:T(8,128)(2,1)S(1)} %preload.1.item_table, bf16[16,100352]{1,0:T(8,128)(2,1)} %user_weights.1), custom_call_target="tpu_custom_call" | custom-call | tf_op jit(solution)/shard_map/pick/pallas_call | solution.py:95
  19.4 0.0 copy-start.2
  19.4 3.9 %all-to-all-start.1 = ((bf16[16,16,3072]{2,1,0:T(8,128)(2,1)}), bf16[16,16,3072]{2,1,0:T(8,128)(2,1)S(1)}, u32[]{:S(2)}, u32[]{:S(2)}) async-start(bf16[16,16,3072]{2,1,0:T(8,128)(2,1)} %pick.1), calls=%async_computation.1 | async-start | bytes 3145728 | tf_op jit(solution)/shard_map/all_to_all | solution.py:412
  23.3 31.9 %all-to-all-done.1.cols = bf16[16,16,3072]{2,1,0:T(8,128)(2,1)S(1)} async-done(((bf16[16,16,3072]{2,1,0:T(8,128)(2,1)}), bf16[16,16,3072]{2,1,0:T(8,128)(2,1)S(1)}, u32[]{:S(2)}, u32[]{:S(2)}) %all-to-all-start.1) | async-done | bytes 1572896 | tf_op jit(solution)/shard_map/all_to_all | solution.py:412
  55.2 0.5 project_halves.1
  55.7 1.6 collective-permute-start.2
  57.3 0.5 project.2
  57.8 0.0 copy-start.5
  57.8 1.1 collective-permute-start
  58.9 0.5 project.3
  59.3 1.1 collective-permute-start.1
  60.4 1.7 collective-permute-done.2
  62.2 7.1 %collective-permute-start.10 = (bf16[256,256]{1,0:T(8,128)(2,1)S(1)}, bf16[256,256]{1,0:T(8,128)(2,1)S(1)}, u32[]{:S(2)}, u32[]{:S(2)}) collective-permute-start(bf16[256,256]{1,0:T(8,128)(2,1)S(1)} %add_convert_fusion.6.refs_4_), channel_id=1, source_target_pairs={{0,8},{1,9},{2,10},{3,11},{4,12},{5,13},{6,14},{7,15},{8,0},{9,1},... | collective-permute-start | bytes 393224 | tf_op jit(solution)/shard_map/ppermute | solution.py:437
  69.2 1.8 collective-permute-start.6
  71.0 3.0 %collective-permute-done.10.refs_12_ = bf16[256,256]{1,0:T(8,128)(2,1)S(1)} collective-permute-done((bf16[256,256]{1,0:T(8,128)(2,1)S(1)}, bf16[256,256]{1,0:T(8,128)(2,1)S(1)}, u32[]{:S(2)}, u32[]{:S(2)}) %collective-permute-start.10) | collective-permute-done | bytes 131104 | tf_op jit(solution)/shard_map/ppermute | solution.py:437
  74.0 0.3 collective-permute-start.14
  74.3 1.1 collective-permute-done.6.refs_8_
  75.4 1.3 collective-permute-start.8
  76.8 0.7 collective-permute-start.12
  77.4 1.5 collective-permute-done.14.refs_16_
  78.9 0.4 collective-permute-start.16
  79.3 0.5 collective-permute-start.15
  79.8 1.9 %collective-permute-done.8.refs_10_ = bf16[256,256]{1,0:T(8,128)(2,1)S(1)} collective-permute-done((bf16[256,256]{1,0:T(8,128)(2,1)S(1)}, bf16[256,256]{1,0:T(8,128)(2,1)S(1)}, u32[]{:S(2)}, u32[]{:S(2)}) %collective-permute-start.8) | collective-permute-done | bytes 131104 | tf_op jit(solution)/shard_map/ppermute | solution.py:437
  81.7 2.8 %collective-permute-done.12.refs_14_ = bf16[256,256]{1,0:T(8,128)(2,1)S(1)} collective-permute-done((bf16[256,256]{1,0:T(8,128)(2,1)S(1)}, bf16[256,256]{1,0:T(8,128)(2,1)S(1)}, u32[]{:S(2)}, u32[]{:S(2)}) %collective-permute-start.12) | collective-permute-done | bytes 131104 | tf_op jit(solution)/shard_map/ppermute | solution.py:437
  84.5 2.4 %collective-permute-done.16.refs_18_ = bf16[256,256]{1,0:T(8,128)(2,1)S(1)} collective-permute-done((bf16[256,256]{1,0:T(8,128)(2,1)S(1)}, bf16[256,256]{1,0:T(8,128)(2,1)S(1)}, u32[]{:S(2)}, u32[]{:S(2)}) %collective-permute-start.16) | collective-permute-done | bytes 131104 | tf_op jit(solution)/shard_map/ppermute | solution.py:437
  87.0 1.4 collective-permute-done.17.refs_19_
  88.4 1.0 copy-done.4
  89.5 12.3 %rate.1 = (f32[512,256]{1,0:T(8,128)S(1)}, bf16[512,256]{1,0:T(8,128)(2,1)S(1)}, f32[512,256]{1,0:T(8,128)S(1)}, bf16[512,256]{1,0:T(8,128)(2,1)S(1)}, bf16[8,12...) custom-call(s32[1]{0:T(128)} %bitcast.1.me, ...), custom_call_target="tpu_custom_call" | custom-call | tf_op jit(solution)/shard_map/rate/pallas_call | solution.py:359
  101.8 0.1 collective-permute-start.20
  101.8 0.5 collective-permute-start.23
  102.3 1.4 collective-permute-done.20
  103.7 0.1 add_convert_fusion.1
  103.9 1.1 collective-permute-start.21
  105.0 0.1 add_convert_fusion
  105.2 2.6 %collective-permute-start.24 = (bf16[4,128,256]{2,1,0:T(8,128)(2,1)S(1)}, bf16[4,128,256]{2,1,0:T(8,128)(2,1)S(1)}, u32[]{:S(2)}, u32[]{:S(2)}) collective-permute-start(bf16[4,128,256]{2,1,0:T(8,128)(2,1)S(1)} %slice.53), channel_id=1, source_target_pairs={{0,4},{1,5},{2,6},{3,7},{4,0},{5,1},{6,2},{7,3},{8,12},{9,13},{10,... | collective-permute-start | bytes 786440 | tf_op jit(solution)/shard_map/ppermute | solution.py:453
  107.7 1.5 collective-permute-start.18
  109.2 0.5 collective-permute-start.19
  109.7 2.6 %collective-permute-done.21 = bf16[4,128,256]{2,1,0:T(8,128)(2,1)S(1)} collective-permute-done((bf16[4,128,256]{2,1,0:T(8,128)(2,1)S(1)}, bf16[4,128,256]{2,1,0:T(8,128)(2,1)S(1)}, u32[]{:S(2)}, u32[]{:S(2)}) %collective-permute-start.21) | collective-permute-done | bytes 262176 | tf_op jit(solution)/shard_map/ppermute | solution.py:453
  112.3 0.1 add_convert_fusion.3
  112.4 2.4 %collective-permute-start.22 = (bf16[2,128,256]{2,1,0:T(8,128)(2,1)S(1)}, bf16[2,128,256]{2,1,0:T(8,128)(2,1)S(1)}, u32[]{:S(2)}, u32[]{:S(2)}) collective-permute-start(bf16[2,128,256]{2,1,0:T(8,128)(2,1)S(1)} %slice.51), channel_id=1, source_target_pairs={{0,4},{1,5},{2,6},{3,7},{4,0},{5,1},{6,2},{7,3},{8,12},{9,13},{10,... | collective-permute-start | bytes 393224 | tf_op jit(solution)/shard_map/ppermute | solution.py:453
  114.8 0.1 add_convert_fusion.2
  114.9 2.3 %collective-permute-start.25 = (bf16[2,128,256]{2,1,0:T(8,128)(2,1)S(1)}, bf16[2,128,256]{2,1,0:T(8,128)(2,1)S(1)}, u32[]{:S(2)}, u32[]{:S(2)}) collective-permute-start(bf16[2,128,256]{2,1,0:T(8,128)(2,1)S(1)} %slice.55), channel_id=1, source_target_pairs={{0,8},{1,9},{2,10},{3,11},{4,12},{5,13},{6,14},{7,15},{8,0},{9,1},... | collective-permute-start | bytes 393224 | tf_op jit(solution)/shard_map/ppermute | solution.py:453
  117.2 1.7 collective-permute-done.22
  119.0 2.3 %collective-permute-start.26 = (bf16[1,128,256]{2,1,0:T(8,128)(2,1)S(1)}, bf16[1,128,256]{2,1,0:T(8,128)(2,1)S(1)}, u32[]{:S(2)}, u32[]{:S(2)}) collective-permute-start(bf16[1,128,256]{2,1,0:T(8,128)(2,1)S(1)} %slice.57), channel_id=1, source_target_pairs={{0,8},{1,9},{2,10},{3,11},{4,12},{5,13},{6,14},{7,15},{8,0},{9,1},... | collective-permute-start | bytes 196616 | tf_op jit(solution)/shard_map/ppermute | solution.py:453
  121.2 3.3 %collective-permute-done.25 = bf16[2,128,256]{2,1,0:T(8,128)(2,1)S(1)} collective-permute-done((bf16[2,128,256]{2,1,0:T(8,128)(2,1)S(1)}, bf16[2,128,256]{2,1,0:T(8,128)(2,1)S(1)}, u32[]{:S(2)}, u32[]{:S(2)}) %collective-permute-start.25) | collective-permute-done | bytes 131104 | tf_op jit(solution)/shard_map/ppermute | solution.py:453
  124.6 1.7 collective-permute-start.27
  126.3 1.7 user_grad_blocks.1.refs_0_
  128.0 0.6 add_convert_fusion.8.refs_1_
  128.6 0.3 collective-permute-done.27
  128.9 0.7 add_convert_fusion.7.refs_2_
  129.5 5.1 %all-to-all-start.2 = ((bf16[16,16,2048]{2,1,0:T(8,128)(2,1)}), bf16[16,16,2048]{2,1,0:T(8,128)(2,1)S(1)}, u32[]{:S(2)}, u32[]{:S(2)}) async-start(bf16[16,16,2048]{2,1,0:T(8,128)(2,1)} %after.2), calls=%async_computation.2 | async-start | bytes 2097152 | tf_op jit(solution)/shard_map/all_to_all | solution.py:412
  134.7 1.6 collective-permute-start.28
  136.3 4.3 %collective-permute-done.28 = bf16[256,256]{1,0:T(8,128)(2,1)S(1)} collective-permute-done((bf16[256,256]{1,0:T(8,128)(2,1)S(1)}, bf16[256,256]{1,0:T(8,128)(2,1)S(1)}, u32[]{:S(2)}, u32[]{:S(2)}) %collective-permute-start.28) | collective-permute-done | bytes 131104 | tf_op jit(solution)/shard_map/ppermute | solution.py:409
  140.7 1.2 item_grad_blocks.1.refs_0_
  141.9 15.7 %all-to-all-done.2.back.refs_1_ = bf16[16,16,2048]{2,1,0:T(8,128)(2,1)S(1)} async-done(((bf16[16,16,2048]{2,1,0:T(8,128)(2,1)}), bf16[16,16,2048]{2,1,0:T(8,128)(2,1)S(1)}, u32[]{:S(2)}, u32[]{:S(2)}) %all-to-all-start.2) | async-done | bytes 1048608 | tf_op jit(solution)/shard_map/all_to_all | solution.py:412
  157.6 1.0 copy-done.6
  158.6 6.9 %all-to-all-start.3 = ((bf16[16,16,1024]{2,1,0:T(8,128)(2,1)}), bf16[16,16,1024]{2,1,0:T(8,128)(2,1)S(1)}, u32[]{:S(2)}, u32[]{:S(2)}) async-start(bf16[16,16,1024]{2,1,0:T(8,128)(2,1)} %after.3), calls=%async_computation.3 | async-start | bytes 1048576 | tf_op jit(solution)/shard_map/all_to_all | solution.py:412
  165.5 5.4 %collect.2 = f32[16,100352]{1,0:T(8,128)} custom-call(s32[16,1,128]{2,1,0:T(1,128)S(1)} %all-to-all-done.ids, bf16[16,16,2048]{2,1,0:T(8,128)(2,1)} %copy-done.6), custom_call_target="tpu_custom_call" | custom-call | tf_op jit(solution)/shard_map/collect/pallas_call | solution.py:244
  170.9 9.1 %all-to-all-done.3.back = bf16[16,16,1024]{2,1,0:T(8,128)(2,1)S(1)} async-done(((bf16[16,16,1024]{2,1,0:T(8,128)(2,1)}), bf16[16,16,1024]{2,1,0:T(8,128)(2,1)S(1)}, u32[]{:S(2)}, u32[]{:S(2)}) %all-to-all-start.3) | async-done | bytes 524320 | tf_op jit(solution)/shard_map/all_to_all | solution.py:412
  179.9 3.1 %collect.3 = f32[16,50176]{1,0:T(8,128)} custom-call(s32[16,1,128]{2,1,0:T(1,128)S(1)} %all-to-all-done.ids, bf16[16,16,1024]{2,1,0:T(8,128)(2,1)S(1)} %all-to-all-done.3.back), custom_call_target="tpu_custom_call" | custom-call | tf_op jit(solution)/shard_map/collect/pallas_call | solution.py:244
  (51 shorter events, 0.3 us)
Async XLA Ops:
  2.0 13.7 %all-to-all-start = ((s32[16,1,128]{2,1,0:T(1,128)}), s32[16,1,128]{2,1,0:T(1,128)S(1)}, u32[]{:S(2)}, u32[]{:S(2)}) async-start(s32[16,1,128]{2,1,0:T(1,128)} %ask.1), calls=%async_computation | async-start | bytes 16384 | tf_op jit(solution)/shard_map/all_to_all | solution.py:412
  19.4 35.8 %copy-start.2 = (bf16[1,1,8,512,128]{4,3,2,1,0:T(8,128)(2,1)S(1)}, bf16[1,1,8,512,128]{4,3,2,1,0:T(8,128)(2,1)}, u32[]{:S(2)}) copy-start(bf16[1,1,8,512,128]{4,3,2,1,0:T(8,128)(2,1)} %param.10) | copy-start | bytes 3145732
  19.4 35.8 %all-to-all-start.1 = ((bf16[16,16,3072]{2,1,0:T(8,128)(2,1)}), bf16[16,16,3072]{2,1,0:T(8,128)(2,1)S(1)}, u32[]{:S(2)}, u32[]{:S(2)}) async-start(bf16[16,16,3072]{2,1,0:T(8,128)(2,1)} %pick.1), calls=%async_computation.1 | async-start | bytes 3145728 | tf_op jit(solution)/shard_map/all_to_all | solution.py:412
  55.2 2.1 %copy-start = (bf16[2,1,8,512,128]{4,3,2,1,0:T(8,128)(2,1)S(1)}, bf16[2,1,8,512,128]{4,3,2,1,0:T(8,128)(2,1)}, u32[]{:S(2)}) copy-start(bf16[2,1,8,512,128]{4,3,2,1,0:T(8,128)(2,1)} %param.8) | copy-start | bytes 6291460
  55.7 6.4 %collective-permute-start.2 = (bf16[256,256]{1,0:T(8,128)(2,1)S(1)}, bf16[256,256]{1,0:T(8,128)(2,1)S(1)}, u32[]{:S(2)}, u32[]{:S(2)}) collective-permute-start(bf16[256,256]{1,0:T(8,128)(2,1)S(1)} %get-tuple-element.16.refs_0_), channel_id=1, source_target_pairs={{0,16},{16,0},{1,17},{17,1},{2,18},{18,2},{3,19},{19,3},{4,20},{20... | collective-permute-start | bytes 393224 | tf_op jit(solution)/shard_map/ppermute | solution.py:409
  57.8 30.7 %copy-start.5 = (s32[2,16]{1,0:T(2,128)S(1)}, s32[2,16]{1,0:T(2,128)}, u32[]{:S(2)}) copy-start(s32[2,16]{1,0:T(2,128)} %observed.1) | copy-start | bytes 388
  57.8 13.2 %collective-permute-start = (bf16[512,256]{1,0:T(8,128)(2,1)S(1)}, bf16[512,256]{1,0:T(8,128)(2,1)S(1)}, u32[]{:S(2)}, u32[]{:S(2)}) collective-permute-start(bf16[512,256]{1,0:T(8,128)(2,1)S(1)} %get-tuple-element.18), channel_id=1, source_target_pairs={{0,16},{16,0},{1,17},{17,1},{2,18},{18,2},{3,19},{19,3},{4,20},{20... | collective-permute-start | bytes 786440 | tf_op jit(solution)/shard_map/ppermute | solution.py:409
  59.3 17.4 %copy-start.3 = (f32[512,256]{1,0:T(8,128)}, f32[512,256]{1,0:T(8,128)S(1)}, u32[]{:S(2)}) copy-start(f32[512,256]{1,0:T(8,128)S(1)} %get-tuple-element.19.refs_2_) | copy-start | bytes 1572868
  59.3 16.1 %collective-permute-start.1 = (bf16[512,256]{1,0:T(8,128)(2,1)S(1)}, bf16[512,256]{1,0:T(8,128)(2,1)S(1)}, u32[]{:S(2)}, u32[]{:S(2)}) collective-permute-start(bf16[512,256]{1,0:T(8,128)(2,1)S(1)} %get-tuple-element.20), channel_id=1, source_target_pairs={{0,16},{16,0},{1,17},{17,1},{2,18},{18,2},{3,19},{19,3},{4,20},{20... | collective-permute-start | bytes 786440 | tf_op jit(solution)/shard_map/ppermute | solution.py:409
  62.2 11.8 %collective-permute-start.10 = (bf16[256,256]{1,0:T(8,128)(2,1)S(1)}, bf16[256,256]{1,0:T(8,128)(2,1)S(1)}, u32[]{:S(2)}, u32[]{:S(2)}) collective-permute-start(bf16[256,256]{1,0:T(8,128)(2,1)S(1)} %add_convert_fusion.6.refs_4_), channel_id=1, source_target_pairs={{0,8},{1,9},{2,10},{3,11},{4,12},{5,13},{6,14},{7,15},{8,0},{9,1},... | collective-permute-start | bytes 393224 | tf_op jit(solution)/shard_map/ppermute | solution.py:437
  69.2 5.1 %collective-permute-start.4 = (bf16[256,256]{1,0:T(8,128)(2,1)S(1)}, bf16[256,256]{1,0:T(8,128)(2,1)S(1)}, u32[]{:S(2)}, u32[]{:S(2)}) collective-permute-start(bf16[256,256]{1,0:T(8,128)(2,1)S(1)} %add_convert_fusion.6.refs_4_), channel_id=1, source_target_pairs={{0,2},{1,3},{2,0},{3,1},{4,6},{5,7},{6,4},{7,5},{8,10},{9,11},{10,... | collective-permute-start | bytes 393224 | tf_op jit(solution)/shard_map/ppermute | solution.py:437
  69.2 6.2 %collective-permute-start.6 = (bf16[256,256]{1,0:T(8,128)(2,1)S(1)}, bf16[256,256]{1,0:T(8,128)(2,1)S(1)}, u32[]{:S(2)}, u32[]{:S(2)}) collective-permute-start(bf16[256,256]{1,0:T(8,128)(2,1)S(1)} %add_convert_fusion.6.refs_4_), channel_id=1, source_target_pairs={{0,4},{1,5},{2,6},{3,7},{4,0},{5,1},{6,2},{7,3},{8,12},{9,13},{10,... | collective-permute-start | bytes 393224 | tf_op jit(solution)/shard_map/ppermute | solution.py:437
  71.0 5.8 %collective-permute-start.3 = (bf16[256,256]{1,0:T(8,128)(2,1)S(1)}, bf16[256,256]{1,0:T(8,128)(2,1)S(1)}, u32[]{:S(2)}, u32[]{:S(2)}) collective-permute-start(bf16[256,256]{1,0:T(8,128)(2,1)S(1)} %add_convert_fusion.6.refs_4_), channel_id=1, source_target_pairs={{0,1},{1,0},{2,3},{3,2},{4,5},{5,4},{6,7},{7,6},{8,9},{9,8},{10,11... | collective-permute-start | bytes 393224 | tf_op jit(solution)/shard_map/ppermute | solution.py:437
  74.0 5.0 %collective-permute-start.14 = (bf16[256,256]{1,0:T(8,128)(2,1)S(1)}, bf16[256,256]{1,0:T(8,128)(2,1)S(1)}, u32[]{:S(2)}, u32[]{:S(2)}) collective-permute-start(bf16[256,256]{1,0:T(8,128)(2,1)S(1)} %collective-permute-done.10.refs_12_), channel_id=1, source_target_pairs={{0,4},{1,5},{2,6},{3,7},{4,0},{5,1},{6,2},{7,3},{8,12},{9,13},{10,... | collective-permute-start | bytes 393224 | tf_op jit(solution)/shard_map/ppermute | solution.py:437
  74.3 5.0 %collective-permute-start.5 = (bf16[256,256]{1,0:T(8,128)(2,1)S(1)}, bf16[256,256]{1,0:T(8,128)(2,1)S(1)}, u32[]{:S(2)}, u32[]{:S(2)}) collective-permute-start(bf16[256,256]{1,0:T(8,128)(2,1)S(1)} %collective-permute-done.4.refs_6_), channel_id=1, source_target_pairs={{0,1},{1,0},{2,3},{3,2},{4,5},{5,4},{6,7},{7,6},{8,9},{9,8},{10,11... | collective-permute-start | bytes 393224 | tf_op jit(solution)/shard_map/ppermute | solution.py:437
  75.4 3.9 %collective-permute-start.7 = (bf16[256,256]{1,0:T(8,128)(2,1)S(1)}, bf16[256,256]{1,0:T(8,128)(2,1)S(1)}, u32[]{:S(2)}, u32[]{:S(2)}) collective-permute-start(bf16[256,256]{1,0:T(8,128)(2,1)S(1)} %collective-permute-done.6.refs_8_), channel_id=1, source_target_pairs={{0,1},{1,0},{2,3},{3,2},{4,5},{5,4},{6,7},{7,6},{8,9},{9,8},{10,11... | collective-permute-start | bytes 393224 | tf_op jit(solution)/shard_map/ppermute | solution.py:437
  75.4 6.3 %collective-permute-start.8 = (bf16[256,256]{1,0:T(8,128)(2,1)S(1)}, bf16[256,256]{1,0:T(8,128)(2,1)S(1)}, u32[]{:S(2)}, u32[]{:S(2)}) collective-permute-start(bf16[256,256]{1,0:T(8,128)(2,1)S(1)} %collective-permute-done.6.refs_8_), channel_id=1, source_target_pairs={{0,2},{1,3},{2,0},{3,1},{4,6},{5,7},{6,4},{7,5},{8,10},{9,11},{10,... | collective-permute-start | bytes 393224 | tf_op jit(solution)/shard_map/ppermute | solution.py:437
  76.8 7.8 %collective-permute-start.12 = (bf16[256,256]{1,0:T(8,128)(2,1)S(1)}, bf16[256,256]{1,0:T(8,128)(2,1)S(1)}, u32[]{:S(2)}, u32[]{:S(2)}) collective-permute-start(bf16[256,256]{1,0:T(8,128)(2,1)S(1)} %collective-permute-done.10.refs_12_), channel_id=1, source_target_pairs={{0,2},{1,3},{2,0},{3,1},{4,6},{5,7},{6,4},{7,5},{8,10},{9,11},{10,... | collective-permute-start | bytes 393224 | tf_op jit(solution)/shard_map/ppermute | solution.py:437
  78.9 8.0 %collective-permute-start.16 = (bf16[256,256]{1,0:T(8,128)(2,1)S(1)}, bf16[256,256]{1,0:T(8,128)(2,1)S(1)}, u32[]{:S(2)}, u32[]{:S(2)}) collective-permute-start(bf16[256,256]{1,0:T(8,128)(2,1)S(1)} %collective-permute-done.14.refs_16_), channel_id=1, source_target_pairs={{0,2},{1,3},{2,0},{3,1},{4,6},{5,7},{6,4},{7,5},{8,10},{9,11},{10,... | collective-permute-start | bytes 393224 | tf_op jit(solution)/shard_map/ppermute | solution.py:437
  79.3 7.6 %collective-permute-start.11 = (bf16[256,256]{1,0:T(8,128)(2,1)S(1)}, bf16[256,256]{1,0:T(8,128)(2,1)}, u32[]{:S(2)}, u32[]{:S(2)}) collective-permute-start(bf16[256,256]{1,0:T(8,128)(2,1)S(1)} %collective-permute-done.10.refs_12_), channel_id=1, source_target_pairs={{0,1},{1,0},{2,3},{3,2},{4,5},{5,4},{6,7},{7,6},{8,9},{9,8},{10,11... | collective-permute-start | bytes 393224 | tf_op jit(solution)/shard_map/ppermute | solution.py:437
  79.3 7.6 %collective-permute-start.15 = (bf16[256,256]{1,0:T(8,128)(2,1)S(1)}, bf16[256,256]{1,0:T(8,128)(2,1)}, u32[]{:S(2)}, u32[]{:S(2)}) collective-permute-start(bf16[256,256]{1,0:T(8,128)(2,1)S(1)} %collective-permute-done.14.refs_16_), channel_id=1, source_target_pairs={{0,1},{1,0},{2,3},{3,2},{4,5},{5,4},{6,7},{7,6},{8,9},{9,8},{10,11... | collective-permute-start | bytes 393224 | tf_op jit(solution)/shard_map/ppermute | solution.py:437
  81.7 5.2 %collective-permute-start.9 = (bf16[256,256]{1,0:T(8,128)(2,1)S(1)}, bf16[256,256]{1,0:T(8,128)(2,1)}, u32[]{:S(2)}, u32[]{:S(2)}) collective-permute-start(bf16[256,256]{1,0:T(8,128)(2,1)S(1)} %collective-permute-done.8.refs_10_), channel_id=1, source_target_pairs={{0,1},{1,0},{2,3},{3,2},{4,5},{5,4},{6,7},{7,6},{8,9},{9,8},{10,11... | collective-permute-start | bytes 393224 | tf_op jit(solution)/shard_map/ppermute | solution.py:437
  84.5 2.4 %collective-permute-start.13 = (bf16[256,256]{1,0:T(8,128)(2,1)S(1)}, bf16[256,256]{1,0:T(8,128)(2,1)}, u32[]{:S(2)}, u32[]{:S(2)}) collective-permute-start(bf16[256,256]{1,0:T(8,128)(2,1)S(1)} %collective-permute-done.12.refs_14_), channel_id=1, source_target_pairs={{0,1},{1,0},{2,3},{3,2},{4,5},{5,4},{6,7},{7,6},{8,9},{9,8},{10,11... | collective-permute-start | bytes 393224 | tf_op jit(solution)/shard_map/ppermute | solution.py:437
  86.9 1.5 collective-permute-start.17
  88.4 1.0 copy-start.4
  101.8 2.0 %collective-permute-start.20 = (bf16[8,128,256]{2,1,0:T(8,128)(2,1)S(1)}, bf16[8,128,256]{2,1,0:T(8,128)(2,1)S(1)}, u32[]{:S(2)}, u32[]{:S(2)}) collective-permute-start(bf16[8,128,256]{2,1,0:T(8,128)(2,1)S(1)} %get-tuple-element.27), channel_id=1, source_target_pairs={{0,1},{1,0},{2,3},{3,2},{4,5},{5,4},{6,7},{7,6},{8,9},{9,8},{10,11... | collective-permute-start | bytes 1572872 | tf_op jit(solution)/shard_map/ppermute | solution.py:453
  101.8 3.1 %collective-permute-start.23 = (bf16[8,128,256]{2,1,0:T(8,128)(2,1)S(1)}, bf16[8,128,256]{2,1,0:T(8,128)(2,1)S(1)}, u32[]{:S(2)}, u32[]{:S(2)}) collective-permute-start(bf16[8,128,256]{2,1,0:T(8,128)(2,1)S(1)} %get-tuple-element.29), channel_id=1, source_target_pairs={{0,1},{1,0},{2,3},{3,2},{4,5},{5,4},{6,7},{7,6},{8,9},{9,8},{10,11... | collective-permute-start | bytes 1572872 | tf_op jit(solution)/shard_map/ppermute | solution.py:453
  103.9 8.4 %collective-permute-start.21 = (bf16[4,128,256]{2,1,0:T(8,128)(2,1)S(1)}, bf16[4,128,256]{2,1,0:T(8,128)(2,1)S(1)}, u32[]{:S(2)}, u32[]{:S(2)}) collective-permute-start(bf16[4,128,256]{2,1,0:T(8,128)(2,1)S(1)} %slice.49), channel_id=1, source_target_pairs={{0,2},{1,3},{2,0},{3,1},{4,6},{5,7},{6,4},{7,5},{8,10},{9,11},{10,... | collective-permute-start | bytes 786440 | tf_op jit(solution)/shard_map/ppermute | solution.py:453
  105.1 21.1 %copy-start.1 = (bf16[2,1,8,512,128]{4,3,2,1,0:T(8,128)(2,1)S(1)}, bf16[2,1,8,512,128]{4,3,2,1,0:T(8,128)(2,1)}, u32[]{:S(2)}) copy-start(bf16[2,1,8,512,128]{4,3,2,1,0:T(8,128)(2,1)} %param.8) | copy-start | bytes 6291460
  105.2 9.6 %collective-permute-start.24 = (bf16[4,128,256]{2,1,0:T(8,128)(2,1)S(1)}, bf16[4,128,256]{2,1,0:T(8,128)(2,1)S(1)}, u32[]{:S(2)}, u32[]{:S(2)}) collective-permute-start(bf16[4,128,256]{2,1,0:T(8,128)(2,1)S(1)} %slice.53), channel_id=1, source_target_pairs={{0,4},{1,5},{2,6},{3,7},{4,0},{5,1},{6,2},{7,3},{8,12},{9,13},{10,... | collective-permute-start | bytes 786440 | tf_op jit(solution)/shard_map/ppermute | solution.py:453
  107.7 18.5 %collective-permute-start.18 = (bf16[512,256]{1,0:T(8,128)(2,1)S(1)}, bf16[512,256]{1,0:T(8,128)(2,1)S(1)}, u32[]{:S(2)}, u32[]{:S(2)}) collective-permute-start(bf16[512,256]{1,0:T(8,128)(2,1)S(1)} %get-tuple-element.23), channel_id=1, source_target_pairs={{0,16},{16,0},{1,17},{17,1},{2,18},{18,2},{3,19},{19,3},{4,20},{20... | collective-permute-start | bytes 786440 | tf_op jit(solution)/shard_map/ppermute | solution.py:409
  109.2 17.0 %collective-permute-start.19 = (bf16[512,256]{1,0:T(8,128)(2,1)S(1)}, bf16[512,256]{1,0:T(8,128)(2,1)S(1)}, u32[]{:S(2)}, u32[]{:S(2)}) collective-permute-start(bf16[512,256]{1,0:T(8,128)(2,1)S(1)} %get-tuple-element.25), channel_id=1, source_target_pairs={{0,16},{16,0},{1,17},{17,1},{2,18},{18,2},{3,19},{19,3},{4,20},{20... | collective-permute-start | bytes 786440 | tf_op jit(solution)/shard_map/ppermute | solution.py:409
  112.4 6.5 %collective-permute-start.22 = (bf16[2,128,256]{2,1,0:T(8,128)(2,1)S(1)}, bf16[2,128,256]{2,1,0:T(8,128)(2,1)S(1)}, u32[]{:S(2)}, u32[]{:S(2)}) collective-permute-start(bf16[2,128,256]{2,1,0:T(8,128)(2,1)S(1)} %slice.51), channel_id=1, source_target_pairs={{0,4},{1,5},{2,6},{3,7},{4,0},{5,1},{6,2},{7,3},{8,12},{9,13},{10,... | collective-permute-start | bytes 393224 | tf_op jit(solution)/shard_map/ppermute | solution.py:453
  114.9 9.6 %collective-permute-start.25 = (bf16[2,128,256]{2,1,0:T(8,128)(2,1)S(1)}, bf16[2,128,256]{2,1,0:T(8,128)(2,1)S(1)}, u32[]{:S(2)}, u32[]{:S(2)}) collective-permute-start(bf16[2,128,256]{2,1,0:T(8,128)(2,1)S(1)} %slice.55), channel_id=1, source_target_pairs={{0,8},{1,9},{2,10},{3,11},{4,12},{5,13},{6,14},{7,15},{8,0},{9,1},... | collective-permute-start | bytes 393224 | tf_op jit(solution)/shard_map/ppermute | solution.py:453
  119.0 9.0 %collective-permute-start.26 = (bf16[1,128,256]{2,1,0:T(8,128)(2,1)S(1)}, bf16[1,128,256]{2,1,0:T(8,128)(2,1)S(1)}, u32[]{:S(2)}, u32[]{:S(2)}) collective-permute-start(bf16[1,128,256]{2,1,0:T(8,128)(2,1)S(1)} %slice.57), channel_id=1, source_target_pairs={{0,8},{1,9},{2,10},{3,11},{4,12},{5,13},{6,14},{7,15},{8,0},{9,1},... | collective-permute-start | bytes 196616 | tf_op jit(solution)/shard_map/ppermute | solution.py:453
  124.6 4.3 %collective-permute-start.27 = (bf16[1,128,256]{2,1,0:T(8,128)(2,1)S(1)}, bf16[1,128,256]{2,1,0:T(8,128)(2,1)S(1)}, u32[]{:S(2)}, u32[]{:S(2)}) collective-permute-start(bf16[1,128,256]{2,1,0:T(8,128)(2,1)S(1)} %slice.59), channel_id=1, source_target_pairs={{0,2},{1,3},{2,0},{3,1},{4,6},{5,7},{6,4},{7,5},{8,10},{9,11},{10,... | collective-permute-start | bytes 196616 | tf_op jit(solution)/shard_map/ppermute | solution.py:453
  129.5 5.1 %copy-start.7 = (bf16[1,128,256]{2,1,0:T(8,128)(2,1)S(1)}, bf16[1,128,256]{2,1,0:T(8,128)(2,1)}, u32[]{:S(2)}) copy-start(bf16[1,128,256]{2,1,0:T(8,128)(2,1)} %add_convert_fusion.8.refs_1_) | copy-start | bytes 196612
  129.5 5.1 %copy-start.8 = (bf16[1,128,256]{2,1,0:T(8,128)(2,1)S(1)}, bf16[1,128,256]{2,1,0:T(8,128)(2,1)}, u32[]{:S(2)}) copy-start(bf16[1,128,256]{2,1,0:T(8,128)(2,1)} %add_convert_fusion.7.refs_2_) | copy-start | bytes 196612
  129.5 28.1 %all-to-all-start.2 = ((bf16[16,16,2048]{2,1,0:T(8,128)(2,1)}), bf16[16,16,2048]{2,1,0:T(8,128)(2,1)S(1)}, u32[]{:S(2)}, u32[]{:S(2)}) async-start(bf16[16,16,2048]{2,1,0:T(8,128)(2,1)} %after.2), calls=%async_computation.2 | async-start | bytes 2097152 | tf_op jit(solution)/shard_map/all_to_all | solution.py:412
  134.7 5.9 %collective-permute-start.28 = (bf16[256,256]{1,0:T(8,128)(2,1)S(1)}, bf16[256,256]{1,0:T(8,128)(2,1)S(1)}, u32[]{:S(2)}, u32[]{:S(2)}) collective-permute-start(bf16[256,256]{1,0:T(8,128)(2,1)S(1)} %pad_maximum_fusion.1), channel_id=1, source_target_pairs={{0,16},{16,0},{1,17},{17,1},{2,18},{18,2},{3,19},{19,3},{4,20},{20... | collective-permute-start | bytes 393224 | tf_op jit(solution)/shard_map/ppermute | solution.py:409
  157.6 1.0 copy-start.6
  158.6 21.3 %all-to-all-start.3 = ((bf16[16,16,1024]{2,1,0:T(8,128)(2,1)}), bf16[16,16,1024]{2,1,0:T(8,128)(2,1)S(1)}, u32[]{:S(2)}, u32[]{:S(2)}) async-start(bf16[16,16,1024]{2,1,0:T(8,128)(2,1)} %after.3), calls=%async_computation.3 | async-start | bytes 1048576 | tf_op jit(solution)/shard_map/all_to_all | solution.py:412

commit v4 on v3

--- a/solution.py
+++ b/solution.py
@@ -440,7 +440,7 @@
 
     me = row_id.reshape(1).astype(jnp.int32)
     bits = [1 << i for i in range(1, n_rows.bit_length() - 1)]
-    orders = [bits, bits[1:] + bits[:1]]
+    orders = [bits, bits[1:2] + bits[:1] + bits[2:]]
     *grads, first, first_give, second, second_give = rate(
         orders, me, observed, parts, items, ratings[:, 0], rank_scale, grad_scale
     )

time: 183 us -> 181 us (0.989)
  starting transfers between devices: 55.5 us -> 53.5 us
where the time goes in v4:
time: 181 us; the launch traced here: 180 us
  waiting for transfers between devices  89.7 us (50%)
  starting transfers between devices  53.5 us (30%)
  Pallas kernels  31.8 us (18%)
  local copies, waits for them, and re-layouts  2.12 us (1%)
  other arithmetic  1.89 us (1%)
    all_to_all x4, waiting for transfers between devices, every(): lax.all_to_all(array, 'rows', split_axis=0, concat_axis=0, tiled=True)  61.5 us
    all_to_all x4, starting transfers between devices, every(): lax.all_to_all(array, 'rows', split_axis=0, concat_axis=0, tiled=True)  22.6 us
    ppermute x15, waiting for transfers between devices, on_device(): items[k + bit] = lax.ppermute(items[k], 'rows', across(n_rows, bit))  14.1 us
    pallas_call x1, Pallas kernels, rate(): pl.pallas_call(functools.partial(rating_kernel, orders, rank_scale, grad_...  12.4 us
    ppermute x15, starting transfers between devices, on_device(): items[k + bit] = lax.ppermute(items[k], 'rows', across(n_rows, bit))  12.1 us
    ppermute x8, starting transfers between devices, give(): return lax.ppermute(array, 'rows', across(n_rows, bit))  11.5 us
    pallas_call x2, Pallas kernels, collect(): pl.pallas_call(functools.partial(collect_kernel, first), out_shape=jax.Sh...  8.5 us
    ppermute x8, waiting for transfers between devices, give(): return lax.ppermute(array, 'rows', across(n_rows, bit))  8.02 us
  transfers between devices with their start and end apart: 33, of which 18 were waited for; matrix products, arithmetic and copies ran while one was open for 1% of the time, Pallas kernels for 6%

profile of v4, /device:TPU:0, one launch (start us, length us, event | category | flops | bytes accessed | tf_op | source)
XLA Modules:
  0.0 180.0 jit_solution(16384937086215712303)
XLA Ops:
  0.6 1.4 ask.1
  2.0 7.4 %all-to-all-start = ((s32[16,1,128]{2,1,0:T(1,128)}), s32[16,1,128]{2,1,0:T(1,128)S(1)}, u32[]{:S(2)}, u32[]{:S(2)}) async-start(s32[16,1,128]{2,1,0:T(1,128)} %ask.1), calls=%async_computation | async-start | bytes 16384 | tf_op jit(solution)/shard_map/all_to_all | solution.py:412
  9.3 1.4 preload.1.item_table
  10.8 4.9 %all-to-all-done.ids = s32[16,1,128]{2,1,0:T(1,128)S(1)} async-done(((s32[16,1,128]{2,1,0:T(1,128)}), s32[16,1,128]{2,1,0:T(1,128)S(1)}, u32[]{:S(2)}, u32[]{:S(2)}) %all-to-all-start) | async-done | bytes 8224 | tf_op jit(solution)/shard_map/all_to_all | solution.py:412
  15.7 3.7 %pick.1 = bf16[16,16,3072]{2,1,0:T(8,128)(2,1)} custom-call(s32[16,1,128]{2,1,0:T(1,128)S(1)} %all-to-all-done.ids, bf16[16,50176]{1,0:T(8,128)(2,1)S(1)} %preload.1.item_table, bf16[16,100352]{1,0:T(8,128)(2,1)} %user_weights.1), custom_call_target="tpu_custom_call" | custom-call | tf_op jit(solution)/shard_map/pick/pallas_call | solution.py:95
  19.4 3.9 %all-to-all-start.1 = ((bf16[16,16,3072]{2,1,0:T(8,128)(2,1)}), bf16[16,16,3072]{2,1,0:T(8,128)(2,1)S(1)}, u32[]{:S(2)}, u32[]{:S(2)}) async-start(bf16[16,16,3072]{2,1,0:T(8,128)(2,1)} %pick.1), calls=%async_computation.1 | async-start | bytes 3145728 | tf_op jit(solution)/shard_map/all_to_all | solution.py:412
  23.3 31.9 %all-to-all-done.1.cols = bf16[16,16,3072]{2,1,0:T(8,128)(2,1)S(1)} async-done(((bf16[16,16,3072]{2,1,0:T(8,128)(2,1)}), bf16[16,16,3072]{2,1,0:T(8,128)(2,1)S(1)}, u32[]{:S(2)}, u32[]{:S(2)}) %all-to-all-start.1) | async-done | bytes 1572896 | tf_op jit(solution)/shard_map/all_to_all | solution.py:412
  55.2 0.5 project_halves.1
  55.7 1.6 collective-permute-start.2
  57.3 0.5 project.2
  57.8 0.0 copy-start.5
  57.8 1.1 collective-permute-start
  58.9 0.5 project.3
  59.3 0.0 copy-start.3
  59.3 1.1 collective-permute-start.1
  60.4 1.7 collective-permute-done.2
  62.2 7.1 %collective-permute-start.10 = (bf16[256,256]{1,0:T(8,128)(2,1)S(1)}, bf16[256,256]{1,0:T(8,128)(2,1)S(1)}, u32[]{:S(2)}, u32[]{:S(2)}) collective-permute-start(bf16[256,256]{1,0:T(8,128)(2,1)S(1)} %add_convert_fusion.6.refs_4_), channel_id=1, source_target_pairs={{0,8},{1,9},{2,10},{3,11},{4,12},{5,13},{6,14},{7,15},{8,0},{9,1},... | collective-permute-start | bytes 393224 | tf_op jit(solution)/shard_map/ppermute | solution.py:437
  69.2 1.8 collective-permute-start.6
  71.0 3.0 %collective-permute-done.10.refs_12_ = bf16[256,256]{1,0:T(8,128)(2,1)S(1)} collective-permute-done((bf16[256,256]{1,0:T(8,128)(2,1)S(1)}, bf16[256,256]{1,0:T(8,128)(2,1)S(1)}, u32[]{:S(2)}, u32[]{:S(2)}) %collective-permute-start.10) | collective-permute-done | bytes 131104 | tf_op jit(solution)/shard_map/ppermute | solution.py:437
  74.0 0.3 collective-permute-start.14
  74.3 1.1 collective-permute-done.6.refs_8_
  75.4 1.3 collective-permute-start.8
  76.8 0.7 collective-permute-start.12
  77.4 1.5 collective-permute-done.14.refs_16_
  78.9 0.4 collective-permute-start.16
  79.3 0.5 collective-permute-start.15
  79.8 1.9 %collective-permute-done.8.refs_10_ = bf16[256,256]{1,0:T(8,128)(2,1)S(1)} collective-permute-done((bf16[256,256]{1,0:T(8,128)(2,1)S(1)}, bf16[256,256]{1,0:T(8,128)(2,1)S(1)}, u32[]{:S(2)}, u32[]{:S(2)}) %collective-permute-start.8) | collective-permute-done | bytes 131104 | tf_op jit(solution)/shard_map/ppermute | solution.py:437
  81.7 2.8 %collective-permute-done.12.refs_14_ = bf16[256,256]{1,0:T(8,128)(2,1)S(1)} collective-permute-done((bf16[256,256]{1,0:T(8,128)(2,1)S(1)}, bf16[256,256]{1,0:T(8,128)(2,1)S(1)}, u32[]{:S(2)}, u32[]{:S(2)}) %collective-permute-start.12) | collective-permute-done | bytes 131104 | tf_op jit(solution)/shard_map/ppermute | solution.py:437
  84.5 2.4 %collective-permute-done.16.refs_18_ = bf16[256,256]{1,0:T(8,128)(2,1)S(1)} collective-permute-done((bf16[256,256]{1,0:T(8,128)(2,1)S(1)}, bf16[256,256]{1,0:T(8,128)(2,1)S(1)}, u32[]{:S(2)}, u32[]{:S(2)}) %collective-permute-start.16) | collective-permute-done | bytes 131104 | tf_op jit(solution)/shard_map/ppermute | solution.py:437
  87.0 1.4 collective-permute-done.17.refs_19_
  88.4 1.0 copy-done.4
  89.5 12.4 %rate.1 = (f32[512,256]{1,0:T(8,128)S(1)}, bf16[512,256]{1,0:T(8,128)(2,1)S(1)}, f32[512,256]{1,0:T(8,128)S(1)}, bf16[512,256]{1,0:T(8,128)(2,1)S(1)}, bf16[8,12...) custom-call(s32[1]{0:T(128)} %bitcast.1.me, ...), custom_call_target="tpu_custom_call" | custom-call | tf_op jit(solution)/shard_map/rate/pallas_call | solution.py:359
  101.9 0.1 collective-permute-start.20
  102.0 0.5 collective-permute-start.23
  102.5 1.4 collective-permute-done.20
  103.9 0.1 add_convert_fusion.1
  104.1 1.8 collective-permute-start.21
  105.8 0.1 add_convert_fusion
  106.0 1.9 %collective-permute-start.24 = (bf16[4,128,256]{2,1,0:T(8,128)(2,1)S(1)}, bf16[4,128,256]{2,1,0:T(8,128)(2,1)S(1)}, u32[]{:S(2)}, u32[]{:S(2)}) collective-permute-start(bf16[4,128,256]{2,1,0:T(8,128)(2,1)S(1)} %slice.53), channel_id=1, source_target_pairs={{0,4},{1,5},{2,6},{3,7},{4,0},{5,1},{6,2},{7,3},{8,12},{9,13},{10,... | collective-permute-start | bytes 786440 | tf_op jit(solution)/shard_map/ppermute | solution.py:453
  107.9 1.5 collective-permute-start.18
  109.4 0.5 collective-permute-start.19
  109.9 2.7 %collective-permute-done.21 = bf16[4,128,256]{2,1,0:T(8,128)(2,1)S(1)} collective-permute-done((bf16[4,128,256]{2,1,0:T(8,128)(2,1)S(1)}, bf16[4,128,256]{2,1,0:T(8,128)(2,1)S(1)}, u32[]{:S(2)}, u32[]{:S(2)}) %collective-permute-start.21) | collective-permute-done | bytes 262176 | tf_op jit(solution)/shard_map/ppermute | solution.py:453
  112.6 0.1 add_convert_fusion.3
  112.7 1.6 collective-permute-start.22
  114.4 0.1 add_convert_fusion.2
  114.5 1.8 %collective-permute-start.25 = (bf16[2,128,256]{2,1,0:T(8,128)(2,1)S(1)}, bf16[2,128,256]{2,1,0:T(8,128)(2,1)S(1)}, u32[]{:S(2)}, u32[]{:S(2)}) collective-permute-start(bf16[2,128,256]{2,1,0:T(8,128)(2,1)S(1)} %slice.55), channel_id=1, source_target_pairs={{0,2},{1,3},{2,0},{3,1},{4,6},{5,7},{6,4},{7,5},{8,10},{9,11},{10,... | collective-permute-start | bytes 393224 | tf_op jit(solution)/shard_map/ppermute | solution.py:453
  116.3 1.5 collective-permute-done.22
  117.8 2.1 %collective-permute-start.26 = (bf16[1,128,256]{2,1,0:T(8,128)(2,1)S(1)}, bf16[1,128,256]{2,1,0:T(8,128)(2,1)S(1)}, u32[]{:S(2)}, u32[]{:S(2)}) collective-permute-start(bf16[1,128,256]{2,1,0:T(8,128)(2,1)S(1)} %slice.57), channel_id=1, source_target_pairs={{0,8},{1,9},{2,10},{3,11},{4,12},{5,13},{6,14},{7,15},{8,0},{9,1},... | collective-permute-start | bytes 196616 | tf_op jit(solution)/shard_map/ppermute | solution.py:453
  119.9 1.8 collective-permute-start.27
  121.7 1.7 user_grad_blocks.1.refs_0_
  123.4 1.6 collective-permute-done.26
  125.1 0.6 add_convert_fusion.8.refs_1_
  125.7 0.8 collective-permute-done.27
  126.5 0.7 add_convert_fusion.7.refs_2_
  127.1 4.5 %all-to-all-start.2 = ((bf16[16,16,2048]{2,1,0:T(8,128)(2,1)}), bf16[16,16,2048]{2,1,0:T(8,128)(2,1)S(1)}, u32[]{:S(2)}, u32[]{:S(2)}) async-start(bf16[16,16,2048]{2,1,0:T(8,128)(2,1)} %after.2), calls=%async_computation.2 | async-start | bytes 2097152 | tf_op jit(solution)/shard_map/all_to_all | solution.py:412
  131.7 1.6 collective-permute-start.28
  133.2 4.3 %collective-permute-done.28 = bf16[256,256]{1,0:T(8,128)(2,1)S(1)} collective-permute-done((bf16[256,256]{1,0:T(8,128)(2,1)S(1)}, bf16[256,256]{1,0:T(8,128)(2,1)S(1)}, u32[]{:S(2)}, u32[]{:S(2)}) %collective-permute-start.28) | collective-permute-done | bytes 131104 | tf_op jit(solution)/shard_map/ppermute | solution.py:409
  137.6 1.3 item_grad_blocks.1.refs_0_
  138.9 15.7 %all-to-all-done.2.back.refs_1_ = bf16[16,16,2048]{2,1,0:T(8,128)(2,1)S(1)} async-done(((bf16[16,16,2048]{2,1,0:T(8,128)(2,1)}), bf16[16,16,2048]{2,1,0:T(8,128)(2,1)S(1)}, u32[]{:S(2)}, u32[]{:S(2)}) %all-to-all-start.2) | async-done | bytes 1048608 | tf_op jit(solution)/shard_map/all_to_all | solution.py:412
  154.6 1.0 copy-done.6
  155.5 6.9 %all-to-all-start.3 = ((bf16[16,16,1024]{2,1,0:T(8,128)(2,1)}), bf16[16,16,1024]{2,1,0:T(8,128)(2,1)S(1)}, u32[]{:S(2)}, u32[]{:S(2)}) async-start(bf16[16,16,1024]{2,1,0:T(8,128)(2,1)} %after.3), calls=%async_computation.3 | async-start | bytes 1048576 | tf_op jit(solution)/shard_map/all_to_all | solution.py:412
  162.4 5.4 %collect.2 = f32[16,100352]{1,0:T(8,128)} custom-call(s32[16,1,128]{2,1,0:T(1,128)S(1)} %all-to-all-done.ids, bf16[16,16,2048]{2,1,0:T(8,128)(2,1)} %copy-done.6), custom_call_target="tpu_custom_call" | custom-call | tf_op jit(solution)/shard_map/collect/pallas_call | solution.py:244
  167.8 9.1 %all-to-all-done.3.back = bf16[16,16,1024]{2,1,0:T(8,128)(2,1)S(1)} async-done(((bf16[16,16,1024]{2,1,0:T(8,128)(2,1)}), bf16[16,16,1024]{2,1,0:T(8,128)(2,1)S(1)}, u32[]{:S(2)}, u32[]{:S(2)}) %all-to-all-start.3) | async-done | bytes 524320 | tf_op jit(solution)/shard_map/all_to_all | solution.py:412
  176.9 3.1 %collect.3 = f32[16,50176]{1,0:T(8,128)} custom-call(s32[16,1,128]{2,1,0:T(1,128)S(1)} %all-to-all-done.ids, bf16[16,16,1024]{2,1,0:T(8,128)(2,1)S(1)} %all-to-all-done.3.back), custom_call_target="tpu_custom_call" | custom-call | tf_op jit(solution)/shard_map/collect/pallas_call | solution.py:244
  (51 shorter events, 0.3 us)
Async XLA Ops:
  2.0 13.7 %all-to-all-start = ((s32[16,1,128]{2,1,0:T(1,128)}), s32[16,1,128]{2,1,0:T(1,128)S(1)}, u32[]{:S(2)}, u32[]{:S(2)}) async-start(s32[16,1,128]{2,1,0:T(1,128)} %ask.1), calls=%async_computation | async-start | bytes 16384 | tf_op jit(solution)/shard_map/all_to_all | solution.py:412
  19.4 35.8 %copy-start.2 = (bf16[1,1,8,512,128]{4,3,2,1,0:T(8,128)(2,1)S(1)}, bf16[1,1,8,512,128]{4,3,2,1,0:T(8,128)(2,1)}, u32[]{:S(2)}) copy-start(bf16[1,1,8,512,128]{4,3,2,1,0:T(8,128)(2,1)} %param.10) | copy-start | bytes 3145732
  19.4 35.8 %all-to-all-start.1 = ((bf16[16,16,3072]{2,1,0:T(8,128)(2,1)}), bf16[16,16,3072]{2,1,0:T(8,128)(2,1)S(1)}, u32[]{:S(2)}, u32[]{:S(2)}) async-start(bf16[16,16,3072]{2,1,0:T(8,128)(2,1)} %pick.1), calls=%async_computation.1 | async-start | bytes 3145728 | tf_op jit(solution)/shard_map/all_to_all | solution.py:412
  55.2 2.1 %copy-start = (bf16[2,1,8,512,128]{4,3,2,1,0:T(8,128)(2,1)S(1)}, bf16[2,1,8,512,128]{4,3,2,1,0:T(8,128)(2,1)}, u32[]{:S(2)}) copy-start(bf16[2,1,8,512,128]{4,3,2,1,0:T(8,128)(2,1)} %param.8) | copy-start | bytes 6291460
  55.7 6.4 %collective-permute-start.2 = (bf16[256,256]{1,0:T(8,128)(2,1)S(1)}, bf16[256,256]{1,0:T(8,128)(2,1)S(1)}, u32[]{:S(2)}, u32[]{:S(2)}) collective-permute-start(bf16[256,256]{1,0:T(8,128)(2,1)S(1)} %get-tuple-element.16.refs_0_), channel_id=1, source_target_pairs={{0,16},{16,0},{1,17},{17,1},{2,18},{18,2},{3,19},{19,3},{4,20},{20... | collective-permute-start | bytes 393224 | tf_op jit(solution)/shard_map/ppermute | solution.py:409
  57.8 30.7 %copy-start.5 = (s32[2,16]{1,0:T(2,128)S(1)}, s32[2,16]{1,0:T(2,128)}, u32[]{:S(2)}) copy-start(s32[2,16]{1,0:T(2,128)} %observed.1) | copy-start | bytes 388
  57.8 13.2 %collective-permute-start = (bf16[512,256]{1,0:T(8,128)(2,1)S(1)}, bf16[512,256]{1,0:T(8,128)(2,1)S(1)}, u32[]{:S(2)}, u32[]{:S(2)}) collective-permute-start(bf16[512,256]{1,0:T(8,128)(2,1)S(1)} %get-tuple-element.18), channel_id=1, source_target_pairs={{0,16},{16,0},{1,17},{17,1},{2,18},{18,2},{3,19},{19,3},{4,20},{20... | collective-permute-start | bytes 786440 | tf_op jit(solution)/shard_map/ppermute | solution.py:409
  59.3 17.4 %copy-start.3 = (f32[512,256]{1,0:T(8,128)}, f32[512,256]{1,0:T(8,128)S(1)}, u32[]{:S(2)}) copy-start(f32[512,256]{1,0:T(8,128)S(1)} %get-tuple-element.19.refs_2_) | copy-start | bytes 1572868
  59.3 16.1 %collective-permute-start.1 = (bf16[512,256]{1,0:T(8,128)(2,1)S(1)}, bf16[512,256]{1,0:T(8,128)(2,1)S(1)}, u32[]{:S(2)}, u32[]{:S(2)}) collective-permute-start(bf16[512,256]{1,0:T(8,128)(2,1)S(1)} %get-tuple-element.20), channel_id=1, source_target_pairs={{0,16},{16,0},{1,17},{17,1},{2,18},{18,2},{3,19},{19,3},{4,20},{20... | collective-permute-start | bytes 786440 | tf_op jit(solution)/shard_map/ppermute | solution.py:409
  62.2 11.8 %collective-permute-start.10 = (bf16[256,256]{1,0:T(8,128)(2,1)S(1)}, bf16[256,256]{1,0:T(8,128)(2,1)S(1)}, u32[]{:S(2)}, u32[]{:S(2)}) collective-permute-start(bf16[256,256]{1,0:T(8,128)(2,1)S(1)} %add_convert_fusion.6.refs_4_), channel_id=1, source_target_pairs={{0,8},{1,9},{2,10},{3,11},{4,12},{5,13},{6,14},{7,15},{8,0},{9,1},... | collective-permute-start | bytes 393224 | tf_op jit(solution)/shard_map/ppermute | solution.py:437
  69.2 5.1 %collective-permute-start.4 = (bf16[256,256]{1,0:T(8,128)(2,1)S(1)}, bf16[256,256]{1,0:T(8,128)(2,1)S(1)}, u32[]{:S(2)}, u32[]{:S(2)}) collective-permute-start(bf16[256,256]{1,0:T(8,128)(2,1)S(1)} %add_convert_fusion.6.refs_4_), channel_id=1, source_target_pairs={{0,2},{1,3},{2,0},{3,1},{4,6},{5,7},{6,4},{7,5},{8,10},{9,11},{10,... | collective-permute-start | bytes 393224 | tf_op jit(solution)/shard_map/ppermute | solution.py:437
  69.2 6.2 %collective-permute-start.6 = (bf16[256,256]{1,0:T(8,128)(2,1)S(1)}, bf16[256,256]{1,0:T(8,128)(2,1)S(1)}, u32[]{:S(2)}, u32[]{:S(2)}) collective-permute-start(bf16[256,256]{1,0:T(8,128)(2,1)S(1)} %add_convert_fusion.6.refs_4_), channel_id=1, source_target_pairs={{0,4},{1,5},{2,6},{3,7},{4,0},{5,1},{6,2},{7,3},{8,12},{9,13},{10,... | collective-permute-start | bytes 393224 | tf_op jit(solution)/shard_map/ppermute | solution.py:437
  71.0 5.8 %collective-permute-start.3 = (bf16[256,256]{1,0:T(8,128)(2,1)S(1)}, bf16[256,256]{1,0:T(8,128)(2,1)S(1)}, u32[]{:S(2)}, u32[]{:S(2)}) collective-permute-start(bf16[256,256]{1,0:T(8,128)(2,1)S(1)} %add_convert_fusion.6.refs_4_), channel_id=1, source_target_pairs={{0,1},{1,0},{2,3},{3,2},{4,5},{5,4},{6,7},{7,6},{8,9},{9,8},{10,11... | collective-permute-start | bytes 393224 | tf_op jit(solution)/shard_map/ppermute | solution.py:437
  74.0 5.0 %collective-permute-start.14 = (bf16[256,256]{1,0:T(8,128)(2,1)S(1)}, bf16[256,256]{1,0:T(8,128)(2,1)S(1)}, u32[]{:S(2)}, u32[]{:S(2)}) collective-permute-start(bf16[256,256]{1,0:T(8,128)(2,1)S(1)} %collective-permute-done.10.refs_12_), channel_id=1, source_target_pairs={{0,4},{1,5},{2,6},{3,7},{4,0},{5,1},{6,2},{7,3},{8,12},{9,13},{10,... | collective-permute-start | bytes 393224 | tf_op jit(solution)/shard_map/ppermute | solution.py:437
  74.3 5.0 %collective-permute-start.5 = (bf16[256,256]{1,0:T(8,128)(2,1)S(1)}, bf16[256,256]{1,0:T(8,128)(2,1)S(1)}, u32[]{:S(2)}, u32[]{:S(2)}) collective-permute-start(bf16[256,256]{1,0:T(8,128)(2,1)S(1)} %collective-permute-done.4.refs_6_), channel_id=1, source_target_pairs={{0,1},{1,0},{2,3},{3,2},{4,5},{5,4},{6,7},{7,6},{8,9},{9,8},{10,11... | collective-permute-start | bytes 393224 | tf_op jit(solution)/shard_map/ppermute | solution.py:437
  75.4 3.9 %collective-permute-start.7 = (bf16[256,256]{1,0:T(8,128)(2,1)S(1)}, bf16[256,256]{1,0:T(8,128)(2,1)S(1)}, u32[]{:S(2)}, u32[]{:S(2)}) collective-permute-start(bf16[256,256]{1,0:T(8,128)(2,1)S(1)} %collective-permute-done.6.refs_8_), channel_id=1, source_target_pairs={{0,1},{1,0},{2,3},{3,2},{4,5},{5,4},{6,7},{7,6},{8,9},{9,8},{10,11... | collective-permute-start | bytes 393224 | tf_op jit(solution)/shard_map/ppermute | solution.py:437
  75.4 6.3 %collective-permute-start.8 = (bf16[256,256]{1,0:T(8,128)(2,1)S(1)}, bf16[256,256]{1,0:T(8,128)(2,1)S(1)}, u32[]{:S(2)}, u32[]{:S(2)}) collective-permute-start(bf16[256,256]{1,0:T(8,128)(2,1)S(1)} %collective-permute-done.6.refs_8_), channel_id=1, source_target_pairs={{0,2},{1,3},{2,0},{3,1},{4,6},{5,7},{6,4},{7,5},{8,10},{9,11},{10,... | collective-permute-start | bytes 393224 | tf_op jit(solution)/shard_map/ppermute | solution.py:437
  76.8 7.8 %collective-permute-start.12 = (bf16[256,256]{1,0:T(8,128)(2,1)S(1)}, bf16[256,256]{1,0:T(8,128)(2,1)S(1)}, u32[]{:S(2)}, u32[]{:S(2)}) collective-permute-start(bf16[256,256]{1,0:T(8,128)(2,1)S(1)} %collective-permute-done.10.refs_12_), channel_id=1, source_target_pairs={{0,2},{1,3},{2,0},{3,1},{4,6},{5,7},{6,4},{7,5},{8,10},{9,11},{10,... | collective-permute-start | bytes 393224 | tf_op jit(solution)/shard_map/ppermute | solution.py:437
  78.9 8.0 %collective-permute-start.16 = (bf16[256,256]{1,0:T(8,128)(2,1)S(1)}, bf16[256,256]{1,0:T(8,128)(2,1)S(1)}, u32[]{:S(2)}, u32[]{:S(2)}) collective-permute-start(bf16[256,256]{1,0:T(8,128)(2,1)S(1)} %collective-permute-done.14.refs_16_), channel_id=1, source_target_pairs={{0,2},{1,3},{2,0},{3,1},{4,6},{5,7},{6,4},{7,5},{8,10},{9,11},{10,... | collective-permute-start | bytes 393224 | tf_op jit(solution)/shard_map/ppermute | solution.py:437
  79.3 7.6 %collective-permute-start.11 = (bf16[256,256]{1,0:T(8,128)(2,1)S(1)}, bf16[256,256]{1,0:T(8,128)(2,1)}, u32[]{:S(2)}, u32[]{:S(2)}) collective-permute-start(bf16[256,256]{1,0:T(8,128)(2,1)S(1)} %collective-permute-done.10.refs_12_), channel_id=1, source_target_pairs={{0,1},{1,0},{2,3},{3,2},{4,5},{5,4},{6,7},{7,6},{8,9},{9,8},{10,11... | collective-permute-start | bytes 393224 | tf_op jit(solution)/shard_map/ppermute | solution.py:437
  79.3 7.6 %collective-permute-start.15 = (bf16[256,256]{1,0:T(8,128)(2,1)S(1)}, bf16[256,256]{1,0:T(8,128)(2,1)}, u32[]{:S(2)}, u32[]{:S(2)}) collective-permute-start(bf16[256,256]{1,0:T(8,128)(2,1)S(1)} %collective-permute-done.14.refs_16_), channel_id=1, source_target_pairs={{0,1},{1,0},{2,3},{3,2},{4,5},{5,4},{6,7},{7,6},{8,9},{9,8},{10,11... | collective-permute-start | bytes 393224 | tf_op jit(solution)/shard_map/ppermute | solution.py:437
  81.7 5.2 %collective-permute-start.9 = (bf16[256,256]{1,0:T(8,128)(2,1)S(1)}, bf16[256,256]{1,0:T(8,128)(2,1)}, u32[]{:S(2)}, u32[]{:S(2)}) collective-permute-start(bf16[256,256]{1,0:T(8,128)(2,1)S(1)} %collective-permute-done.8.refs_10_), channel_id=1, source_target_pairs={{0,1},{1,0},{2,3},{3,2},{4,5},{5,4},{6,7},{7,6},{8,9},{9,8},{10,11... | collective-permute-start | bytes 393224 | tf_op jit(solution)/shard_map/ppermute | solution.py:437
  84.5 2.4 %collective-permute-start.13 = (bf16[256,256]{1,0:T(8,128)(2,1)S(1)}, bf16[256,256]{1,0:T(8,128)(2,1)}, u32[]{:S(2)}, u32[]{:S(2)}) collective-permute-start(bf16[256,256]{1,0:T(8,128)(2,1)S(1)} %collective-permute-done.12.refs_14_), channel_id=1, source_target_pairs={{0,1},{1,0},{2,3},{3,2},{4,5},{5,4},{6,7},{7,6},{8,9},{9,8},{10,11... | collective-permute-start | bytes 393224 | tf_op jit(solution)/shard_map/ppermute | solution.py:437
  86.9 1.5 collective-permute-start.17
  88.4 1.0 copy-start.4
  101.9 2.0 %collective-permute-start.20 = (bf16[8,128,256]{2,1,0:T(8,128)(2,1)S(1)}, bf16[8,128,256]{2,1,0:T(8,128)(2,1)S(1)}, u32[]{:S(2)}, u32[]{:S(2)}) collective-permute-start(bf16[8,128,256]{2,1,0:T(8,128)(2,1)S(1)} %get-tuple-element.27), channel_id=1, source_target_pairs={{0,1},{1,0},{2,3},{3,2},{4,5},{5,4},{6,7},{7,6},{8,9},{9,8},{10,11... | collective-permute-start | bytes 1572872 | tf_op jit(solution)/shard_map/ppermute | solution.py:453
  102.0 3.8 %collective-permute-start.23 = (bf16[8,128,256]{2,1,0:T(8,128)(2,1)S(1)}, bf16[8,128,256]{2,1,0:T(8,128)(2,1)S(1)}, u32[]{:S(2)}, u32[]{:S(2)}) collective-permute-start(bf16[8,128,256]{2,1,0:T(8,128)(2,1)S(1)} %get-tuple-element.29), channel_id=1, source_target_pairs={{0,1},{1,0},{2,3},{3,2},{4,5},{5,4},{6,7},{7,6},{8,9},{9,8},{10,11... | collective-permute-start | bytes 1572872 | tf_op jit(solution)/shard_map/ppermute | solution.py:453
  104.1 8.6 %collective-permute-start.21 = (bf16[4,128,256]{2,1,0:T(8,128)(2,1)S(1)}, bf16[4,128,256]{2,1,0:T(8,128)(2,1)S(1)}, u32[]{:S(2)}, u32[]{:S(2)}) collective-permute-start(bf16[4,128,256]{2,1,0:T(8,128)(2,1)S(1)} %slice.49), channel_id=1, source_target_pairs={{0,2},{1,3},{2,0},{3,1},{4,6},{5,7},{6,4},{7,5},{8,10},{9,11},{10,... | collective-permute-start | bytes 786440 | tf_op jit(solution)/shard_map/ppermute | solution.py:453
  106.0 15.8 %copy-start.1 = (bf16[2,1,8,512,128]{4,3,2,1,0:T(8,128)(2,1)S(1)}, bf16[2,1,8,512,128]{4,3,2,1,0:T(8,128)(2,1)}, u32[]{:S(2)}) copy-start(bf16[2,1,8,512,128]{4,3,2,1,0:T(8,128)(2,1)} %param.8) | copy-start | bytes 6291460
  106.0 8.4 %collective-permute-start.24 = (bf16[4,128,256]{2,1,0:T(8,128)(2,1)S(1)}, bf16[4,128,256]{2,1,0:T(8,128)(2,1)S(1)}, u32[]{:S(2)}, u32[]{:S(2)}) collective-permute-start(bf16[4,128,256]{2,1,0:T(8,128)(2,1)S(1)} %slice.53), channel_id=1, source_target_pairs={{0,4},{1,5},{2,6},{3,7},{4,0},{5,1},{6,2},{7,3},{8,12},{9,13},{10,... | collective-permute-start | bytes 786440 | tf_op jit(solution)/shard_map/ppermute | solution.py:453
  107.9 13.8 %collective-permute-start.18 = (bf16[512,256]{1,0:T(8,128)(2,1)S(1)}, bf16[512,256]{1,0:T(8,128)(2,1)S(1)}, u32[]{:S(2)}, u32[]{:S(2)}) collective-permute-start(bf16[512,256]{1,0:T(8,128)(2,1)S(1)} %get-tuple-element.23), channel_id=1, source_target_pairs={{0,16},{16,0},{1,17},{17,1},{2,18},{18,2},{3,19},{19,3},{4,20},{20... | collective-permute-start | bytes 786440 | tf_op jit(solution)/shard_map/ppermute | solution.py:409
  109.4 12.3 %collective-permute-start.19 = (bf16[512,256]{1,0:T(8,128)(2,1)S(1)}, bf16[512,256]{1,0:T(8,128)(2,1)S(1)}, u32[]{:S(2)}, u32[]{:S(2)}) collective-permute-start(bf16[512,256]{1,0:T(8,128)(2,1)S(1)} %get-tuple-element.25), channel_id=1, source_target_pairs={{0,16},{16,0},{1,17},{17,1},{2,18},{18,2},{3,19},{19,3},{4,20},{20... | collective-permute-start | bytes 786440 | tf_op jit(solution)/shard_map/ppermute | solution.py:409
  112.7 5.0 %collective-permute-start.22 = (bf16[2,128,256]{2,1,0:T(8,128)(2,1)S(1)}, bf16[2,128,256]{2,1,0:T(8,128)(2,1)S(1)}, u32[]{:S(2)}, u32[]{:S(2)}) collective-permute-start(bf16[2,128,256]{2,1,0:T(8,128)(2,1)S(1)} %slice.51), channel_id=1, source_target_pairs={{0,4},{1,5},{2,6},{3,7},{4,0},{5,1},{6,2},{7,3},{8,12},{9,13},{10,... | collective-permute-start | bytes 393224 | tf_op jit(solution)/shard_map/ppermute | solution.py:453
  114.5 5.4 %collective-permute-start.25 = (bf16[2,128,256]{2,1,0:T(8,128)(2,1)S(1)}, bf16[2,128,256]{2,1,0:T(8,128)(2,1)S(1)}, u32[]{:S(2)}, u32[]{:S(2)}) collective-permute-start(bf16[2,128,256]{2,1,0:T(8,128)(2,1)S(1)} %slice.55), channel_id=1, source_target_pairs={{0,2},{1,3},{2,0},{3,1},{4,6},{5,7},{6,4},{7,5},{8,10},{9,11},{10,... | collective-permute-start | bytes 393224 | tf_op jit(solution)/shard_map/ppermute | solution.py:453
  117.8 7.2 %collective-permute-start.26 = (bf16[1,128,256]{2,1,0:T(8,128)(2,1)S(1)}, bf16[1,128,256]{2,1,0:T(8,128)(2,1)S(1)}, u32[]{:S(2)}, u32[]{:S(2)}) collective-permute-start(bf16[1,128,256]{2,1,0:T(8,128)(2,1)S(1)} %slice.57), channel_id=1, source_target_pairs={{0,8},{1,9},{2,10},{3,11},{4,12},{5,13},{6,14},{7,15},{8,0},{9,1},... | collective-permute-start | bytes 196616 | tf_op jit(solution)/shard_map/ppermute | solution.py:453
  119.9 6.5 %collective-permute-start.27 = (bf16[1,128,256]{2,1,0:T(8,128)(2,1)S(1)}, bf16[1,128,256]{2,1,0:T(8,128)(2,1)S(1)}, u32[]{:S(2)}, u32[]{:S(2)}) collective-permute-start(bf16[1,128,256]{2,1,0:T(8,128)(2,1)S(1)} %slice.59), channel_id=1, source_target_pairs={{0,8},{1,9},{2,10},{3,11},{4,12},{5,13},{6,14},{7,15},{8,0},{9,1},... | collective-permute-start | bytes 196616 | tf_op jit(solution)/shard_map/ppermute | solution.py:453
  127.1 4.5 %copy-start.7 = (bf16[1,128,256]{2,1,0:T(8,128)(2,1)S(1)}, bf16[1,128,256]{2,1,0:T(8,128)(2,1)}, u32[]{:S(2)}) copy-start(bf16[1,128,256]{2,1,0:T(8,128)(2,1)} %add_convert_fusion.8.refs_1_) | copy-start | bytes 196612
  127.1 4.5 %copy-start.8 = (bf16[1,128,256]{2,1,0:T(8,128)(2,1)S(1)}, bf16[1,128,256]{2,1,0:T(8,128)(2,1)}, u32[]{:S(2)}) copy-start(bf16[1,128,256]{2,1,0:T(8,128)(2,1)} %add_convert_fusion.7.refs_2_) | copy-start | bytes 196612
  127.1 27.4 %all-to-all-start.2 = ((bf16[16,16,2048]{2,1,0:T(8,128)(2,1)}), bf16[16,16,2048]{2,1,0:T(8,128)(2,1)S(1)}, u32[]{:S(2)}, u32[]{:S(2)}) async-start(bf16[16,16,2048]{2,1,0:T(8,128)(2,1)} %after.2), calls=%async_computation.2 | async-start | bytes 2097152 | tf_op jit(solution)/shard_map/all_to_all | solution.py:412
  131.7 5.9 %collective-permute-start.28 = (bf16[256,256]{1,0:T(8,128)(2,1)S(1)}, bf16[256,256]{1,0:T(8,128)(2,1)S(1)}, u32[]{:S(2)}, u32[]{:S(2)}) collective-permute-start(bf16[256,256]{1,0:T(8,128)(2,1)S(1)} %pad_maximum_fusion.1), channel_id=1, source_target_pairs={{0,16},{16,0},{1,17},{17,1},{2,18},{18,2},{3,19},{19,3},{4,20},{20... | collective-permute-start | bytes 393224 | tf_op jit(solution)/shard_map/ppermute | solution.py:409
  154.6 1.0 copy-start.6
  155.5 21.3 %all-to-all-start.3 = ((bf16[16,16,1024]{2,1,0:T(8,128)(2,1)}), bf16[16,16,1024]{2,1,0:T(8,128)(2,1)S(1)}, u32[]{:S(2)}, u32[]{:S(2)}) async-start(bf16[16,16,1024]{2,1,0:T(8,128)(2,1)} %after.3), calls=%async_computation.3 | async-start | bytes 1048576 | tf_op jit(solution)/shard_map/all_to_all | solution.py:412

commit v5 on v4

--- a/solution.py
+++ b/solution.py
@@ -453,14 +453,16 @@
         return lax.ppermute(array, "rows", across(n_rows, bit))
 
     sums = [plus(first, give(first_give, 1)), plus(second, give(second_give, 1))]
+    sent = [None] * len(orders)
     for step in range(len(bits)):
         for h, order in enumerate(orders):
             half = sums[h].shape[0] // 2
-            sums[h] = plus(sums[h][:half], give(sums[h][half:], order[step]))
+            sent[h] = give(sums[h][half:], order[step])
+            sums[h] = plus(sums[h][:half], sent[h])
         if step == len(bits) - 2:
             user_ask = user_grad_blocks(grads, x_vals, n_rows, sums)
     item_grad = jnp.concatenate([part[0] for part in sums])
-    user_back = in_hbm(every(*after([user_ask], sums)))
+    user_back = in_hbm(every(*after([user_ask], sent)))
     if n_feat == 2:
         other = swap(item_grad)
         first = feat_id == 0

time: 181 us -> 181 us (level)
  starting transfers between devices: 53.5 us -> 51 us
  waiting for transfers between devices: 89.7 us -> 92.1 us
    ppermute x8, starting transfers between devices: 11.5 us -> 8.9 us  [give(): return lax.ppermute(array, 'rows', across(n_rows, bit))]
    ppermute x8, waiting for transfers between devices: 8.02 us -> 10.5 us  [give(): return lax.ppermute(array, 'rows', across(n_rows, bit))]
  transfers between devices with their start and end apart: 33 -> 33, of which waited for: 18 -> 19; matrix products, arithmetic and copies ran while one was open for 1% -> 0% of each run, Pallas kernels for 6% -> 6%
where the time goes in v5:
time: 181 us; the launch traced here: 180 us
  waiting for transfers between devices  92.1 us (51%)
  starting transfers between devices  51 us (28%)
  Pallas kernels  32.8 us (18%)
  local copies, waits for them, and re-layouts  2.75 us (2%)
    all_to_all x4, waiting for transfers between devices, every(): lax.all_to_all(array, 'rows', split_axis=0, concat_axis=0, tiled=True)  61.5 us
    all_to_all x4, starting transfers between devices, every(): lax.all_to_all(array, 'rows', split_axis=0, concat_axis=0, tiled=True)  22.6 us
    ppermute x15, waiting for transfers between devices, on_device(): items[k + bit] = lax.ppermute(items[k], 'rows', across(n_rows, bit))  14.1 us
    pallas_call x1, Pallas kernels, rate(): pl.pallas_call(functools.partial(rating_kernel, orders, rank_scale, grad_...  13.4 us
    ppermute x15, starting transfers between devices, on_device(): items[k + bit] = lax.ppermute(items[k], 'rows', across(n_rows, bit))  12.1 us
    ppermute x8, waiting for transfers between devices, give(): return lax.ppermute(array, 'rows', across(n_rows, bit))  10.5 us
    ppermute x8, starting transfers between devices, give(): return lax.ppermute(array, 'rows', across(n_rows, bit))  8.9 us
    pallas_call x2, Pallas kernels, collect(): pl.pallas_call(functools.partial(collect_kernel, first), out_shape=jax.Sh...  8.5 us
  transfers between devices with their start and end apart: 33, of which 19 were waited for; matrix products, arithmetic and copies ran while one was open for 0% of the time, Pallas kernels for 6%

profile of v5, /device:TPU:0, one launch (start us, length us, event | category | flops | bytes accessed | tf_op | source)
XLA Modules:
  0.0 180.2 jit_solution(2700357277602378043)
XLA Ops:
  0.6 1.4 ask.1
  2.0 7.4 %all-to-all-start = ((s32[16,1,128]{2,1,0:T(1,128)}), s32[16,1,128]{2,1,0:T(1,128)S(1)}, u32[]{:S(2)}, u32[]{:S(2)}) async-start(s32[16,1,128]{2,1,0:T(1,128)} %ask.1), calls=%async_computation | async-start | bytes 16384 | tf_op jit(solution)/shard_map/all_to_all | solution.py:412
  9.3 1.4 preload.1.item_table
  10.8 4.9 %all-to-all-done.ids = s32[16,1,128]{2,1,0:T(1,128)S(1)} async-done(((s32[16,1,128]{2,1,0:T(1,128)}), s32[16,1,128]{2,1,0:T(1,128)S(1)}, u32[]{:S(2)}, u32[]{:S(2)}) %all-to-all-start) | async-done | bytes 8224 | tf_op jit(solution)/shard_map/all_to_all | solution.py:412
  15.7 3.7 %pick.1 = bf16[16,16,3072]{2,1,0:T(8,128)(2,1)} custom-call(s32[16,1,128]{2,1,0:T(1,128)S(1)} %all-to-all-done.ids, bf16[16,50176]{1,0:T(8,128)(2,1)S(1)} %preload.1.item_table, bf16[16,100352]{1,0:T(8,128)(2,1)} %user_weights.1), custom_call_target="tpu_custom_call" | custom-call | tf_op jit(solution)/shard_map/pick/pallas_call | solution.py:95
  19.4 0.0 copy-start.2
  19.4 3.9 %all-to-all-start.1 = ((bf16[16,16,3072]{2,1,0:T(8,128)(2,1)}), bf16[16,16,3072]{2,1,0:T(8,128)(2,1)S(1)}, u32[]{:S(2)}, u32[]{:S(2)}) async-start(bf16[16,16,3072]{2,1,0:T(8,128)(2,1)} %pick.1), calls=%async_computation.1 | async-start | bytes 3145728 | tf_op jit(solution)/shard_map/all_to_all | solution.py:412
  23.3 31.9 %all-to-all-done.1.cols = bf16[16,16,3072]{2,1,0:T(8,128)(2,1)S(1)} async-done(((bf16[16,16,3072]{2,1,0:T(8,128)(2,1)}), bf16[16,16,3072]{2,1,0:T(8,128)(2,1)S(1)}, u32[]{:S(2)}, u32[]{:S(2)}) %all-to-all-start.1) | async-done | bytes 1572896 | tf_op jit(solution)/shard_map/all_to_all | solution.py:412
  55.2 0.5 project_halves.1
  55.7 1.6 collective-permute-start.2
  57.3 0.5 project.2
  57.8 0.0 copy-start.5
  57.8 1.1 collective-permute-start
  58.9 0.5 project.3
  59.4 1.1 collective-permute-start.1
  60.4 1.7 collective-permute-done.2
  62.1 7.1 %collective-permute-start.10 = (bf16[256,256]{1,0:T(8,128)(2,1)S(1)}, bf16[256,256]{1,0:T(8,128)(2,1)S(1)}, u32[]{:S(2)}, u32[]{:S(2)}) collective-permute-start(bf16[256,256]{1,0:T(8,128)(2,1)S(1)} %add_convert_fusion.6.refs_4_), channel_id=1, source_target_pairs={{0,8},{1,9},{2,10},{3,11},{4,12},{5,13},{6,14},{7,15},{8,0},{9,1},... | collective-permute-start | bytes 393224 | tf_op jit(solution)/shard_map/ppermute | solution.py:437
  69.2 1.8 collective-permute-start.6
  71.0 3.0 %collective-permute-done.10.refs_12_ = bf16[256,256]{1,0:T(8,128)(2,1)S(1)} collective-permute-done((bf16[256,256]{1,0:T(8,128)(2,1)S(1)}, bf16[256,256]{1,0:T(8,128)(2,1)S(1)}, u32[]{:S(2)}, u32[]{:S(2)}) %collective-permute-start.10) | collective-permute-done | bytes 131104 | tf_op jit(solution)/shard_map/ppermute | solution.py:437
  74.0 0.3 collective-permute-start.14
  74.3 1.1 collective-permute-done.6.refs_8_
  75.4 1.3 collective-permute-start.8
  76.8 0.7 collective-permute-start.12
  77.5 1.5 collective-permute-done.14.refs_16_
  78.9 0.4 collective-permute-start.16
  79.3 0.5 collective-permute-start.15
  79.8 1.9 %collective-permute-done.8.refs_10_ = bf16[256,256]{1,0:T(8,128)(2,1)S(1)} collective-permute-done((bf16[256,256]{1,0:T(8,128)(2,1)S(1)}, bf16[256,256]{1,0:T(8,128)(2,1)S(1)}, u32[]{:S(2)}, u32[]{:S(2)}) %collective-permute-start.8) | collective-permute-done | bytes 131104 | tf_op jit(solution)/shard_map/ppermute | solution.py:437
  81.7 2.8 %collective-permute-done.12.refs_14_ = bf16[256,256]{1,0:T(8,128)(2,1)S(1)} collective-permute-done((bf16[256,256]{1,0:T(8,128)(2,1)S(1)}, bf16[256,256]{1,0:T(8,128)(2,1)S(1)}, u32[]{:S(2)}, u32[]{:S(2)}) %collective-permute-start.12) | collective-permute-done | bytes 131104 | tf_op jit(solution)/shard_map/ppermute | solution.py:437
  84.5 2.4 %collective-permute-done.16.refs_18_ = bf16[256,256]{1,0:T(8,128)(2,1)S(1)} collective-permute-done((bf16[256,256]{1,0:T(8,128)(2,1)S(1)}, bf16[256,256]{1,0:T(8,128)(2,1)S(1)}, u32[]{:S(2)}, u32[]{:S(2)}) %collective-permute-start.16) | collective-permute-done | bytes 131104 | tf_op jit(solution)/shard_map/ppermute | solution.py:437
  87.0 1.4 collective-permute-done.17.refs_19_
  88.4 1.0 copy-done.4
  89.5 13.4 %rate.1 = (f32[512,256]{1,0:T(8,128)S(1)}, bf16[512,256]{1,0:T(8,128)(2,1)S(1)}, f32[512,256]{1,0:T(8,128)S(1)}, bf16[512,256]{1,0:T(8,128)(2,1)S(1)}, bf16[8,12...) custom-call(s32[1]{0:T(128)} %bitcast.1.me, ...), custom_call_target="tpu_custom_call" | custom-call | tf_op jit(solution)/shard_map/rate/pallas_call | solution.py:359
  102.9 0.1 collective-permute-start.20
  103.0 0.5 collective-permute-start.23
  103.4 1.4 collective-permute-done.20
  104.8 0.1 add_convert_fusion.1
  105.0 0.1 collective-permute-start.21
  105.1 0.5 collective-permute-done.23
  105.6 0.1 add_convert_fusion
  105.8 2.3 %collective-permute-start.24 = (bf16[4,128,256]{2,1,0:T(8,128)(2,1)S(1)}, bf16[4,128,256]{2,1,0:T(8,128)(2,1)S(1)}, u32[]{:S(2)}, u32[]{:S(2)}) collective-permute-start(bf16[4,128,256]{2,1,0:T(8,128)(2,1)S(1)} %slice.53), channel_id=1, source_target_pairs={{0,4},{1,5},{2,6},{3,7},{4,0},{5,1},{6,2},{7,3},{8,12},{9,13},{10,... | collective-permute-start | bytes 786440 | tf_op jit(solution)/shard_map/ppermute | solution.py:453
  108.1 1.6 collective-permute-start.18
  109.7 0.5 collective-permute-start.19
  110.1 3.3 %collective-permute-done.21 = bf16[4,128,256]{2,1,0:T(8,128)(2,1)S(1)} collective-permute-done((bf16[4,128,256]{2,1,0:T(8,128)(2,1)S(1)}, bf16[4,128,256]{2,1,0:T(8,128)(2,1)S(1)}, u32[]{:S(2)}, u32[]{:S(2)}) %collective-permute-start.21) | collective-permute-done | bytes 262176 | tf_op jit(solution)/shard_map/ppermute | solution.py:453
  113.4 0.1 add_convert_fusion.3
  113.5 1.1 collective-permute-start.22
  114.6 0.1 add_convert_fusion.2
  114.7 1.8 %collective-permute-start.25 = (bf16[2,128,256]{2,1,0:T(8,128)(2,1)S(1)}, bf16[2,128,256]{2,1,0:T(8,128)(2,1)S(1)}, u32[]{:S(2)}, u32[]{:S(2)}) collective-permute-start(bf16[2,128,256]{2,1,0:T(8,128)(2,1)S(1)} %slice.55), channel_id=1, source_target_pairs={{0,2},{1,3},{2,0},{3,1},{4,6},{5,7},{6,4},{7,5},{8,10},{9,11},{10,... | collective-permute-start | bytes 393224 | tf_op jit(solution)/shard_map/ppermute | solution.py:453
  116.5 2.1 %collective-permute-done.22 = bf16[2,128,256]{2,1,0:T(8,128)(2,1)S(1)} collective-permute-done((bf16[2,128,256]{2,1,0:T(8,128)(2,1)S(1)}, bf16[2,128,256]{2,1,0:T(8,128)(2,1)S(1)}, u32[]{:S(2)}, u32[]{:S(2)}) %collective-permute-start.22) | collective-permute-done | bytes 131104 | tf_op jit(solution)/shard_map/ppermute | solution.py:453
  118.6 1.6 collective-permute-start.26
  120.2 1.5 collective-permute-start.27
  121.7 1.7 user_grad_blocks.1.refs_0_
  123.4 1.8 collective-permute-done.26.refs_1_
  125.2 1.4 collective-permute-done.27.refs_2_
  126.7 0.6 copy-done.9
  127.3 4.5 %all-to-all-start.2 = ((bf16[16,16,2048]{2,1,0:T(8,128)(2,1)}), bf16[16,16,2048]{2,1,0:T(8,128)(2,1)S(1)}, u32[]{:S(2)}, u32[]{:S(2)}) async-start(bf16[16,16,2048]{2,1,0:T(8,128)(2,1)} %after.2), calls=%async_computation.2 | async-start | bytes 2097152 | tf_op jit(solution)/shard_map/all_to_all | solution.py:412
  131.9 1.6 collective-permute-start.28
  133.5 4.3 %collective-permute-done.28 = bf16[256,256]{1,0:T(8,128)(2,1)S(1)} collective-permute-done((bf16[256,256]{1,0:T(8,128)(2,1)S(1)}, bf16[256,256]{1,0:T(8,128)(2,1)S(1)}, u32[]{:S(2)}, u32[]{:S(2)}) %collective-permute-start.28) | collective-permute-done | bytes 131104 | tf_op jit(solution)/shard_map/ppermute | solution.py:409
  137.9 1.2 item_grad_blocks.1.refs_0_
  139.1 15.6 %all-to-all-done.2.back.refs_1_ = bf16[16,16,2048]{2,1,0:T(8,128)(2,1)S(1)} async-done(((bf16[16,16,2048]{2,1,0:T(8,128)(2,1)}), bf16[16,16,2048]{2,1,0:T(8,128)(2,1)S(1)}, u32[]{:S(2)}, u32[]{:S(2)}) %all-to-all-start.2) | async-done | bytes 1048608 | tf_op jit(solution)/shard_map/all_to_all | solution.py:412
  154.8 1.0 copy-done.6
  155.7 6.9 %all-to-all-start.3 = ((bf16[16,16,1024]{2,1,0:T(8,128)(2,1)}), bf16[16,16,1024]{2,1,0:T(8,128)(2,1)S(1)}, u32[]{:S(2)}, u32[]{:S(2)}) async-start(bf16[16,16,1024]{2,1,0:T(8,128)(2,1)} %after.3), calls=%async_computation.3 | async-start | bytes 1048576 | tf_op jit(solution)/shard_map/all_to_all | solution.py:412
  162.6 5.4 %collect.2 = f32[16,100352]{1,0:T(8,128)} custom-call(s32[16,1,128]{2,1,0:T(1,128)S(1)} %all-to-all-done.ids, bf16[16,16,2048]{2,1,0:T(8,128)(2,1)} %copy-done.6), custom_call_target="tpu_custom_call" | custom-call | tf_op jit(solution)/shard_map/collect/pallas_call | solution.py:244
  168.0 9.1 %all-to-all-done.3.back = bf16[16,16,1024]{2,1,0:T(8,128)(2,1)S(1)} async-done(((bf16[16,16,1024]{2,1,0:T(8,128)(2,1)}), bf16[16,16,1024]{2,1,0:T(8,128)(2,1)S(1)}, u32[]{:S(2)}, u32[]{:S(2)}) %all-to-all-start.3) | async-done | bytes 524320 | tf_op jit(solution)/shard_map/all_to_all | solution.py:412
  177.1 3.1 %collect.3 = f32[16,50176]{1,0:T(8,128)} custom-call(s32[16,1,128]{2,1,0:T(1,128)S(1)} %all-to-all-done.ids, bf16[16,16,1024]{2,1,0:T(8,128)(2,1)S(1)} %all-to-all-done.3.back), custom_call_target="tpu_custom_call" | custom-call | tf_op jit(solution)/shard_map/collect/pallas_call | solution.py:244
  (55 shorter events, 0.4 us)
Async XLA Ops:
  2.0 13.7 %all-to-all-start = ((s32[16,1,128]{2,1,0:T(1,128)}), s32[16,1,128]{2,1,0:T(1,128)S(1)}, u32[]{:S(2)}, u32[]{:S(2)}) async-start(s32[16,1,128]{2,1,0:T(1,128)} %ask.1), calls=%async_computation | async-start | bytes 16384 | tf_op jit(solution)/shard_map/all_to_all | solution.py:412
  19.4 35.8 %copy-start.2 = (bf16[1,1,8,512,128]{4,3,2,1,0:T(8,128)(2,1)S(1)}, bf16[1,1,8,512,128]{4,3,2,1,0:T(8,128)(2,1)}, u32[]{:S(2)}) copy-start(bf16[1,1,8,512,128]{4,3,2,1,0:T(8,128)(2,1)} %param.10) | copy-start | bytes 3145732
  19.4 35.8 %all-to-all-start.1 = ((bf16[16,16,3072]{2,1,0:T(8,128)(2,1)}), bf16[16,16,3072]{2,1,0:T(8,128)(2,1)S(1)}, u32[]{:S(2)}, u32[]{:S(2)}) async-start(bf16[16,16,3072]{2,1,0:T(8,128)(2,1)} %pick.1), calls=%async_computation.1 | async-start | bytes 3145728 | tf_op jit(solution)/shard_map/all_to_all | solution.py:412
  55.2 2.1 %copy-start = (bf16[2,1,8,512,128]{4,3,2,1,0:T(8,128)(2,1)S(1)}, bf16[2,1,8,512,128]{4,3,2,1,0:T(8,128)(2,1)}, u32[]{:S(2)}) copy-start(bf16[2,1,8,512,128]{4,3,2,1,0:T(8,128)(2,1)} %param.8) | copy-start | bytes 6291460
  55.7 6.4 %collective-permute-start.2 = (bf16[256,256]{1,0:T(8,128)(2,1)S(1)}, bf16[256,256]{1,0:T(8,128)(2,1)S(1)}, u32[]{:S(2)}, u32[]{:S(2)}) collective-permute-start(bf16[256,256]{1,0:T(8,128)(2,1)S(1)} %get-tuple-element.16.refs_0_), channel_id=1, source_target_pairs={{0,16},{16,0},{1,17},{17,1},{2,18},{18,2},{3,19},{19,3},{4,20},{20... | collective-permute-start | bytes 393224 | tf_op jit(solution)/shard_map/ppermute | solution.py:409
  57.8 30.7 %copy-start.5 = (s32[2,16]{1,0:T(2,128)S(1)}, s32[2,16]{1,0:T(2,128)}, u32[]{:S(2)}) copy-start(s32[2,16]{1,0:T(2,128)} %observed.1) | copy-start | bytes 388
  57.8 13.2 %collective-permute-start = (bf16[512,256]{1,0:T(8,128)(2,1)S(1)}, bf16[512,256]{1,0:T(8,128)(2,1)S(1)}, u32[]{:S(2)}, u32[]{:S(2)}) collective-permute-start(bf16[512,256]{1,0:T(8,128)(2,1)S(1)} %get-tuple-element.18), channel_id=1, source_target_pairs={{0,16},{16,0},{1,17},{17,1},{2,18},{18,2},{3,19},{19,3},{4,20},{20... | collective-permute-start | bytes 786440 | tf_op jit(solution)/shard_map/ppermute | solution.py:409
  59.3 17.4 %copy-start.3 = (f32[512,256]{1,0:T(8,128)}, f32[512,256]{1,0:T(8,128)S(1)}, u32[]{:S(2)}) copy-start(f32[512,256]{1,0:T(8,128)S(1)} %get-tuple-element.19.refs_2_) | copy-start | bytes 1572868
  59.4 16.1 %collective-permute-start.1 = (bf16[512,256]{1,0:T(8,128)(2,1)S(1)}, bf16[512,256]{1,0:T(8,128)(2,1)S(1)}, u32[]{:S(2)}, u32[]{:S(2)}) collective-permute-start(bf16[512,256]{1,0:T(8,128)(2,1)S(1)} %get-tuple-element.20), channel_id=1, source_target_pairs={{0,16},{16,0},{1,17},{17,1},{2,18},{18,2},{3,19},{19,3},{4,20},{20... | collective-permute-start | bytes 786440 | tf_op jit(solution)/shard_map/ppermute | solution.py:409
  62.1 11.8 %collective-permute-start.10 = (bf16[256,256]{1,0:T(8,128)(2,1)S(1)}, bf16[256,256]{1,0:T(8,128)(2,1)S(1)}, u32[]{:S(2)}, u32[]{:S(2)}) collective-permute-start(bf16[256,256]{1,0:T(8,128)(2,1)S(1)} %add_convert_fusion.6.refs_4_), channel_id=1, source_target_pairs={{0,8},{1,9},{2,10},{3,11},{4,12},{5,13},{6,14},{7,15},{8,0},{9,1},... | collective-permute-start | bytes 393224 | tf_op jit(solution)/shard_map/ppermute | solution.py:437
  69.2 5.1 %collective-permute-start.4 = (bf16[256,256]{1,0:T(8,128)(2,1)S(1)}, bf16[256,256]{1,0:T(8,128)(2,1)S(1)}, u32[]{:S(2)}, u32[]{:S(2)}) collective-permute-start(bf16[256,256]{1,0:T(8,128)(2,1)S(1)} %add_convert_fusion.6.refs_4_), channel_id=1, source_target_pairs={{0,2},{1,3},{2,0},{3,1},{4,6},{5,7},{6,4},{7,5},{8,10},{9,11},{10,... | collective-permute-start | bytes 393224 | tf_op jit(solution)/shard_map/ppermute | solution.py:437
  69.2 6.2 %collective-permute-start.6 = (bf16[256,256]{1,0:T(8,128)(2,1)S(1)}, bf16[256,256]{1,0:T(8,128)(2,1)S(1)}, u32[]{:S(2)}, u32[]{:S(2)}) collective-permute-start(bf16[256,256]{1,0:T(8,128)(2,1)S(1)} %add_convert_fusion.6.refs_4_), channel_id=1, source_target_pairs={{0,4},{1,5},{2,6},{3,7},{4,0},{5,1},{6,2},{7,3},{8,12},{9,13},{10,... | collective-permute-start | bytes 393224 | tf_op jit(solution)/shard_map/ppermute | solution.py:437
  71.0 5.8 %collective-permute-start.3 = (bf16[256,256]{1,0:T(8,128)(2,1)S(1)}, bf16[256,256]{1,0:T(8,128)(2,1)S(1)}, u32[]{:S(2)}, u32[]{:S(2)}) collective-permute-start(bf16[256,256]{1,0:T(8,128)(2,1)S(1)} %add_convert_fusion.6.refs_4_), channel_id=1, source_target_pairs={{0,1},{1,0},{2,3},{3,2},{4,5},{5,4},{6,7},{7,6},{8,9},{9,8},{10,11... | collective-permute-start | bytes 393224 | tf_op jit(solution)/shard_map/ppermute | solution.py:437
  74.0 5.0 %collective-permute-start.14 = (bf16[256,256]{1,0:T(8,128)(2,1)S(1)}, bf16[256,256]{1,0:T(8,128)(2,1)S(1)}, u32[]{:S(2)}, u32[]{:S(2)}) collective-permute-start(bf16[256,256]{1,0:T(8,128)(2,1)S(1)} %collective-permute-done.10.refs_12_), channel_id=1, source_target_pairs={{0,4},{1,5},{2,6},{3,7},{4,0},{5,1},{6,2},{7,3},{8,12},{9,13},{10,... | collective-permute-start | bytes 393224 | tf_op jit(solution)/shard_map/ppermute | solution.py:437
  74.3 5.0 %collective-permute-start.5 = (bf16[256,256]{1,0:T(8,128)(2,1)S(1)}, bf16[256,256]{1,0:T(8,128)(2,1)S(1)}, u32[]{:S(2)}, u32[]{:S(2)}) collective-permute-start(bf16[256,256]{1,0:T(8,128)(2,1)S(1)} %collective-permute-done.4.refs_6_), channel_id=1, source_target_pairs={{0,1},{1,0},{2,3},{3,2},{4,5},{5,4},{6,7},{7,6},{8,9},{9,8},{10,11... | collective-permute-start | bytes 393224 | tf_op jit(solution)/shard_map/ppermute | solution.py:437
  75.4 3.9 %collective-permute-start.7 = (bf16[256,256]{1,0:T(8,128)(2,1)S(1)}, bf16[256,256]{1,0:T(8,128)(2,1)S(1)}, u32[]{:S(2)}, u32[]{:S(2)}) collective-permute-start(bf16[256,256]{1,0:T(8,128)(2,1)S(1)} %collective-permute-done.6.refs_8_), channel_id=1, source_target_pairs={{0,1},{1,0},{2,3},{3,2},{4,5},{5,4},{6,7},{7,6},{8,9},{9,8},{10,11... | collective-permute-start | bytes 393224 | tf_op jit(solution)/shard_map/ppermute | solution.py:437
  75.4 6.3 %collective-permute-start.8 = (bf16[256,256]{1,0:T(8,128)(2,1)S(1)}, bf16[256,256]{1,0:T(8,128)(2,1)S(1)}, u32[]{:S(2)}, u32[]{:S(2)}) collective-permute-start(bf16[256,256]{1,0:T(8,128)(2,1)S(1)} %collective-permute-done.6.refs_8_), channel_id=1, source_target_pairs={{0,2},{1,3},{2,0},{3,1},{4,6},{5,7},{6,4},{7,5},{8,10},{9,11},{10,... | collective-permute-start | bytes 393224 | tf_op jit(solution)/shard_map/ppermute | solution.py:437
  76.8 7.8 %collective-permute-start.12 = (bf16[256,256]{1,0:T(8,128)(2,1)S(1)}, bf16[256,256]{1,0:T(8,128)(2,1)S(1)}, u32[]{:S(2)}, u32[]{:S(2)}) collective-permute-start(bf16[256,256]{1,0:T(8,128)(2,1)S(1)} %collective-permute-done.10.refs_12_), channel_id=1, source_target_pairs={{0,2},{1,3},{2,0},{3,1},{4,6},{5,7},{6,4},{7,5},{8,10},{9,11},{10,... | collective-permute-start | bytes 393224 | tf_op jit(solution)/shard_map/ppermute | solution.py:437
  78.9 8.0 %collective-permute-start.16 = (bf16[256,256]{1,0:T(8,128)(2,1)S(1)}, bf16[256,256]{1,0:T(8,128)(2,1)S(1)}, u32[]{:S(2)}, u32[]{:S(2)}) collective-permute-start(bf16[256,256]{1,0:T(8,128)(2,1)S(1)} %collective-permute-done.14.refs_16_), channel_id=1, source_target_pairs={{0,2},{1,3},{2,0},{3,1},{4,6},{5,7},{6,4},{7,5},{8,10},{9,11},{10,... | collective-permute-start | bytes 393224 | tf_op jit(solution)/shard_map/ppermute | solution.py:437
  79.3 7.6 %collective-permute-start.11 = (bf16[256,256]{1,0:T(8,128)(2,1)S(1)}, bf16[256,256]{1,0:T(8,128)(2,1)}, u32[]{:S(2)}, u32[]{:S(2)}) collective-permute-start(bf16[256,256]{1,0:T(8,128)(2,1)S(1)} %collective-permute-done.10.refs_12_), channel_id=1, source_target_pairs={{0,1},{1,0},{2,3},{3,2},{4,5},{5,4},{6,7},{7,6},{8,9},{9,8},{10,11... | collective-permute-start | bytes 393224 | tf_op jit(solution)/shard_map/ppermute | solution.py:437
  79.3 7.6 %collective-permute-start.15 = (bf16[256,256]{1,0:T(8,128)(2,1)S(1)}, bf16[256,256]{1,0:T(8,128)(2,1)}, u32[]{:S(2)}, u32[]{:S(2)}) collective-permute-start(bf16[256,256]{1,0:T(8,128)(2,1)S(1)} %collective-permute-done.14.refs_16_), channel_id=1, source_target_pairs={{0,1},{1,0},{2,3},{3,2},{4,5},{5,4},{6,7},{7,6},{8,9},{9,8},{10,11... | collective-permute-start | bytes 393224 | tf_op jit(solution)/shard_map/ppermute | solution.py:437
  81.7 5.2 %collective-permute-start.9 = (bf16[256,256]{1,0:T(8,128)(2,1)S(1)}, bf16[256,256]{1,0:T(8,128)(2,1)}, u32[]{:S(2)}, u32[]{:S(2)}) collective-permute-start(bf16[256,256]{1,0:T(8,128)(2,1)S(1)} %collective-permute-done.8.refs_10_), channel_id=1, source_target_pairs={{0,1},{1,0},{2,3},{3,2},{4,5},{5,4},{6,7},{7,6},{8,9},{9,8},{10,11... | collective-permute-start | bytes 393224 | tf_op jit(solution)/shard_map/ppermute | solution.py:437
  84.5 2.4 %collective-permute-start.13 = (bf16[256,256]{1,0:T(8,128)(2,1)S(1)}, bf16[256,256]{1,0:T(8,128)(2,1)}, u32[]{:S(2)}, u32[]{:S(2)}) collective-permute-start(bf16[256,256]{1,0:T(8,128)(2,1)S(1)} %collective-permute-done.12.refs_14_), channel_id=1, source_target_pairs={{0,1},{1,0},{2,3},{3,2},{4,5},{5,4},{6,7},{7,6},{8,9},{9,8},{10,11... | collective-permute-start | bytes 393224 | tf_op jit(solution)/shard_map/ppermute | solution.py:437
  86.9 1.5 collective-permute-start.17
  88.4 1.0 copy-start.4
  102.9 2.0 %collective-permute-start.20 = (bf16[8,128,256]{2,1,0:T(8,128)(2,1)S(1)}, bf16[8,128,256]{2,1,0:T(8,128)(2,1)S(1)}, u32[]{:S(2)}, u32[]{:S(2)}) collective-permute-start(bf16[8,128,256]{2,1,0:T(8,128)(2,1)S(1)} %get-tuple-element.27), channel_id=1, source_target_pairs={{0,1},{1,0},{2,3},{3,2},{4,5},{5,4},{6,7},{7,6},{8,9},{9,8},{10,11... | collective-permute-start | bytes 1572872 | tf_op jit(solution)/shard_map/ppermute | solution.py:453
  103.0 2.6 %collective-permute-start.23 = (bf16[8,128,256]{2,1,0:T(8,128)(2,1)S(1)}, bf16[8,128,256]{2,1,0:T(8,128)(2,1)S(1)}, u32[]{:S(2)}, u32[]{:S(2)}) collective-permute-start(bf16[8,128,256]{2,1,0:T(8,128)(2,1)S(1)} %get-tuple-element.29), channel_id=1, source_target_pairs={{0,1},{1,0},{2,3},{3,2},{4,5},{5,4},{6,7},{7,6},{8,9},{9,8},{10,11... | collective-permute-start | bytes 1572872 | tf_op jit(solution)/shard_map/ppermute | solution.py:453
  105.0 8.4 %collective-permute-start.21 = (bf16[4,128,256]{2,1,0:T(8,128)(2,1)S(1)}, bf16[4,128,256]{2,1,0:T(8,128)(2,1)S(1)}, u32[]{:S(2)}, u32[]{:S(2)}) collective-permute-start(bf16[4,128,256]{2,1,0:T(8,128)(2,1)S(1)} %slice.49), channel_id=1, source_target_pairs={{0,2},{1,3},{2,0},{3,1},{4,6},{5,7},{6,4},{7,5},{8,10},{9,11},{10,... | collective-permute-start | bytes 786440 | tf_op jit(solution)/shard_map/ppermute | solution.py:453
  105.7 16.0 %copy-start.1 = (bf16[2,1,8,512,128]{4,3,2,1,0:T(8,128)(2,1)S(1)}, bf16[2,1,8,512,128]{4,3,2,1,0:T(8,128)(2,1)}, u32[]{:S(2)}) copy-start(bf16[2,1,8,512,128]{4,3,2,1,0:T(8,128)(2,1)} %param.8) | copy-start | bytes 6291460
  105.8 8.8 %collective-permute-start.24 = (bf16[4,128,256]{2,1,0:T(8,128)(2,1)S(1)}, bf16[4,128,256]{2,1,0:T(8,128)(2,1)S(1)}, u32[]{:S(2)}, u32[]{:S(2)}) collective-permute-start(bf16[4,128,256]{2,1,0:T(8,128)(2,1)S(1)} %slice.53), channel_id=1, source_target_pairs={{0,4},{1,5},{2,6},{3,7},{4,0},{5,1},{6,2},{7,3},{8,12},{9,13},{10,... | collective-permute-start | bytes 786440 | tf_op jit(solution)/shard_map/ppermute | solution.py:453
  108.1 13.6 %collective-permute-start.18 = (bf16[512,256]{1,0:T(8,128)(2,1)S(1)}, bf16[512,256]{1,0:T(8,128)(2,1)S(1)}, u32[]{:S(2)}, u32[]{:S(2)}) collective-permute-start(bf16[512,256]{1,0:T(8,128)(2,1)S(1)} %get-tuple-element.23), channel_id=1, source_target_pairs={{0,16},{16,0},{1,17},{17,1},{2,18},{18,2},{3,19},{19,3},{4,20},{20... | collective-permute-start | bytes 786440 | tf_op jit(solution)/shard_map/ppermute | solution.py:409
  109.7 12.1 %collective-permute-start.19 = (bf16[512,256]{1,0:T(8,128)(2,1)S(1)}, bf16[512,256]{1,0:T(8,128)(2,1)S(1)}, u32[]{:S(2)}, u32[]{:S(2)}) collective-permute-start(bf16[512,256]{1,0:T(8,128)(2,1)S(1)} %get-tuple-element.25), channel_id=1, source_target_pairs={{0,16},{16,0},{1,17},{17,1},{2,18},{18,2},{3,19},{19,3},{4,20},{20... | collective-permute-start | bytes 786440 | tf_op jit(solution)/shard_map/ppermute | solution.py:409
  113.5 5.0 %collective-permute-start.22 = (bf16[2,128,256]{2,1,0:T(8,128)(2,1)S(1)}, bf16[2,128,256]{2,1,0:T(8,128)(2,1)S(1)}, u32[]{:S(2)}, u32[]{:S(2)}) collective-permute-start(bf16[2,128,256]{2,1,0:T(8,128)(2,1)S(1)} %slice.51), channel_id=1, source_target_pairs={{0,4},{1,5},{2,6},{3,7},{4,0},{5,1},{6,2},{7,3},{8,12},{9,13},{10,... | collective-permute-start | bytes 393224 | tf_op jit(solution)/shard_map/ppermute | solution.py:453
  114.7 5.5 %collective-permute-start.25 = (bf16[2,128,256]{2,1,0:T(8,128)(2,1)S(1)}, bf16[2,128,256]{2,1,0:T(8,128)(2,1)S(1)}, u32[]{:S(2)}, u32[]{:S(2)}) collective-permute-start(bf16[2,128,256]{2,1,0:T(8,128)(2,1)S(1)} %slice.55), channel_id=1, source_target_pairs={{0,2},{1,3},{2,0},{3,1},{4,6},{5,7},{6,4},{7,5},{8,10},{9,11},{10,... | collective-permute-start | bytes 393224 | tf_op jit(solution)/shard_map/ppermute | solution.py:453
  118.6 6.6 %collective-permute-start.26 = (bf16[1,128,256]{2,1,0:T(8,128)(2,1)S(1)}, bf16[1,128,256]{2,1,0:T(8,128)(2,1)S(1)}, u32[]{:S(2)}, u32[]{:S(2)}) collective-permute-start(bf16[1,128,256]{2,1,0:T(8,128)(2,1)S(1)} %slice.56), channel_id=1, source_target_pairs={{0,8},{1,9},{2,10},{3,11},{4,12},{5,13},{6,14},{7,15},{8,0},{9,1},... | collective-permute-start | bytes 196616 | tf_op jit(solution)/shard_map/ppermute | solution.py:453
  120.2 6.4 %collective-permute-start.27 = (bf16[1,128,256]{2,1,0:T(8,128)(2,1)S(1)}, bf16[1,128,256]{2,1,0:T(8,128)(2,1)S(1)}, u32[]{:S(2)}, u32[]{:S(2)}) collective-permute-start(bf16[1,128,256]{2,1,0:T(8,128)(2,1)S(1)} %slice.57), channel_id=1, source_target_pairs={{0,8},{1,9},{2,10},{3,11},{4,12},{5,13},{6,14},{7,15},{8,0},{9,1},... | collective-permute-start | bytes 196616 | tf_op jit(solution)/shard_map/ppermute | solution.py:453
  125.2 1.4 copy-start.7
  126.6 0.6 copy-start.9
  127.3 4.5 %copy-start.10 = (bf16[1,128,256]{2,1,0:T(8,128)(2,1)S(1)}, bf16[1,128,256]{2,1,0:T(8,128)(2,1)}, u32[]{:S(2)}) copy-start(bf16[1,128,256]{2,1,0:T(8,128)(2,1)} %copy-done.9) | copy-start | bytes 196612
  127.3 4.6 %copy-start.8 = (bf16[1,128,256]{2,1,0:T(8,128)(2,1)S(1)}, bf16[1,128,256]{2,1,0:T(8,128)(2,1)}, u32[]{:S(2)}) copy-start(bf16[1,128,256]{2,1,0:T(8,128)(2,1)} %copy-done.7) | copy-start | bytes 196612
  127.3 27.5 %all-to-all-start.2 = ((bf16[16,16,2048]{2,1,0:T(8,128)(2,1)}), bf16[16,16,2048]{2,1,0:T(8,128)(2,1)S(1)}, u32[]{:S(2)}, u32[]{:S(2)}) async-start(bf16[16,16,2048]{2,1,0:T(8,128)(2,1)} %after.2), calls=%async_computation.2 | async-start | bytes 2097152 | tf_op jit(solution)/shard_map/all_to_all | solution.py:412
  131.9 5.9 %collective-permute-start.28 = (bf16[256,256]{1,0:T(8,128)(2,1)S(1)}, bf16[256,256]{1,0:T(8,128)(2,1)S(1)}, u32[]{:S(2)}, u32[]{:S(2)}) collective-permute-start(bf16[256,256]{1,0:T(8,128)(2,1)S(1)} %pad_maximum_fusion.1), channel_id=1, source_target_pairs={{0,16},{16,0},{1,17},{17,1},{2,18},{18,2},{3,19},{19,3},{4,20},{20... | collective-permute-start | bytes 393224 | tf_op jit(solution)/shard_map/ppermute | solution.py:409
  154.8 1.0 copy-start.6
  155.7 21.3 %all-to-all-start.3 = ((bf16[16,16,1024]{2,1,0:T(8,128)(2,1)}), bf16[16,16,1024]{2,1,0:T(8,128)(2,1)S(1)}, u32[]{:S(2)}, u32[]{:S(2)}) async-start(bf16[16,16,1024]{2,1,0:T(8,128)(2,1)} %after.3), calls=%async_computation.3 | async-start | bytes 1048576 | tf_op jit(solution)/shard_map/all_to_all | solution.py:412
